TPU v7x, 32 devices: a whole 2x2x4 slice. The times are simulated.
32 devices in a mesh: groups: 2 (over y), seq: 16 (over z, x, core).
Axes of the slice: x: 2, y: 2, z: 4, core: 2. Of those that a mesh axis runs over, the one named last changes fastest.
Arguments:
- grad_rows: bfloat16 [8192, 3584], P(('groups', 'seq')), parts along dimension 0, may hold values from -6 to 6
- route_ids: int32 [8192, 1], P(('groups', 'seq')), parts along dimension 0, may hold values from 0 to 31; in each aligned block of 256 rows (0 to 255, 256 to 511, ...) at most 16 rows name the same one
- audio_proj: bfloat16 [1280, 3584], P(None, 'seq'), may hold values from -0.15625 to 0.15625
- vision_proj: bfloat16 [1280, 3584], P(None, 'seq'), may hold values from -0.15625 to 0.15625
- audio_states: bfloat16 [8192, 1280], P(('groups', 'seq')), parts along dimension 0, may hold values from -120 to 120
- vision_states: bfloat16 [8192, 1280], P(('groups', 'seq')), parts along dimension 0, may hold values from -120 to 120
- audio_gain: float32 [1280], replicated, may hold values from 0.25 to 1.75
- vision_gain: float32 [1280], replicated, may hold values from 0.25 to 1.75
Outputs:
- audio_input_grad: bfloat16 [8192, 1280], P(('groups', 'seq')), parts along dimension 0
- vision_input_grad: bfloat16 [8192, 1280], P(('groups', 'seq')), parts along dimension 0
- gain_grads: float32 [4, 1280], P('groups'), parts along dimension 0
There are 2 independent parts, one for each index of `groups`. A program takes and returns all parts, laid end to end along the dimension named above; an argument that names none is the same for every part. Nothing has to cross between parts.
Inputs may be any that keep to these rules, and one draw needn't show every extreme that they name: `route_ids`: within the rows of one device no number is named by more than 16 rows, a bound that some block reaches; every number is named somewhere.
All inputs are finite; a program needn't handle non-finite values.
Results may differ from a plain program's by a relative error of at most 0.0085.
Values may be sent and summed in bfloat16 or wider, within the bound.
No kernel may reach another device: no remote copies, remote signals or barrier semaphores. Data moves between devices by JAX's collectives and lax.ppermute only.
A program may use at most 128 MiB of HBM per device.

v0:
```python
import jax
import jax.numpy as jnp
from jax import lax
from jax.sharding import PartitionSpec as P


def layer_back(states, upstream, gain):
    h = states.astype(jnp.float32)
    mu = jnp.mean(h, axis=-1, keepdims=True)
    centred = h - mu
    scale = lax.rsqrt(jnp.mean(centred * centred, axis=-1, keepdims=True) + 1e-05)
    normed = centred * scale
    upper = upstream.astype(jnp.float32)
    scaled = upper * gain[None, :]
    back = scale * (
        scaled
        - jnp.mean(scaled, axis=-1, keepdims=True)
        - normed * jnp.mean(scaled * normed, axis=-1, keepdims=True)
    )
    return (back.astype(jnp.bfloat16), jnp.sum(upper * normed, axis=0))


def rms_back(states, upstream, gain):
    h = states.astype(jnp.float32)
    scale = lax.rsqrt(jnp.mean(h * h, axis=-1, keepdims=True) + 1e-06)
    normed = h * scale
    upper = upstream.astype(jnp.float32)
    scaled = upper * gain[None, :]
    back = scale * (scaled - normed * jnp.mean(scaled * normed, axis=-1, keepdims=True))
    return (back.astype(jnp.bfloat16), jnp.sum(upper * normed, axis=0))


def project_back(inputs, audio_proj, vision_proj):
    dims = (((1,), (1,)), ((), ()))
    audio_part = lax.dot_general(
        inputs[0],
        lax.all_gather(audio_proj, "seq", axis=1, tiled=True),
        dims,
        preferred_element_type=jnp.float32,
    )
    vision_part = lax.dot_general(
        inputs[1],
        lax.all_gather(vision_proj, "seq", axis=1, tiled=True),
        dims,
        preferred_element_type=jnp.float32,
    )
    return (audio_part.astype(jnp.bfloat16), vision_part.astype(jnp.bfloat16))


def on_device(
    grad_rows,
    route_ids,
    audio_proj,
    vision_proj,
    audio_states,
    vision_states,
    audio_gain,
    vision_gain,
):
    devices = lax.axis_size("seq")
    rows = grad_rows.shape[0]
    width = grad_rows.shape[1]
    cap = rows // devices
    kinds = 2 * devices
    ids = route_ids[:, 0]
    onehot = (ids[:, None] == jnp.arange(kinds, dtype=jnp.int32)[None, :]).astype(jnp.int32)
    earlier = jnp.cumsum(onehot, axis=0) - onehot
    slot = jnp.sum(earlier * onehot, axis=1)
    position = ids * cap + slot
    packed = jnp.zeros((kinds * cap, width), grad_rows.dtype).at[position].set(grad_rows)
    arrived = lax.all_to_all(
        packed.reshape(2, devices, cap, width), "seq", split_axis=1, concat_axis=1, tiled=True
    )
    upstream_a, upstream_v = project_back(arrived.reshape(2, rows, width), audio_proj, vision_proj)
    audio_grad, audio_part = layer_back(audio_states, upstream_a, audio_gain)
    vision_grad, vision_part = rms_back(vision_states, upstream_v, vision_gain)
    audio_total, vision_total = lax.psum((audio_part, vision_part), "seq")
    return (audio_grad, vision_grad, jnp.stack([audio_total, vision_total]))


def solution(mesh):
    placed = (
        P(("groups", "seq"), None),
        P(("groups", "seq"), None),
        P(None, "seq"),
        P(None, "seq"),
        P(("groups", "seq"), None),
        P(("groups", "seq"), None),
        P(),
        P(),
    )
    return jax.shard_map(
        on_device,
        mesh=mesh,
        in_specs=placed,
        out_specs=(P(("groups", "seq"), None), P(("groups", "seq"), None), P("groups", None)),
        check_vma=False,
    )
```

profile of v0, /device:TPU:0, one launch (start us, length us, event | category | flops | bytes accessed | tf_op | source)
XLA Modules:
  0.0 311.9 jit_solution(3479598806976032151)
XLA Ops:
  7.2 0.0 all-gather.3.cloned.1.call-start
  7.2 0.7 all-gather.3.cloned.1.call-update
  7.9 0.0 all-gather.5.cloned.1.call-start
  8.0 0.7 all-gather.5.cloned.1.call-update
  8.7 0.7 fusion.27
  9.3 0.6 reduce-window.6
  9.9 0.2 slice_reduce_fusion
  10.1 0.8 fusion.26
  10.9 6.4 %scatter_custom_fusion = bf16[512,3584]{1,0:T(8,128)(2,1)} fusion(s32[256]{0:T(256)S(1)} %bitcast.36, bf16[256,3584]{1,0:T(8,128)(2,1)} %param.8, bf16[]{:T(256)} %constant.22.clone.1), kind=kCustom, calls=%fused_computation.5 | custom fusion | bytes 3670528 | tf_op jit(solution)/shard_map/scatter | solution.py:70
  17.4 4.2 %copy.13 = bf16[2,16,16,3584]{3,2,0,1:T(8,128)(2,1)} copy(bf16[2,16,16,3584]{3,2,1,0:T(8,128)(2,1)} %bitcast.30) | data formatting | bytes 7340032 | tf_op jit(solution)/shard_map/reshape | solution.py:72
  21.6 7.7 %all-to-all-start = ((bf16[2,16,16,3584]{3,2,0,1:T(8,128)(2,1)}), bf16[2,16,16,3584]{3,2,0,1:T(8,128)(2,1)}, u32[]{:S(2)}, u32[]{:S(2)}) async-start(bf16[2,16,16,3584]{3,2,0,1:T(8,128)(2,1)} %copy.13), calls=%async_computation | async-start | bytes 7340032 | tf_op jit(solution)/shard_map/all_to_all | solution.py:71
  29.3 0.2 convert_reduce_fusion
  29.5 0.2 fusion.23
  29.7 0.3 fusion.17
  30.1 110.5 %all-to-all-done = bf16[2,16,16,3584]{3,2,0,1:T(8,128)(2,1)} async-done(((bf16[2,16,16,3584]{3,2,0,1:T(8,128)(2,1)}), bf16[2,16,16,3584]{3,2,0,1:T(8,128)(2,1)}, u32[]{:S(2)}, u32[]{:S(2)}) %all-to-all-start) | async-done | bytes 3670048 | tf_op jit(solution)/shard_map/all_to_all | solution.py:71
  140.6 3.6 %fusion.28 = (bf16[1,16,16,3584]{3,2,0,1:T(8,128)(2,1)S(1)}, bf16[1,16,16,3584]{3,2,0,1:T(8,128)(2,1)}) fusion(bf16[2,16,16,3584]{3,2,0,1:T(8,128)(2,1)} %all-to-all-done), kind=kLoop, calls=%fused_computation.49 | loop fusion | bytes 7340032 | tf_op jit(solution)/shard_map/slice | solution.py:42
  144.2 6.9 %all-gather.3.cloned.1.call-done = bf16[1280,3584]{0,1:T(8,128)(2,1)} async-done(((bf16[1280,224]{0,1:T(8,128)(2,1)}), bf16[1280,3584]{0,1:T(8,128)(2,1)}) %all-gather.3.cloned.1.call-update) | async-done | bytes 9175056 | tf_op jit(solution)/shard_map/all_gather | solution.py:37
  151.1 7.9 %fusion.16 = (f32[1280]{0:T(1024)S(1)}, f32[256]{0:T(256)S(1)}, f32[256]{0:T(256)S(1)}, f32[256,1280]{1,0:T(8,128)}) fusion(bf16[256,1280]{1,0:T(8,128)(2,1)S(1)} %copy-done, f32[256]{0:T(256)S(1)} %add_rsqrt_fusion.1, f32[256]{0:T(256)S(1)} %broadcast_multiply_fusion.3, f32[1280]{0:T(1024)S(1)} %copy-done.5, bf16[256,3584]{1,0:T(8,128)(2,1)} %bitcast.32, ...), kind=kOutput, calls=%fused_computation.23 | convolution fusion | flops 2352412928 | bytes 12990464 | tf_op jit(solution)/shard_map/dot_general | solution.py:35
  158.9 75.5 %all-gather.5.cloned.1.call-done = bf16[1280,3584]{0,1:T(8,128)(2,1)} async-done(((bf16[1280,224]{0,1:T(8,128)(2,1)}), bf16[1280,3584]{0,1:T(8,128)(2,1)}) %all-gather.5.cloned.1.call-update) | async-done | bytes 9175056 | tf_op jit(solution)/shard_map/all_gather | solution.py:43
  234.5 7.2 %fusion.22 = (f32[1280]{0:T(1024)S(1)}, f32[256]{0:T(256)S(1)}, f32[256,1280]{1,0:T(8,128)}) fusion(bf16[256,1280]{1,0:T(8,128)(2,1)S(1)} %copy-done.1, f32[256]{0:T(256)S(1)} %add_rsqrt_fusion, f32[1280]{0:T(1024)S(1)} %copy-done.4, bf16[256,3584]{1,0:T(8,128)(2,1)S(1)} %bitcast.31, bf16[1280,3584]{0,1:T(8,128)(2,1)} %all-gather.5.cloned.1.call-done), kind=kOutput, calls=%fused_computation.29 | convolution fusion | flops 2351757824 | bytes 12988416 | tf_op jit(solution)/shard_map/dot_general | solution.py:41
  241.7 58.9 %all-reduce = (f32[1,1280]{1,0:T(1,128)S(1)}, f32[1,1280]{1,0:T(1,128)S(1)}) all-reduce(f32[1,1280]{1,0:T(1,128)S(1)} %stack.10, f32[1,1280]{1,0:T(1,128)S(1)} %stack.9), channel_id=1, replica_groups=mesh['groups'=2,'seq'=16] {'seq'}, use_global_device_ids=true, to_apply=%region_13.14 | all-reduce | flops 2560 | bytes 20480 | tf_op jit(solution)/shard_map/psum | solution.py:77
  300.6 0.6 pad_maximum_fusion
  301.2 2.6 fusion.21
  303.8 1.3 fusion.15
  (22 shorter events, 0.1 us)
Async XLA Ops:
  7.2 3.8 %copy-start.3 = (s32[256,1]{0,1:T(1,128)S(1)}, s32[256,1]{0,1:T(1,128)}, u32[]{:S(2)}) copy-start(s32[256,1]{0,1:T(1,128)} %param.9) | copy-start | bytes 3076
  7.2 143.9 %all-gather.3.cloned.1.call-start = ((), (), s32[]{:S(2)}) async-start(), calls=%async_computation.1 | async-start | bytes 9748480 | tf_op jit(solution)/shard_map/all_gather | solution.py:37
  7.9 226.6 %all-gather.5.cloned.1.call-start = ((), (), s32[]{:S(2)}) async-start(), calls=%async_computation.2 | async-start | bytes 9748480 | tf_op jit(solution)/shard_map/all_gather | solution.py:43
  21.6 7.8 %copy-start = (bf16[256,1280]{1,0:T(8,128)(2,1)S(1)}, bf16[256,1280]{1,0:T(8,128)(2,1)}, u32[]{:S(2)}) copy-start(bf16[256,1280]{1,0:T(8,128)(2,1)} %param.12) | copy-start | bytes 1966084
  21.6 7.9 %copy-start.1 = (bf16[256,1280]{1,0:T(8,128)(2,1)S(1)}, bf16[256,1280]{1,0:T(8,128)(2,1)}, u32[]{:S(2)}) copy-start(bf16[256,1280]{1,0:T(8,128)(2,1)} %param.13) | copy-start | bytes 1966084
  21.6 119.0 %all-to-all-start = ((bf16[2,16,16,3584]{3,2,0,1:T(8,128)(2,1)}), bf16[2,16,16,3584]{3,2,0,1:T(8,128)(2,1)}, u32[]{:S(2)}, u32[]{:S(2)}) async-start(bf16[2,16,16,3584]{3,2,0,1:T(8,128)(2,1)} %copy.13), calls=%async_computation | async-start | bytes 7340032 | tf_op jit(solution)/shard_map/all_to_all | solution.py:71
  30.1 121.0 %copy-start.5 = (f32[1280]{0:T(1024)S(1)}, f32[1280]{0:T(1024)}, u32[]{:S(2)}) copy-start(f32[1280]{0:T(1024)} %param.14) | copy-start | bytes 15364
  151.1 83.4 %copy-start.4 = (f32[1280]{0:T(1024)S(1)}, f32[1280]{0:T(1024)}, u32[]{:S(2)}) copy-start(f32[1280]{0:T(1024)} %param.15) | copy-start | bytes 15364
  301.2 2.6 copy-start.2
Sparse Core Ops, SparseCore 0:
  10.3 140.7 all-gather.2
  153.3 81.0 all-gather.4
where the time goes:
time: 312 us
  waiting for transfers between devices  194 us (62%)
  blocking collectives  58.9 us (19%)
  matrix products  15.1 us (5%)
  local copies, waits for them, and re-layouts  14.4 us (5%)
  between operations  14.1 us (5%)
  starting transfers between devices  7.81 us (3%)
  other arithmetic  7.27 us (2%)
    all_to_all x1, waiting for transfers between devices, on_device(): lax.all_to_all(packed.reshape(2, devices, cap, width), 'seq', split_axis=...  111 us
    all_gather x1, waiting for transfers between devices, project_back(): lax.all_gather(vision_proj, 'seq', axis=1, tiled=True)  75.5 us
    psum x1, blocking collectives, on_device(): audio_total, vision_total = lax.psum((audio_part, vision_part), 'seq')  58.9 us
    dot_general x1, matrix products, project_back(): lax.dot_general(inputs[0], lax.all_gather(audio_proj, 'seq', axis=1, tile...  7.87 us
    all_to_all x1, starting transfers between devices, on_device(): lax.all_to_all(packed.reshape(2, devices, cap, width), 'seq', split_axis=...  7.74 us
    dot_general x1, matrix products, project_back(): lax.dot_general(inputs[1], lax.all_gather(vision_proj, 'seq', axis=1, til...  7.22 us
    all_gather x1, waiting for transfers between devices, project_back(): lax.all_gather(audio_proj, 'seq', axis=1, tiled=True)  6.88 us
    scatter x1, local copies, waits for them, and re-layouts, on_device(): jnp.zeros((kinds * cap, width), grad_rows.dtype).at[position].set(grad_rows)  6.45 us
  transfers between devices with their start and end apart: 3, of which 3 were waited for; matrix products, arithmetic and copies ran while one was open for 8% of the time, Pallas kernels for 0%

commit v1 on v0

v1 whole, which is shorter than its diff:
```python
import functools

import jax
import jax.numpy as jnp
from jax import lax
from jax.experimental import pallas as pl
from jax.experimental.pallas import tpu as pltpu
from jax.sharding import PartitionSpec as P

F32 = jnp.float32
BF16 = jnp.bfloat16
BOTH = ("groups", "seq")
BIG = 48 * 1024 * 1024
VM = pl.BlockSpec(memory_space=pltpu.VMEM)
SM = pl.BlockSpec(memory_space=pltpu.SMEM)
ANY = pl.BlockSpec(memory_space=pl.ANY)


def place(line, pair, core):
    return (line * 2 + pair) * 2 + core


def flip(value, bit, devices):
    return lax.ppermute(value, "seq", [(i, i ^ bit) for i in range(devices)])


def along(value, moves):
    pairs = []
    for a, b in moves:
        for p in range(2):
            for c in range(2):
                pairs.append((place(a, p, c), place(b, p, c)))
    return lax.ppermute(value, "seq", pairs)


def across(value, lines, devices):
    pairs = []
    for a in lines:
        for p in range(2):
            for c in range(2):
                i = place(a, p, c)
                pairs += [(i, devices + i), (devices + i, i)]
    return lax.ppermute(value, BOTH, pairs)


def multiply(blocks, mine_w, other_w, masks, keep_ref, send_ref):
    rows = blocks[0].shape[0]
    for i, (ref, start) in enumerate(blocks_of(blocks)):
        lhs = ref[start : start + rows, :]
        one = jnp.dot(lhs, mine_w[...], preferred_element_type=F32)
        two = jnp.dot(lhs, other_w[...], preferred_element_type=F32)
        value = jnp.where(masks[i * rows : (i + 1) * rows, :] > 0, one, two)
        half = (i // 2) * rows
        if i % 2 == 0:
            keep_ref[half : half + rows, :] = value
        else:
            send_ref[half : half + rows, :] = value.astype(BF16)


def blocks_of(blocks):
    own, pair, far = blocks
    return [(own, 0), (pair, 0), (far, 0), (far, own.shape[0])]


def product_line(*refs):
    line, masks, own, pair, far = refs[:5]
    parts = refs[5:17]
    keep_ref, send_ref, mine_w, other_w, sems = refs[17:]
    deep = parts[0].shape[0]
    choice = {0: (0, 2, 4, 5), 1: (1, 0, 2, 3), 2: (3, 1, 0, 2), 3: (5, 4, 1, 0)}
    for where, order in choice.items():

        @pl.when(line[0] == where)
        def _():
            for s, k in enumerate(order):
                rows = pl.ds(s * deep, deep)
                pltpu.make_async_copy(parts[k], mine_w.at[rows], sems.at[s]).start()
                pltpu.make_async_copy(parts[6 + k], other_w.at[rows], sems.at[4 + s]).start()

    for s in range(4):
        rows = pl.ds(s * deep, deep)
        pltpu.make_async_copy(parts[0], mine_w.at[rows], sems.at[s]).wait()
        pltpu.make_async_copy(parts[6], other_w.at[rows], sems.at[4 + s]).wait()
    multiply((own, pair, far), mine_w, other_w, masks, keep_ref, send_ref)


def product_plain(masks, own, pair, far, mine_w, other_w, keep_ref, send_ref):
    multiply((own, pair, far), mine_w, other_w, masks, keep_ref, send_ref)


def pack(base_col, base_row, keep, recv, out):
    total = keep.shape[0]
    first = lax.broadcasted_iota(jnp.int32, (total, total), 0)
    second = lax.broadcasted_iota(jnp.int32, (total, total), 1)
    same = jnp.logical_and(base_col[...] == base_row[...], first < second)
    count = jnp.sum(same.astype(F32), axis=0, keepdims=True).astype(jnp.int32)
    slot = base_row[...] + count
    up = (keep[...] + recv[...].astype(F32)).astype(BF16)
    step = out.shape[0] // 2
    for i in range(2):
        place_of = lax.broadcasted_iota(jnp.int32, (step, total), 0) + i * step
        pick = (place_of == slot).astype(F32).astype(BF16)
        out[i * step : (i + 1) * step, :] = jnp.dot(pick, up, preferred_element_type=F32).astype(BF16)


def norms(recv, a_states, v_states, a_gain, v_gain, a_out, v_out, gains):
    rows, width = a_states.shape
    half = width // 2
    inv = 1.0 / width

    def upstream(h, m):
        return recv[:, h, :, m].reshape(rows, half).astype(F32)

    def cols(h):
        return slice(h * half, (h + 1) * half)

    h = a_states[...].astype(F32)
    mu = jnp.sum(h, axis=1, keepdims=True) * inv
    centred = h - mu
    scale = lax.rsqrt(jnp.sum(centred * centred, axis=1, keepdims=True) * inv + 1e-5)
    normed = centred * scale
    ps, pn, parts = 0.0, 0.0, []
    for k in range(2):
        u = upstream(k, 0)
        n = normed[:, cols(k)]
        p = u * a_gain[:, cols(k)]
        ps = ps + jnp.sum(p, axis=1, keepdims=True)
        pn = pn + jnp.sum(p * n, axis=1, keepdims=True)
        gains[0:1, cols(k)] = jnp.sum(u * n, axis=0, keepdims=True)
        parts.append((p, n))
    for k in range(2):
        p, n = parts[k]
        a_out[:, cols(k)] = (scale * (p - ps * inv - n * (pn * inv))).astype(BF16)

    h = v_states[...].astype(F32)
    scale = lax.rsqrt(jnp.sum(h * h, axis=1, keepdims=True) * inv + 1e-6)
    normed = h * scale
    pn, parts = 0.0, []
    for k in range(2):
        u = upstream(k, 1)
        n = normed[:, cols(k)]
        p = u * v_gain[:, cols(k)]
        pn = pn + jnp.sum(p * n, axis=1, keepdims=True)
        gains[1:2, cols(k)] = jnp.sum(u * n, axis=0, keepdims=True)
        parts.append((p, n))
    for k in range(2):
        p, n = parts[k]
        v_out[:, cols(k)] = (scale * (p - n * (pn * inv))).astype(BF16)


def call(body, outs, specs, scratch=()):
    return pl.pallas_call(
        body,
        out_shape=outs,
        in_specs=specs,
        out_specs=jax.tree.map(lambda _: VM, outs),
        scratch_shapes=list(scratch),
        compiler_params=pltpu.CompilerParams(vmem_limit_bytes=BIG),
    )


def on_device(
    grad_rows,
    route_ids,
    audio_proj,
    vision_proj,
    audio_states,
    vision_states,
    audio_gain,
    vision_gain,
):
    devices = lax.axis_size("seq")
    lines = devices // 4
    rows, width = grad_rows.shape
    enc, k = audio_proj.shape
    half = enc // 2
    cap = rows // devices
    group = lax.axis_index("groups")
    me = lax.axis_index("seq")
    line, pair, core = me // 4, (me // 2) % 2, me % 2

    both = jnp.stack([audio_proj.T, vision_proj.T])
    keep = lax.dynamic_slice_in_dim(both, core * half, half, axis=2)
    give = lax.dynamic_slice_in_dim(both, (1 - core) * half, half, axis=2)
    got = flip(give, 1, devices)
    own = jnp.concatenate(
        [jnp.where(core == 0, keep, got), jnp.where(core == 0, got, keep)], axis=1
    )
    mine = jnp.where(group == 0, own[0], own[1])
    other = jnp.where(group == 0, own[1], own[0])

    ids = route_ids[:, 0]
    split = grad_rows.reshape(rows, lines, 2, 2 * k)
    near = jnp.where(pair == 0, split[:, :, 0], split[:, :, 1]).reshape(rows, lines * 2 * k)
    away = jnp.where(pair == 0, split[:, :, 1], split[:, :, 0]).reshape(rows, lines * 2 * k)
    partner = flip(away, 2, devices)
    far = flip(jnp.concatenate([near, partner]), 1, devices)
    pair_ids = flip(ids, 2, devices)
    far_ids = flip(jnp.concatenate([ids, pair_ids]), 1, devices)
    all_ids = jnp.concatenate([ids, pair_ids, far_ids])
    masks = (all_ids // devices == group).astype(jnp.int32)[:, None]

    outs = (
        jax.ShapeDtypeStruct((2 * rows, half), F32),
        jax.ShapeDtypeStruct((2 * rows, half), BF16),
    )
    if lines == 4:
        right1 = along(mine, [(0, 1), (1, 2), (2, 3)])
        left1 = along(mine, [(1, 0), (2, 1), (3, 2)])
        two_mid = along(jnp.where(line == 1, right1, left1), [(1, 2), (2, 1)])
        two_end = along(jnp.where(line == 1, left1, right1), [(2, 3), (1, 0)])
        three = along(two_mid, [(2, 3), (1, 0)])
        parts = [
            (mine, other),
            (right1, across(right1, [1, 2, 3], devices)),
            (left1, across(left1, [0, 1, 2], devices)),
            (two_mid, across(two_mid, [1, 2], devices)),
            (two_end, across(two_end, [0, 3], devices)),
            (three, across(three, [0, 3], devices)),
        ]
        scratch = [pltpu.VMEM((8 * k, half), BF16)] * 2 + [pltpu.SemaphoreType.DMA((8,))]
        kept, sent = call(product_line, outs, [SM] + [VM] * 4 + [ANY] * 12, scratch)(
            line.reshape(1), masks, near, partner, far, *[p[0] for p in parts], *[p[1] for p in parts]
        )
    else:
        groups = [[place(a, p, c) for a in range(lines)] for p in range(2) for c in range(2)]
        mine_w = lax.all_gather(mine, "seq", axis=0, tiled=True, axis_index_groups=groups)
        other_w = lax.all_gather(other, "seq", axis=0, tiled=True, axis_index_groups=groups)
        kept, sent = call(product_plain, outs, [VM] * 6)(masks, near, partner, far, mine_w, other_w)
    taken = flip(sent, 2, devices)

    src_ids = jnp.concatenate([ids, far_ids[:rows]])
    src_core = jnp.concatenate([jnp.full((rows,), core), jnp.full((rows,), 1 - core)])
    base = (src_ids % devices) * (4 * cap) + src_core * (2 * cap) + (src_ids // devices) * cap
    packed = call(pack, jax.ShapeDtypeStruct((4 * rows, half), BF16), [VM] * 4)(
        base[:, None], base[None, :], kept, taken
    )
    arrived = lax.all_to_all(packed.reshape(devices, 4 * cap, half), "seq", 0, 0, tiled=True)
    arrived = arrived.reshape(devices // 2, 2, 2, 2, cap, half)
    if cap % 16 != 0:
        arrived = arrived.transpose(1, 3, 0, 2, 4, 5).reshape(1, 2, 1, 2, rows, half)

    audio_grad, vision_grad, gains = call(
        norms,
        (
            jax.ShapeDtypeStruct((rows, enc), BF16),
            jax.ShapeDtypeStruct((rows, enc), BF16),
            jax.ShapeDtypeStruct((2, enc), F32),
        ),
        [VM] * 5,
    )(arrived, audio_states, vision_states, audio_gain[None, :], vision_gain[None, :])
    bit = 1
    while bit < devices:
        gains = gains + flip(gains, bit, devices)
        bit *= 2
    return (audio_grad, vision_grad, gains)


def solution(mesh):
    placed = (
        P(("groups", "seq"), None),
        P(("groups", "seq"), None),
        P(None, "seq"),
        P(None, "seq"),
        P(("groups", "seq"), None),
        P(("groups", "seq"), None),
        P(),
        P(),
    )
    return jax.shard_map(
        on_device,
        mesh=mesh,
        in_specs=placed,
        out_specs=(P(("groups", "seq"), None), P(("groups", "seq"), None), P("groups", None)),
        check_vma=False,
    )
```

time: 312 us -> 172 us (0.55)
  waiting for transfers between devices: 194 us -> 91.8 us
  blocking collectives: 58.9 us -> 0 us
  starting transfers between devices: 7.81 us -> 45.6 us
  Pallas kernels: 0 us -> 15.4 us
  matrix products: 15.1 us -> 0 us
  between operations: 14.1 us -> 0.93 us
  local copies, waits for them, and re-layouts: 14.4 us -> 9.06 us
    all_to_all x1, waiting for transfers between devices: 111 us -> 27.4 us  [on_device(): lax.all_to_all(packed.reshape(devices, 4 * cap, half), 'seq', 0, 0, tiled...]
    all_gather x2 -> x0, waiting for transfers between devices: 82.4 us -> none  [the longest x1 75.5 us: project_back(): lax.all_gather(vision_proj, 'seq', axis=1, tiled=True)]
    ppermute x0 -> x20, waiting for transfers between devices: none -> 64.5 us  [the longest x10 37.4 us: flip(): return lax.ppermute(value, 'seq', [(i, i ^ bit) for i in range(devices)])]
    psum x1 -> x0, blocking collectives: 58.9 us -> none  [on_device(): audio_total, vision_total = lax.psum((audio_part, vision_part), 'seq')]
    ppermute x0 -> x20, starting transfers between devices: none -> 37.8 us  [the longest x10 17.1 us: flip(): return lax.ppermute(value, 'seq', [(i, i ^ bit) for i in range(devices)])]
    pallas_call x0 -> x3, Pallas kernels: none -> 15.4 us  [the longest x1 10.7 us: on_device(): call(product_line, outs, [SM] + [VM] * 4 + [ANY] * 12, scratch)]
    dot_general x2 -> x0, matrix products: 15.1 us -> none  [the longest x1 7.87 us: project_back(): lax.dot_general(inputs[0], lax.all_gather(audio_proj, 'seq', axis=1, tile...]
    scatter x1 -> x0, local copies, waits for them, and re-layouts: 6.45 us -> none  [on_device(): jnp.zeros((kinds * cap, width), grad_rows.dtype).at[position].set(grad_rows)]
  transfers between devices with their start and end apart: 3 -> 21, of which waited for: 3 -> 13; matrix products, arithmetic and copies ran while one was open for 8% -> 7% of each run, Pallas kernels for 0% -> 0%
where the time goes in v1:
time: 172 us; the launch traced here: 171 us
  waiting for transfers between devices  91.8 us (53%)
  starting transfers between devices  45.6 us (27%)
  Pallas kernels  15.4 us (9%)
  local copies, waits for them, and re-layouts  9.06 us (5%)
  other arithmetic  8.15 us (5%)
    ppermute x10, waiting for transfers between devices, flip(): return lax.ppermute(value, 'seq', [(i, i ^ bit) for i in range(devices)])  37.4 us
    all_to_all x1, waiting for transfers between devices, on_device(): lax.all_to_all(packed.reshape(devices, 4 * cap, half), 'seq', 0, 0, tiled...  27.4 us
    ppermute x10, starting transfers between devices, flip(): return lax.ppermute(value, 'seq', [(i, i ^ bit) for i in range(devices)])  17.1 us
    ppermute x5, waiting for transfers between devices, along(): return lax.ppermute(value, 'seq', pairs)  15.1 us
    ppermute x5, starting transfers between devices, across(): return lax.ppermute(value, BOTH, pairs)  12.7 us
    ppermute x5, waiting for transfers between devices, across(): return lax.ppermute(value, BOTH, pairs)  12 us
    pallas_call x1, Pallas kernels, on_device(): call(product_line, outs, [SM] + [VM] * 4 + [ANY] * 12, scratch)  10.7 us
    ppermute x5, starting transfers between devices, along(): return lax.ppermute(value, 'seq', pairs)  8.09 us
  transfers between devices with their start and end apart: 21, of which 13 were waited for; matrix products, arithmetic and copies ran while one was open for 7% of the time, Pallas kernels for 0%

profile of v1, /device:TPU:0, one launch (start us, length us, event | category | flops | bytes accessed | tf_op | source)
XLA Modules:
  0.0 171.0 jit_solution(11347132470701215689)
XLA Ops:
  0.7 1.9 %fusion.1 = bf16[2,224,640]{2,1,0:T(8,128)(2,1)} fusion(s32[]{:T(128)S(6)} %select_n.120, bf16[1,224,1280]{2,1,0:T(8,128)(2,1)} %bitcast.27, bf16[1,224,1280]{2,1,0:T(8,128)(2,1)} %bitcast.29), kind=kLoop, calls=%fused_computation.14 | loop fusion | flops 1146880 | bytes 1720324 | tf_op jit(solution)/shard_map/stack | solution.py:182
  3.0 2.9 %copy.26 = bf16[256,3584]{0,1:T(8,128)(2,1)S(1)} copy(bf16[256,3584]{1,0:T(8,128)(2,1)} %param.8) | data formatting | bytes 3670016 | tf_op args[0]
  8.3 2.5 %collective-permute-start.2 = (bf16[256,1792]{1,0:T(8,128)(2,1)}, bf16[256,1792]{1,0:T(8,128)(2,1)}, u32[]{:S(2)}, u32[]{:S(2)}) collective-permute-start(bf16[256,1792]{1,0:T(8,128)(2,1)} %copy.27), channel_id=1, source_target_pairs={{0,2},{1,3},{2,0},{3,1},{4,6},{5,7},{6,4},{7,5},{8,10},{9,11},{10,... | collective-permute-start | bytes 2752520 | tf_op jit(solution)/shard_map/ppermute | solution.py:24
  11.3 3.5 %collective-permute-start.5 = (bf16[448,640]{1,0:T(8,128)(2,1)S(1)}, bf16[448,640]{1,0:T(8,128)(2,1)S(1)}, u32[]{:S(2)}, u32[]{:S(2)}) collective-permute-start(bf16[448,640]{1,0:T(8,128)(2,1)S(1)} %get-tuple-element.18.refs_5_), channel_id=1, source_target_pairs={{0,4},{1,5},{2,6},{3,7},{4,8},{5,9},{6,10},{7,11},{8,12},{9,13},{1... | collective-permute-start | bytes 1720328 | tf_op jit(solution)/shard_map/ppermute | solution.py:33
  17.6 14.5 %collective-permute-done.2.refs_3_ = bf16[256,1792]{1,0:T(8,128)(2,1)} collective-permute-done((bf16[256,1792]{1,0:T(8,128)(2,1)}, bf16[256,1792]{1,0:T(8,128)(2,1)}, u32[]{:S(2)}, u32[]{:S(2)}) %collective-permute-start.2) | collective-permute-done | bytes 917536 | tf_op jit(solution)/shard_map/ppermute | solution.py:24
  32.2 2.5 %pad_maximum_fusion = bf16[512,1792]{1,0:T(8,128)(2,1)} fusion(bf16[256,1792]{1,0:T(8,128)(2,1)} %collective-permute-done.2.refs_3_, bf16[256,1792]{1,0:T(8,128)(2,1)S(1)} %copy.29.refs_2_), kind=kLoop, calls=%fused_computation | loop fusion | flops 3670016 | bytes 3670016 | tf_op jit(solution)/shard_map/concatenate | solution.py:197
  38.9 1.8 %collective-permute-start = (s32[256]{0:T(256)S(1)}, s32[256]{0:T(256)S(1)}, u32[]{:S(2)}, u32[]{:S(2)}) collective-permute-start(s32[256]{0:T(256)S(1)} %bitcast.31), channel_id=1, source_target_pairs={{0,2},{1,3},{2,0},{3,1},{4,6},{5,7},{6,4},{7,5},{8,10},{9,11},{10,... | collective-permute-start | bytes 3080 | tf_op jit(solution)/shard_map/ppermute | solution.py:24
  40.7 1.8 %collective-permute-done = s32[256]{0:T(256)S(1)} collective-permute-done((s32[256]{0:T(256)S(1)}, s32[256]{0:T(256)S(1)}, u32[]{:S(2)}, u32[]{:S(2)}) %collective-permute-start) | collective-permute-done | bytes 1056 | tf_op jit(solution)/shard_map/ppermute | solution.py:24
  43.7 3.7 %collective-permute-start.11 = (bf16[448,640]{1,0:T(8,128)(2,1)S(1)}, bf16[448,640]{1,0:T(8,128)(2,1)}, u32[]{:S(2)}, u32[]{:S(2)}) collective-permute-start(bf16[448,640]{1,0:T(8,128)(2,1)S(1)} %collective-permute-done.6.refs_7_), channel_id=1, source_target_pairs={{0,16},{16,0},{1,17},{17,1},{2,18},{18,2},{3,19},{19,3},{4,20},{20... | collective-permute-start | bytes 1720328 | tf_op jit(solution)/shard_map/ppermute | solution.py:43
  47.3 7.4 %collective-permute-done.8.refs_9_ = bf16[448,640]{1,0:T(8,128)(2,1)S(1)} collective-permute-done((bf16[448,640]{1,0:T(8,128)(2,1)S(1)}, bf16[448,640]{1,0:T(8,128)(2,1)S(1)}, u32[]{:S(2)}, u32[]{:S(2)}) %collective-permute-start.8) | collective-permute-done | bytes 573472 | tf_op jit(solution)/shard_map/ppermute | solution.py:33
  57.1 3.4 %collective-permute-start.13 = (bf16[448,640]{1,0:T(8,128)(2,1)S(1)}, bf16[448,640]{1,0:T(8,128)(2,1)}, u32[]{:S(2)}, u32[]{:S(2)}) collective-permute-start(bf16[448,640]{1,0:T(8,128)(2,1)S(1)} %collective-permute-done.8.refs_9_), channel_id=1, source_target_pairs={{0,16},{16,0},{1,17},{17,1},{2,18},{18,2},{3,19},{19,3},{12,28},{2... | collective-permute-start | bytes 1720328 | tf_op jit(solution)/shard_map/ppermute | solution.py:43
  60.5 7.7 %collective-permute-done.9.refs_10_ = bf16[448,640]{1,0:T(8,128)(2,1)} collective-permute-done((bf16[448,640]{1,0:T(8,128)(2,1)S(1)}, bf16[448,640]{1,0:T(8,128)(2,1)}, u32[]{:S(2)}, u32[]{:S(2)}) %collective-permute-start.9) | collective-permute-done | bytes 573472 | tf_op jit(solution)/shard_map/ppermute | solution.py:33
  68.1 3.4 %collective-permute-start.14 = (bf16[448,640]{1,0:T(8,128)(2,1)}, bf16[448,640]{1,0:T(8,128)(2,1)}, u32[]{:S(2)}, u32[]{:S(2)}) collective-permute-start(bf16[448,640]{1,0:T(8,128)(2,1)} %collective-permute-done.9.refs_10_), channel_id=1, source_target_pairs={{0,16},{16,0},{1,17},{17,1},{2,18},{18,2},{3,19},{19,3},{12,28},{2... | collective-permute-start | bytes 1720328 | tf_op jit(solution)/shard_map/ppermute | solution.py:43
  74.9 11.1 %collective-permute-done.14.refs_16_ = bf16[448,640]{1,0:T(8,128)(2,1)} collective-permute-done((bf16[448,640]{1,0:T(8,128)(2,1)}, bf16[448,640]{1,0:T(8,128)(2,1)}, u32[]{:S(2)}, u32[]{:S(2)}) %collective-permute-start.14) | collective-permute-done | bytes 573472 | tf_op jit(solution)/shard_map/ppermute | solution.py:43
  86.0 10.7 %shard_map.103 = (f32[512,640]{1,0:T(8,128)}, bf16[512,640]{1,0:T(8,128)(2,1)}) custom-call(s32[1]{0:T(128)} %bitcast.3.refs_0_, s32[1024,1]{1,0:T(8,128)S(1)} %fusion.6.refs_1_, bf16[256,1792]{1,0:T(8,128)(2,1)} %copy-done.5, bf16[256,1792]{1,0:T(8,128)(2,1)} %collective-permute-done.2.refs_3_, bf16[512,1792]{1,0:T(8,128)(2,1)} %collective-permute-done.3.refs_4_, ...), custom_call_target="tpu_custom_call" | custom-call | tf_op jit(solution)/shard_map/pallas_call | solution.py:222
  98.5 14.1 %collective-permute-done.15.recv = bf16[512,640]{1,0:T(8,128)(2,1)S(1)} collective-permute-done((bf16[512,640]{1,0:T(8,128)(2,1)}, bf16[512,640]{1,0:T(8,128)(2,1)S(1)}, u32[]{:S(2)}, u32[]{:S(2)}) %collective-permute-start.15) | collective-permute-done | bytes 655392 | tf_op jit(solution)/shard_map/ppermute | solution.py:24
  113.9 2.2 %shard_map.104 = bf16[1024,640]{1,0:T(8,128)(2,1)} custom-call(s32[512,1]{1,0:T(8,128)S(1)} %copy.30.base_col, s32[1,512]{1,0:T(1,128)S(1)} %bitcast.23, f32[512,640]{1,0:T(8,128)S(1)} %copy-done, bf16[512,640]{1,0:T(8,128)(2,1)S(1)} %collective-permute-done.15.recv), custom_call_target="tpu_custom_call" | custom-call | tf_op jit(solution)/shard_map/pallas_call | solution.py:235
  116.2 7.8 %all-to-all-start = ((bf16[16,64,640]{2,1,0:T(8,128)(2,1)}), bf16[16,64,640]{2,1,0:T(8,128)(2,1)S(1)}, u32[]{:S(2)}, u32[]{:S(2)}) async-start(bf16[16,64,640]{2,1,0:T(8,128)(2,1)} %bitcast.15), calls=%async_computation | async-start | bytes 2621440 | tf_op jit(solution)/shard_map/all_to_all | solution.py:238
  124.0 27.4 %all-to-all-done = bf16[16,64,640]{2,1,0:T(8,128)(2,1)S(1)} async-done(((bf16[16,64,640]{2,1,0:T(8,128)(2,1)}), bf16[16,64,640]{2,1,0:T(8,128)(2,1)S(1)}, u32[]{:S(2)}, u32[]{:S(2)}) %all-to-all-start) | async-done | bytes 1310752 | tf_op jit(solution)/shard_map/all_to_all | solution.py:238
  151.4 2.5 %shard_map.105 = (bf16[256,1280]{1,0:T(8,128)(2,1)}, bf16[256,1280]{1,0:T(8,128)(2,1)}, f32[2,1280]{1,0:T(2,128)S(1)}) custom-call(bf16[8,2,2,2,16,640]{5,4,3,2,1,0:T(8,128)(2,1)S(1)} %bitcast.21, bf16[256,1280]{1,0:T(8,128)(2,1)S(1)} %copy-done.1, bf16[256,1280]{1,0:T(8,128)(2,1)S(1)} %copy-done.2, f32[1,1280]{1,0:T(1,128)S(1)} %broadcast_in_dim.20.a_gain, ...), custom_call_target="tpu_custom_call" | custom-call | tf_op jit(solution)/shard_map/pallas_call | solution.py:243
  155.5 2.3 %collective-permute-start.17 = (f32[2,1280]{1,0:T(2,128)S(1)}, f32[2,1280]{1,0:T(2,128)S(1)}, u32[]{:S(2)}, u32[]{:S(2)}) collective-permute-start(f32[2,1280]{1,0:T(2,128)S(1)} %add.57), channel_id=1, source_target_pairs={{0,2},{1,3},{2,0},{3,1},{4,6},{5,7},{6,4},{7,5},{8,10},{9,11},{10,... | collective-permute-start | bytes 30728 | tf_op jit(solution)/shard_map/ppermute | solution.py:24
  159.4 3.8 %collective-permute-start.18 = (f32[2,1280]{1,0:T(2,128)S(1)}, f32[2,1280]{1,0:T(2,128)S(1)}, u32[]{:S(2)}, u32[]{:S(2)}) collective-permute-start(f32[2,1280]{1,0:T(2,128)S(1)} %add.58), channel_id=1, source_target_pairs={{0,4},{1,5},{2,6},{3,7},{4,0},{5,1},{6,2},{7,3},{8,12},{9,13},{10,... | collective-permute-start | bytes 30728 | tf_op jit(solution)/shard_map/ppermute | solution.py:24
  163.3 1.7 collective-permute-done.18
  164.9 3.8 %collective-permute-start.19 = (f32[2,1280]{1,0:T(2,128)S(1)}, f32[2,1280]{1,0:T(2,128)S(1)}, u32[]{:S(2)}, u32[]{:S(2)}) collective-permute-start(f32[2,1280]{1,0:T(2,128)S(1)} %add.59), channel_id=1, source_target_pairs={{0,8},{1,9},{2,10},{3,11},{4,12},{5,13},{6,14},{7,15},{8,0},{9,1},... | collective-permute-start | bytes 30728 | tf_op jit(solution)/shard_map/ppermute | solution.py:24
  (66 shorter events, 25.6 us)
Async XLA Ops:
  2.6 8.3 %collective-permute-start.4 = (bf16[2,224,640]{2,1,0:T(8,128)(2,1)}, bf16[2,224,640]{2,1,0:T(8,128)(2,1)S(1)}, u32[]{:S(2)}, u32[]{:S(2)}) collective-permute-start(bf16[2,224,640]{2,1,0:T(8,128)(2,1)} %fusion.1), channel_id=1, source_target_pairs={{0,1},{1,0},{2,3},{3,2},{4,5},{5,4},{6,7},{7,6},{8,9},{9,8},{10,11... | collective-permute-start | bytes 1720328 | tf_op jit(solution)/shard_map/ppermute | solution.py:24
  8.3 23.8 %collective-permute-start.2 = (bf16[256,1792]{1,0:T(8,128)(2,1)}, bf16[256,1792]{1,0:T(8,128)(2,1)}, u32[]{:S(2)}, u32[]{:S(2)}) collective-permute-start(bf16[256,1792]{1,0:T(8,128)(2,1)} %copy.27), channel_id=1, source_target_pairs={{0,2},{1,3},{2,0},{3,1},{4,6},{5,7},{6,4},{7,5},{8,10},{9,11},{10,... | collective-permute-start | bytes 2752520 | tf_op jit(solution)/shard_map/ppermute | solution.py:24
  11.3 23.4 %collective-permute-start.5 = (bf16[448,640]{1,0:T(8,128)(2,1)S(1)}, bf16[448,640]{1,0:T(8,128)(2,1)S(1)}, u32[]{:S(2)}, u32[]{:S(2)}) collective-permute-start(bf16[448,640]{1,0:T(8,128)(2,1)S(1)} %get-tuple-element.18.refs_5_), channel_id=1, source_target_pairs={{0,4},{1,5},{2,6},{3,7},{4,8},{5,9},{6,10},{7,11},{8,12},{9,13},{1... | collective-permute-start | bytes 1720328 | tf_op jit(solution)/shard_map/ppermute | solution.py:33
  14.8 19.9 %collective-permute-start.6 = (bf16[448,640]{1,0:T(8,128)(2,1)S(1)}, bf16[448,640]{1,0:T(8,128)(2,1)S(1)}, u32[]{:S(2)}, u32[]{:S(2)}) collective-permute-start(bf16[448,640]{1,0:T(8,128)(2,1)S(1)} %get-tuple-element.18.refs_5_), channel_id=1, source_target_pairs={{4,0},{5,1},{6,2},{7,3},{8,4},{9,5},{10,6},{11,7},{12,8},{13,9},{1... | collective-permute-start | bytes 1720328 | tf_op jit(solution)/shard_map/ppermute | solution.py:33
  17.6 17.1 %copy-start.5 = (bf16[256,1792]{1,0:T(8,128)(2,1)}, bf16[256,1792]{1,0:T(8,128)(2,1)S(1)}, u32[]{:S(2)}) copy-start(bf16[256,1792]{1,0:T(8,128)(2,1)S(1)} %copy.29.refs_2_) | copy-start | bytes 2752516
  34.7 40.2 %collective-permute-start.3 = (bf16[512,1792]{1,0:T(8,128)(2,1)}, bf16[512,1792]{1,0:T(8,128)(2,1)}, u32[]{:S(2)}, u32[]{:S(2)}) collective-permute-start(bf16[512,1792]{1,0:T(8,128)(2,1)} %pad_maximum_fusion), channel_id=1, source_target_pairs={{0,1},{1,0},{2,3},{3,2},{4,5},{5,4},{6,7},{7,6},{8,9},{9,8},{10,11... | collective-permute-start | bytes 5505032 | tf_op jit(solution)/shard_map/ppermute | solution.py:24
  34.8 2.7 %collective-permute-start.7 = (bf16[448,640]{1,0:T(8,128)(2,1)S(1)}, bf16[448,640]{1,0:T(8,128)(2,1)S(1)}, u32[]{:S(2)}, u32[]{:S(2)}) collective-permute-start(bf16[448,640]{1,0:T(8,128)(2,1)S(1)} %get-tuple-element.20), channel_id=1, source_target_pairs={{4,8},{5,9},{6,10},{7,11},{8,4},{9,5},{10,6},{11,7},{20,24},{21,25... | collective-permute-start | bytes 1720328 | tf_op jit(solution)/shard_map/ppermute | solution.py:33
  35.5 19.2 %collective-permute-start.8 = (bf16[448,640]{1,0:T(8,128)(2,1)S(1)}, bf16[448,640]{1,0:T(8,128)(2,1)S(1)}, u32[]{:S(2)}, u32[]{:S(2)}) collective-permute-start(bf16[448,640]{1,0:T(8,128)(2,1)S(1)} %get-tuple-element.19), channel_id=1, source_target_pairs={{8,12},{9,13},{10,14},{11,15},{4,0},{5,1},{6,2},{7,3},{24,28},{25,... | collective-permute-start | bytes 1720328 | tf_op jit(solution)/shard_map/ppermute | solution.py:33
  36.8 19.4 %collective-permute-start.10 = (bf16[448,640]{1,0:T(8,128)(2,1)S(1)}, bf16[448,640]{1,0:T(8,128)(2,1)S(1)}, u32[]{:S(2)}, u32[]{:S(2)}) collective-permute-start(bf16[448,640]{1,0:T(8,128)(2,1)S(1)} %collective-permute-done.5.refs_6_), channel_id=1, source_target_pairs={{4,20},{20,4},{5,21},{21,5},{6,22},{22,6},{7,23},{23,7},{8,24},{24... | collective-permute-start | bytes 1720328 | tf_op jit(solution)/shard_map/ppermute | solution.py:43
  37.6 30.6 %collective-permute-start.9 = (bf16[448,640]{1,0:T(8,128)(2,1)S(1)}, bf16[448,640]{1,0:T(8,128)(2,1)}, u32[]{:S(2)}, u32[]{:S(2)}) collective-permute-start(bf16[448,640]{1,0:T(8,128)(2,1)S(1)} %collective-permute-done.7.refs_8_), channel_id=1, source_target_pairs={{8,12},{9,13},{10,14},{11,15},{4,0},{5,1},{6,2},{7,3},{24,28},{25,... | collective-permute-start | bytes 1720328 | tf_op jit(solution)/shard_map/ppermute | solution.py:33
  38.9 3.6 %collective-permute-start = (s32[256]{0:T(256)S(1)}, s32[256]{0:T(256)S(1)}, u32[]{:S(2)}, u32[]{:S(2)}) collective-permute-start(s32[256]{0:T(256)S(1)} %bitcast.31), channel_id=1, source_target_pairs={{0,2},{1,3},{2,0},{3,1},{4,6},{5,7},{6,4},{7,5},{8,10},{9,11},{10,... | collective-permute-start | bytes 3080 | tf_op jit(solution)/shard_map/ppermute | solution.py:24
  42.5 1.2 collective-permute-start.1
  43.7 30.4 %collective-permute-start.11 = (bf16[448,640]{1,0:T(8,128)(2,1)S(1)}, bf16[448,640]{1,0:T(8,128)(2,1)}, u32[]{:S(2)}, u32[]{:S(2)}) collective-permute-start(bf16[448,640]{1,0:T(8,128)(2,1)S(1)} %collective-permute-done.6.refs_7_), channel_id=1, source_target_pairs={{0,16},{16,0},{1,17},{17,1},{2,18},{18,2},{3,19},{19,3},{4,20},{20... | collective-permute-start | bytes 1720328 | tf_op jit(solution)/shard_map/ppermute | solution.py:43
  54.8 19.3 %collective-permute-start.12 = (bf16[448,640]{1,0:T(8,128)(2,1)S(1)}, bf16[448,640]{1,0:T(8,128)(2,1)}, u32[]{:S(2)}, u32[]{:S(2)}) collective-permute-start(bf16[448,640]{1,0:T(8,128)(2,1)S(1)} %collective-permute-done.7.refs_8_), channel_id=1, source_target_pairs={{4,20},{20,4},{5,21},{21,5},{6,22},{22,6},{7,23},{23,7},{8,24},{24... | collective-permute-start | bytes 1720328 | tf_op jit(solution)/shard_map/ppermute | solution.py:43
  57.1 17.9 %collective-permute-start.13 = (bf16[448,640]{1,0:T(8,128)(2,1)S(1)}, bf16[448,640]{1,0:T(8,128)(2,1)}, u32[]{:S(2)}, u32[]{:S(2)}) collective-permute-start(bf16[448,640]{1,0:T(8,128)(2,1)S(1)} %collective-permute-done.8.refs_9_), channel_id=1, source_target_pairs={{0,16},{16,0},{1,17},{17,1},{2,18},{18,2},{3,19},{19,3},{12,28},{2... | collective-permute-start | bytes 1720328 | tf_op jit(solution)/shard_map/ppermute | solution.py:43
  68.1 17.9 %collective-permute-start.14 = (bf16[448,640]{1,0:T(8,128)(2,1)}, bf16[448,640]{1,0:T(8,128)(2,1)}, u32[]{:S(2)}, u32[]{:S(2)}) collective-permute-start(bf16[448,640]{1,0:T(8,128)(2,1)} %collective-permute-done.9.refs_10_), channel_id=1, source_target_pairs={{0,16},{16,0},{1,17},{17,1},{2,18},{18,2},{3,19},{19,3},{12,28},{2... | collective-permute-start | bytes 1720328 | tf_op jit(solution)/shard_map/ppermute | solution.py:43
  96.7 15.8 %collective-permute-start.15 = (bf16[512,640]{1,0:T(8,128)(2,1)}, bf16[512,640]{1,0:T(8,128)(2,1)S(1)}, u32[]{:S(2)}, u32[]{:S(2)}) collective-permute-start(bf16[512,640]{1,0:T(8,128)(2,1)} %get-tuple-element.9), channel_id=1, source_target_pairs={{0,2},{1,3},{2,0},{3,1},{4,6},{5,7},{6,4},{7,5},{8,10},{9,11},{10,... | collective-permute-start | bytes 1966088 | tf_op jit(solution)/shard_map/ppermute | solution.py:24
  116.1 35.2 %copy-start.1 = (bf16[256,1280]{1,0:T(8,128)(2,1)S(1)}, bf16[256,1280]{1,0:T(8,128)(2,1)}, u32[]{:S(2)}) copy-start(bf16[256,1280]{1,0:T(8,128)(2,1)} %a_states.1) | copy-start | bytes 1966084
  116.1 35.2 %copy-start.2 = (bf16[256,1280]{1,0:T(8,128)(2,1)S(1)}, bf16[256,1280]{1,0:T(8,128)(2,1)}, u32[]{:S(2)}) copy-start(bf16[256,1280]{1,0:T(8,128)(2,1)} %v_states.1) | copy-start | bytes 1966084
  116.2 35.2 %all-to-all-start = ((bf16[16,64,640]{2,1,0:T(8,128)(2,1)}), bf16[16,64,640]{2,1,0:T(8,128)(2,1)S(1)}, u32[]{:S(2)}, u32[]{:S(2)}) async-start(bf16[16,64,640]{2,1,0:T(8,128)(2,1)} %bitcast.15), calls=%async_computation | async-start | bytes 2621440 | tf_op jit(solution)/shard_map/all_to_all | solution.py:238
  153.9 1.6 collective-permute-start.16
  155.5 4.0 %collective-permute-start.17 = (f32[2,1280]{1,0:T(2,128)S(1)}, f32[2,1280]{1,0:T(2,128)S(1)}, u32[]{:S(2)}, u32[]{:S(2)}) collective-permute-start(f32[2,1280]{1,0:T(2,128)S(1)} %add.57), channel_id=1, source_target_pairs={{0,2},{1,3},{2,0},{3,1},{4,6},{5,7},{6,4},{7,5},{8,10},{9,11},{10,... | collective-permute-start | bytes 30728 | tf_op jit(solution)/shard_map/ppermute | solution.py:24
  159.4 5.5 %collective-permute-start.18 = (f32[2,1280]{1,0:T(2,128)S(1)}, f32[2,1280]{1,0:T(2,128)S(1)}, u32[]{:S(2)}, u32[]{:S(2)}) collective-permute-start(f32[2,1280]{1,0:T(2,128)S(1)} %add.58), channel_id=1, source_target_pairs={{0,4},{1,5},{2,6},{3,7},{4,0},{5,1},{6,2},{7,3},{8,12},{9,13},{10,... | collective-permute-start | bytes 30728 | tf_op jit(solution)/shard_map/ppermute | solution.py:24
  164.9 5.5 %collective-permute-start.19 = (f32[2,1280]{1,0:T(2,128)S(1)}, f32[2,1280]{1,0:T(2,128)S(1)}, u32[]{:S(2)}, u32[]{:S(2)}) collective-permute-start(f32[2,1280]{1,0:T(2,128)S(1)} %add.59), channel_id=1, source_target_pairs={{0,8},{1,9},{2,10},{3,11},{4,12},{5,13},{6,14},{7,15},{8,0},{9,1},... | collective-permute-start | bytes 30728 | tf_op jit(solution)/shard_map/ppermute | solution.py:24
  (8 other events, 43.1 us)

commit v2 on v1

v2 whole, which is shorter than its diff:
```python
import functools

import jax
import jax.numpy as jnp
from jax import lax
from jax.experimental import pallas as pl
from jax.experimental.pallas import tpu as pltpu
from jax.sharding import PartitionSpec as P

F32 = jnp.float32
BF16 = jnp.bfloat16
BOTH = ("groups", "seq")
BIG = 48 * 1024 * 1024
VM = pl.BlockSpec(memory_space=pltpu.VMEM)
SM = pl.BlockSpec(memory_space=pltpu.SMEM)
ANY = pl.BlockSpec(memory_space=pl.ANY)


def flip(value, bits, devices):
    return lax.ppermute(value, "seq", [(i, i ^ bits) for i in range(devices)])


def spot(p, low, devices):
    group, line = (0, p) if p < 4 else (1, 7 - p)
    return group * devices + line * 4 + low


def cycle(value, moves, devices):
    pairs = [(spot(a, w, devices), spot(b, w, devices)) for a, b in moves for w in range(4)]
    return lax.ppermute(value, BOTH, pairs)


def gather_cycle(block, p, devices):
    fwd, bwd = [block], [block]
    for k in (1, 2, 3):
        up = [(a, (a + 1) % 8) for a in range(8)]
        down = [(a, (a - 1) % 8) for a in range(8)]
        if k == 3:
            up = [(a, b) for a, b in up if (b - k) % 8 != 7 - b]
            down = [(a, b) for a, b in down if (b + k) % 8 != 7 - b]
        fwd.append(cycle(fwd[-1], up, devices))
        bwd.append(cycle(bwd[-1], down, devices))
    first = (p % 4 == 0) | (p % 4 == 1)
    inner = cycle(jnp.where(first, bwd[1], fwd[1]), [(a, 7 - a) for a in (1, 2, 5, 6)], devices)
    outer = cycle(jnp.where(first, bwd[3], fwd[3]), [(a, 7 - a) for a in (0, 3, 4, 7)], devices)
    return fwd[1:] + bwd[1:] + [inner, outer]


def cut(place, a_ref, v_ref, keep, to_core, to_pair, to_both, sems):
    pair, core = place[0], place[1]
    half = keep.shape[1]
    near = pl.ds(pl.multiple_of(pair * half, 128), half)
    away = pl.ds(pl.multiple_of((1 - pair) * half, 128), half)
    for here in range(2):
        mine, other = (a_ref, v_ref) if here == 0 else (v_ref, a_ref)

        @pl.when(core == here)
        def _():
            pltpu.make_async_copy(other.at[:, near], to_core, sems.at[0]).start()
            pltpu.make_async_copy(mine.at[:, near], keep, sems.at[1]).start()
            pltpu.make_async_copy(mine.at[:, away], to_pair, sems.at[2]).start()
            pltpu.make_async_copy(other.at[:, away], to_both, sems.at[3]).start()

    for i, out in enumerate((to_core, keep, to_pair, to_both)):
        pltpu.make_async_copy(a_ref.at[:, near], out, sems.at[i]).wait()


def one_hot_pack(lhs, w, base_col, base_row, source, out):
    rows = lhs[0].shape[0]
    devices, sources, cap, half = out.shape
    first = lax.broadcasted_iota(jnp.int32, (rows, rows), 0)
    second = lax.broadcasted_iota(jnp.int32, (rows, rows), 1)
    slots = lax.broadcasted_iota(jnp.int32, (devices * cap, rows), 0)
    for s in range(4):
        col = base_col[s * rows : (s + 1) * rows, :]
        row = base_row[:, s * rows : (s + 1) * rows]
        same = jnp.logical_and(col == row, first < second)
        count = jnp.sum(same.astype(F32), axis=0, keepdims=True).astype(jnp.int32)
        pick = (slots == row + count).astype(F32).astype(BF16)
        up = jnp.dot(lhs[s][...], w[...], preferred_element_type=F32).astype(BF16)
        packed = jnp.dot(pick, up, preferred_element_type=F32).astype(BF16)
        out[:, source[s]] = packed.reshape(devices, cap, half)


def product_cycle(*refs):
    place, source, base_col, base_row = refs[:4]
    lhs, parts = refs[4:8], refs[8:28]
    out, w, sems = refs[28:]
    deep = parts[0].shape[0]
    p, x = place[0], place[1]

    def spread(op):
        for chain in range(2):
            own, pair, f1, f2, f3, b1, b2, b3, inner, outer = parts[chain * 10 : chain * 10 + 10]
            which = jnp.where(chain == 0, x, 1 - x)

            def move(ref, q, i):
                group = q // 4
                line = jnp.where(group == 0, q, 7 - q)
                start = pl.multiple_of(((line * 2 + which) * 2 + group) * deep, 16)
                op(pltpu.make_async_copy(ref, w.at[pl.ds(start, deep)], sems.at[chain * 8 + i]))

            move(own, p, 0)
            move(pair, 7 - p, 1)
            far = (p + 4) % 8
            ends = p % 4
            for i, (ref, step) in enumerate(((f1, 7), (f2, 6), (f3, 5), (b1, 1), (b2, 2), (b3, 3))):
                q = (p + step) % 8

                @pl.when(q != 7 - p)
                def _():
                    move(ref, q, 2 + i if i < 5 else 7)

            spare = jnp.where(ends == 0, 2, jnp.where(ends == 1, 4, jnp.where(ends == 2, 7, 5)))

            @pl.when((ends == 0) | (ends == 3))
            def _():
                move(outer, far, spare)

            @pl.when((ends == 1) | (ends == 2))
            def _():
                move(inner, far, spare)

    spread(lambda c: c.start())
    spread(lambda c: c.wait())
    one_hot_pack(lhs, w, base_col, base_row, source, out)


def product_plain(base_col, base_row, l0, l1, l2, l3, w, out):
    rows = l0.shape[0]
    total = 4 * rows
    first = lax.broadcasted_iota(jnp.int32, (total, total), 0)
    second = lax.broadcasted_iota(jnp.int32, (total, total), 1)
    same = jnp.logical_and(base_col[...] == base_row[...], first < second)
    slot = base_row[...] + jnp.sum(same.astype(F32), axis=0, keepdims=True).astype(jnp.int32)
    slots = lax.broadcasted_iota(jnp.int32, (total, rows), 0)
    acc = jnp.zeros(out.shape, F32)
    for s, ref in enumerate((l0, l1, l2, l3)):
        pick = (slots == slot[:, s * rows : (s + 1) * rows]).astype(F32).astype(BF16)
        up = jnp.dot(ref[...], w[...], preferred_element_type=F32).astype(BF16)
        acc = acc + jnp.dot(pick, up, preferred_element_type=F32)
    out[...] = acc.astype(BF16)


def norms(recv, a_states, v_states, a_gain, v_gain, a_out, v_out, gains):
    rows, width = a_states.shape
    half = width // 2
    inv = 1.0 / width

    def upstream(h, m):
        return recv[:, h, m].reshape(rows, half).astype(F32)

    def cols(h):
        return slice(h * half, (h + 1) * half)

    h = a_states[...].astype(F32)
    mu = jnp.sum(h, axis=1, keepdims=True) * inv
    centred = h - mu
    scale = lax.rsqrt(jnp.sum(centred * centred, axis=1, keepdims=True) * inv + 1e-5)
    normed = centred * scale
    ps, pn, parts = 0.0, 0.0, []
    for k in range(2):
        u = upstream(k, 0)
        n = normed[:, cols(k)]
        p = u * a_gain[:, cols(k)]
        ps = ps + jnp.sum(p, axis=1, keepdims=True)
        pn = pn + jnp.sum(p * n, axis=1, keepdims=True)
        gains[0:1, cols(k)] = jnp.sum(u * n, axis=0, keepdims=True)
        parts.append((p, n))
    for k in range(2):
        p, n = parts[k]
        a_out[:, cols(k)] = (scale * (p - ps * inv - n * (pn * inv))).astype(BF16)

    h = v_states[...].astype(F32)
    scale = lax.rsqrt(jnp.sum(h * h, axis=1, keepdims=True) * inv + 1e-6)
    normed = h * scale
    pn, parts = 0.0, []
    for k in range(2):
        u = upstream(k, 1)
        n = normed[:, cols(k)]
        p = u * v_gain[:, cols(k)]
        pn = pn + jnp.sum(p * n, axis=1, keepdims=True)
        gains[1:2, cols(k)] = jnp.sum(u * n, axis=0, keepdims=True)
        parts.append((p, n))
    for k in range(2):
        p, n = parts[k]
        v_out[:, cols(k)] = (scale * (p - n * (pn * inv))).astype(BF16)


def call(body, outs, specs, scratch=(), out_spec=VM):
    return pl.pallas_call(
        body,
        out_shape=outs,
        in_specs=specs,
        out_specs=jax.tree.map(lambda _: out_spec, outs),
        scratch_shapes=list(scratch),
        compiler_params=pltpu.CompilerParams(vmem_limit_bytes=BIG),
    )


def on_device(
    grad_rows,
    route_ids,
    audio_proj,
    vision_proj,
    audio_states,
    vision_states,
    audio_gain,
    vision_gain,
):
    devices = lax.axis_size("seq")
    lines = devices // 4
    rows, width = grad_rows.shape
    enc, k = audio_proj.shape
    half = enc // 2
    cap = rows // devices
    group = lax.axis_index("groups")
    me = lax.axis_index("seq")
    line, pair, core = me // 4, (me // 2) % 2, me % 2

    block = jax.ShapeDtypeStruct((k, half), BF16)
    if lines == 4:
        keep, to_core, to_pair, to_both = call(
            cut, (block,) * 4, [SM, ANY, ANY], [pltpu.SemaphoreType.DMA((4,))], ANY
        )(jnp.stack([pair, core]), audio_proj.T, vision_proj.T)
    else:
        both = jnp.stack([audio_proj.T, vision_proj.T]).reshape(2, k, 2, half)
        pick = lambda m, h: both[m, :, h]
        keep, to_core = pick(core, pair), pick(1 - core, pair)
        to_pair, to_both = pick(core, 1 - pair), pick(1 - core, 1 - pair)
    from_core = flip(to_core, 1, devices)
    from_pair = flip(to_pair, 2, devices)
    from_both = flip(to_both, 3, devices)

    r_pair = flip(grad_rows, 2, devices)
    r_core = flip(grad_rows, 1, devices)
    r_both = flip(r_pair, 1, devices)
    ids = route_ids[:, 0]
    i_pair = flip(ids, 2, devices)
    i_far = flip(jnp.concatenate([ids, i_pair]), 1, devices)
    all_ids = jnp.concatenate([ids, i_pair, i_far])
    lhs = (grad_rows, r_pair, r_core, r_both)
    low = me % 4
    source = jnp.stack([low, low ^ 2, low ^ 1, low ^ 3])
    named = all_ids // devices == core

    if lines == 4:
        p = jnp.where(group == 0, line, 7 - line)
        straight = core == group
        block1 = jnp.where(straight, keep, from_core)
        mirror1 = jnp.where(straight, from_core, keep)
        block2 = jnp.where(straight, from_pair, from_both)
        mirror2 = jnp.where(straight, from_both, from_pair)
        parts1 = [block1, mirror1] + gather_cycle(block1, p, devices)
        parts2 = [block2, mirror2] + gather_cycle(block2, p, devices)
        base = jnp.where(named, all_ids % devices * cap, -(2 * rows))
        packed = call(
            product_cycle,
            jax.ShapeDtypeStruct((devices, 4, cap, half), BF16),
            [SM, SM] + [VM] * 6 + [ANY] * 20,
            [pltpu.VMEM((width, half), BF16), pltpu.SemaphoreType.DMA((16,))],
        )(jnp.stack([p, pair]), source, base[:, None], base[None, :], *lhs, *parts1, *parts2)
        packed = packed.reshape(devices, 4 * cap, half)
    else:
        straight = jnp.stack([keep, from_pair, from_core, from_both])
        plane = jnp.zeros_like(straight).at[source].set(straight)
        ranks = [[a * 4 + w for a in range(lines)] for w in range(4)]
        w = lax.all_gather(plane.reshape(4 * k, half), "seq", axis=0, tiled=True, axis_index_groups=ranks)
        where_from = jnp.repeat(source, rows)
        base = jnp.where(named, (all_ids % devices * 4 + where_from) * cap, -(8 * rows))
        packed = call(product_plain, jax.ShapeDtypeStruct((4 * rows, half), BF16), [VM] * 7)(
            base[:, None], base[None, :], *lhs, w
        )
        packed = packed.reshape(devices, 4 * cap, half)

    arrived = lax.all_to_all(packed, "seq", 0, 0, tiled=True)
    arrived = arrived.reshape(lines, 2, 2, 4, cap, half)
    if cap % 16 != 0:
        arrived = arrived.transpose(1, 2, 0, 3, 4, 5).reshape(1, 2, 2, 1, rows, half)

    audio_grad, vision_grad, gains = call(
        norms,
        (
            jax.ShapeDtypeStruct((rows, enc), BF16),
            jax.ShapeDtypeStruct((rows, enc), BF16),
            jax.ShapeDtypeStruct((2, enc), F32),
        ),
        [VM] * 5,
    )(arrived, audio_states, vision_states, audio_gain[None, :], vision_gain[None, :])
    bit = 1
    while bit < devices:
        near = flip(gains, bit, devices)
        if 2 * bit < devices:
            far = flip(gains, 2 * bit, devices) + flip(gains, 3 * bit, devices)
            gains = (gains + near) + far
        else:
            gains = gains + near
        bit *= 4
    return (audio_grad, vision_grad, gains)


def solution(mesh):
    placed = (
        P(("groups", "seq"), None),
        P(("groups", "seq"), None),
        P(None, "seq"),
        P(None, "seq"),
        P(("groups", "seq"), None),
        P(("groups", "seq"), None),
        P(),
        P(),
    )
    return jax.shard_map(
        on_device,
        mesh=mesh,
        in_specs=placed,
        out_specs=(P(("groups", "seq"), None), P(("groups", "seq"), None), P("groups", None)),
        check_vma=False,
    )
```

time: 172 us -> 191 us (1.11)
  waiting for transfers between devices: 91.8 us -> 114 us
  other arithmetic: 8.15 us -> 5.72 us
    ppermute x20 -> x30, waiting for transfers between devices: 64.5 us -> 86.5 us  [the longest x14 55.2 us: flip(): return lax.ppermute(value, 'seq', [(i, i ^ bits) for i in range(devices)])]
    select_n x4 -> x8, other arithmetic: 1.63 us -> 4.86 us  [the longest x2 2.36 us: on_device(): base = jnp.where(named, all_ids % devices * cap, -(2 * rows))]
    select_n x2 -> x0, local copies, waits for them, and re-layouts: 2.83 us -> none  [the longest x1 1.46 us: on_device(): jnp.where(pair == 0, split[:, :, 0], split[:, :, 1])]
    concatenate x3 -> x2, other arithmetic: 2.53 us -> 0.01 us  [the longest x1 0.01 us: on_device(): i_far = flip(jnp.concatenate([ids, i_pair]), 1, devices)]
    unnamed x23 -> x30, local copies, waits for them, and re-layouts: 5.04 us -> 6.72 us
    ppermute x20 -> x30, starting transfers between devices: 37.8 us -> 39.1 us  [the longest x16 24 us: cycle(): return lax.ppermute(value, BOTH, pairs)]
  transfers between devices with their start and end apart: 21 -> 31, of which waited for: 13 -> 19; matrix products, arithmetic and copies ran while one was open for 7% -> 3% of each run, Pallas kernels for 0% -> 0%
where the time goes in v2:
time: 191 us; the launch traced here: 190 us
  waiting for transfers between devices  114 us (60%)
  starting transfers between devices  45.4 us (24%)
  Pallas kernels  16.4 us (9%)
  local copies, waits for them, and re-layouts  7.75 us (4%)
  other arithmetic  5.72 us (3%)
    ppermute x14, waiting for transfers between devices, flip(): return lax.ppermute(value, 'seq', [(i, i ^ bits) for i in range(devices)])  55.2 us
    ppermute x16, waiting for transfers between devices, cycle(): return lax.ppermute(value, BOTH, pairs)  31.3 us
    all_to_all x1, waiting for transfers between devices, on_device(): arrived = lax.all_to_all(packed, 'seq', 0, 0, tiled=True)  27.4 us
    ppermute x16, starting transfers between devices, cycle(): return lax.ppermute(value, BOTH, pairs)  24 us
    ppermute x14, starting transfers between devices, flip(): return lax.ppermute(value, 'seq', [(i, i ^ bits) for i in range(devices)])  15.1 us
    pallas_call x1, Pallas kernels, on_device(): call(product_cycle, jax.ShapeDtypeStruct((devices, 4, cap, half), BF16),...  13.2 us
    unnamed x30, local copies, waits for them, and re-layouts  6.72 us
    all_to_all x1, starting transfers between devices, on_device(): arrived = lax.all_to_all(packed, 'seq', 0, 0, tiled=True)  6.31 us
  transfers between devices with their start and end apart: 31, of which 19 were waited for; matrix products, arithmetic and copies ran while one was open for 3% of the time, Pallas kernels for 0%

profile of v2, /device:TPU:0, one launch (start us, length us, event | category | flops | bytes accessed | tf_op | source)
XLA Modules:
  0.0 190.0 jit_solution(9134845030279179112)
XLA Ops:
  0.6 3.0 %collective-permute-start.2 = (bf16[256,3584]{1,0:T(8,128)(2,1)}, bf16[256,3584]{1,0:T(8,128)(2,1)}, u32[]{:S(2)}, u32[]{:S(2)}) collective-permute-start(bf16[256,3584]{1,0:T(8,128)(2,1)} %refs_4_.1), channel_id=1, source_target_pairs={{0,2},{1,3},{2,0},{3,1},{4,6},{5,7},{6,4},{7,5},{8,10},{9,11},{10,... | collective-permute-start | bytes 5505032 | tf_op jit(solution)/shard_map/ppermute | solution.py:20
  8.8 42.0 %collective-permute-done.14 = bf16[224,640]{1,0:T(8,128)(2,1)S(1)} collective-permute-done((bf16[224,640]{1,0:T(8,128)(2,1)S(1)}, bf16[224,640]{1,0:T(8,128)(2,1)S(1)}, u32[]{:S(2)}, u32[]{:S(2)}) %collective-permute-start.14) | collective-permute-done | bytes 286752 | tf_op jit(solution)/shard_map/ppermute | solution.py:20
  50.8 4.6 %collective-permute-done.15 = bf16[224,640]{1,0:T(8,128)(2,1)S(1)} collective-permute-done((bf16[224,640]{1,0:T(8,128)(2,1)S(1)}, bf16[224,640]{1,0:T(8,128)(2,1)S(1)}, u32[]{:S(2)}, u32[]{:S(2)}) %collective-permute-start.15) | collective-permute-done | bytes 286752 | tf_op jit(solution)/shard_map/ppermute | solution.py:20
  61.0 4.2 %collective-permute-done.16.refs_20_ = bf16[224,640]{1,0:T(8,128)(2,1)S(1)} collective-permute-done((bf16[224,640]{1,0:T(8,128)(2,1)S(1)}, bf16[224,640]{1,0:T(8,128)(2,1)S(1)}, u32[]{:S(2)}, u32[]{:S(2)}) %collective-permute-start.16) | collective-permute-done | bytes 286752 | tf_op jit(solution)/shard_map/ppermute | solution.py:30
  68.3 4.2 %collective-permute-done.9.refs_13_ = bf16[224,640]{1,0:T(8,128)(2,1)S(1)} collective-permute-done((bf16[224,640]{1,0:T(8,128)(2,1)S(1)}, bf16[224,640]{1,0:T(8,128)(2,1)S(1)}, u32[]{:S(2)}, u32[]{:S(2)}) %collective-permute-start.9) | collective-permute-done | bytes 286752 | tf_op jit(solution)/shard_map/ppermute | solution.py:30
  74.7 2.5 %collective-permute-done.17.refs_21_ = bf16[224,640]{1,0:T(8,128)(2,1)S(1)} collective-permute-done((bf16[224,640]{1,0:T(8,128)(2,1)S(1)}, bf16[224,640]{1,0:T(8,128)(2,1)S(1)}, u32[]{:S(2)}, u32[]{:S(2)}) %collective-permute-start.17) | collective-permute-done | bytes 286752 | tf_op jit(solution)/shard_map/ppermute | solution.py:30
  79.0 3.4 %collective-permute-done.20.refs_24_ = bf16[224,640]{1,0:T(8,128)(2,1)} collective-permute-done((bf16[224,640]{1,0:T(8,128)(2,1)S(1)}, bf16[224,640]{1,0:T(8,128)(2,1)}, u32[]{:S(2)}, u32[]{:S(2)}) %collective-permute-start.20) | collective-permute-done | bytes 286752 | tf_op jit(solution)/shard_map/ppermute | solution.py:30
  83.7 3.5 %collective-permute-done.10.refs_14_ = bf16[224,640]{1,0:T(8,128)(2,1)S(1)} collective-permute-done((bf16[224,640]{1,0:T(8,128)(2,1)S(1)}, bf16[224,640]{1,0:T(8,128)(2,1)S(1)}, u32[]{:S(2)}, u32[]{:S(2)}) %collective-permute-start.10) | collective-permute-done | bytes 286752 | tf_op jit(solution)/shard_map/ppermute | solution.py:30
  87.2 2.2 %collective-permute-start.21 = (bf16[224,640]{1,0:T(8,128)(2,1)}, bf16[224,640]{1,0:T(8,128)(2,1)S(1)}, u32[]{:S(2)}, u32[]{:S(2)}) collective-permute-start(bf16[224,640]{1,0:T(8,128)(2,1)} %collective-permute-done.20.refs_24_), channel_id=1, source_target_pairs={{0,16},{1,17},{2,18},{3,19},{4,0},{5,1},{6,2},{7,3},{8,4},{9,5},{1... | collective-permute-start | bytes 860168 | tf_op jit(solution)/shard_map/ppermute | solution.py:30
  89.4 1.9 %collective-permute-start.11 = (bf16[224,640]{1,0:T(8,128)(2,1)S(1)}, bf16[224,640]{1,0:T(8,128)(2,1)S(1)}, u32[]{:S(2)}, u32[]{:S(2)}) collective-permute-start(bf16[224,640]{1,0:T(8,128)(2,1)S(1)} %collective-permute-done.10.refs_14_), channel_id=1, source_target_pairs={{0,16},{1,17},{2,18},{3,19},{4,0},{5,1},{6,2},{7,3},{8,4},{9,5},{1... | collective-permute-start | bytes 860168 | tf_op jit(solution)/shard_map/ppermute | solution.py:30
  94.2 4.9 %collective-permute-done.21.refs_25_ = bf16[224,640]{1,0:T(8,128)(2,1)S(1)} collective-permute-done((bf16[224,640]{1,0:T(8,128)(2,1)}, bf16[224,640]{1,0:T(8,128)(2,1)S(1)}, u32[]{:S(2)}, u32[]{:S(2)}) %collective-permute-start.21) | collective-permute-done | bytes 286752 | tf_op jit(solution)/shard_map/ppermute | solution.py:30
  100.5 2.5 %collective-permute-done.11.refs_15_ = bf16[224,640]{1,0:T(8,128)(2,1)S(1)} collective-permute-done((bf16[224,640]{1,0:T(8,128)(2,1)S(1)}, bf16[224,640]{1,0:T(8,128)(2,1)S(1)}, u32[]{:S(2)}, u32[]{:S(2)}) %collective-permute-start.11) | collective-permute-done | bytes 286752 | tf_op jit(solution)/shard_map/ppermute | solution.py:30
  104.4 2.2 %collective-permute-start.23 = (bf16[224,640]{1,0:T(8,128)(2,1)}, bf16[224,640]{1,0:T(8,128)(2,1)}, u32[]{:S(2)}, u32[]{:S(2)}) collective-permute-start(bf16[224,640]{1,0:T(8,128)(2,1)} %broadcast_select_fusion), channel_id=1, source_target_pairs={{0,16},{1,17},{2,18},{3,19},{12,28},{13,29},{14,30},{15,31},{28,12... | collective-permute-start | bytes 860168 | tf_op jit(solution)/shard_map/ppermute | solution.py:30
  108.1 3.6 %collective-permute-start.13 = (bf16[224,640]{1,0:T(8,128)(2,1)}, bf16[224,640]{1,0:T(8,128)(2,1)}, u32[]{:S(2)}, u32[]{:S(2)}) collective-permute-start(bf16[224,640]{1,0:T(8,128)(2,1)} %broadcast_select_fusion.2), channel_id=1, source_target_pairs={{0,16},{1,17},{2,18},{3,19},{12,28},{13,29},{14,30},{15,31},{28,12... | collective-permute-start | bytes 860168 | tf_op jit(solution)/shard_map/ppermute | solution.py:30
  112.8 2.3 %fusion.2.refs_2_ = s32[1024,1]{1,0:T(8,128)} fusion(s32[1024,1]{1,0:T(8,128)} %copy.15, s32[]{:T(128)} %select_n.142), kind=kLoop, calls=%fused_computation.7 | loop fusion | flops 22528 | bytes 8196 | tf_op jit(solution)/shard_map/jit(_where)/select_n | solution.py:256
  116.1 3.4 %collective-permute-done.13.refs_17_ = bf16[224,640]{1,0:T(8,128)(2,1)} collective-permute-done((bf16[224,640]{1,0:T(8,128)(2,1)}, bf16[224,640]{1,0:T(8,128)(2,1)}, u32[]{:S(2)}, u32[]{:S(2)}) %collective-permute-start.13) | collective-permute-done | bytes 286752 | tf_op jit(solution)/shard_map/ppermute | solution.py:30
  123.3 13.2 %shard_map.104 = bf16[16,4,16,640]{3,2,1,0:T(8,128)(2,1)} custom-call(s32[2]{0:T(128)S(1)} %pad_add_fusion.3.refs_0_, s32[4]{0:T(128)S(1)} %pad_add_fusion.4.refs_1_, s32[1024,1]{1,0:T(8,128)} %fusion.2.refs_2_, s32[1,1024]{1,0:T(1,128)S(1)} %compare_select_fusion.refs_3_, bf16[256,3584]{1,0:T(8,128)(2,1)} %refs_4_.1, ...), custom_call_target="tpu_custom_call" | custom-call | tf_op jit(solution)/shard_map/pallas_call | solution.py:257
  136.5 6.3 %all-to-all-start = ((bf16[16,64,640]{2,1,0:T(8,128)(2,1)}), bf16[16,64,640]{2,1,0:T(8,128)(2,1)S(1)}, u32[]{:S(2)}, u32[]{:S(2)}) async-start(bf16[16,64,640]{2,1,0:T(8,128)(2,1)} %bitcast.20), calls=%async_computation | async-start | bytes 2621440 | tf_op jit(solution)/shard_map/all_to_all | solution.py:276
  142.9 27.4 %all-to-all-done = bf16[16,64,640]{2,1,0:T(8,128)(2,1)S(1)} async-done(((bf16[16,64,640]{2,1,0:T(8,128)(2,1)}), bf16[16,64,640]{2,1,0:T(8,128)(2,1)S(1)}, u32[]{:S(2)}, u32[]{:S(2)}) %all-to-all-start) | async-done | bytes 1310752 | tf_op jit(solution)/shard_map/all_to_all | solution.py:276
  170.2 2.5 %shard_map.105 = (bf16[256,1280]{1,0:T(8,128)(2,1)}, bf16[256,1280]{1,0:T(8,128)(2,1)}, f32[2,1280]{1,0:T(2,128)S(1)}) custom-call(bf16[4,2,2,4,16,640]{5,4,3,2,1,0:T(8,128)(2,1)S(1)} %bitcast.17, bf16[256,1280]{1,0:T(8,128)(2,1)S(1)} %copy-done, bf16[256,1280]{1,0:T(8,128)(2,1)S(1)} %copy-done.1, f32[1,1280]{1,0:T(1,128)S(1)} %broadcast_in_dim.16.a_gain, ...), custom_call_target="tpu_custom_call" | custom-call | tf_op jit(solution)/shard_map/pallas_call | solution.py:281
  173.5 2.3 %collective-permute-start.25 = (f32[2,1280]{1,0:T(2,128)S(1)}, f32[2,1280]{1,0:T(2,128)S(1)}, u32[]{:S(2)}, u32[]{:S(2)}) collective-permute-start(f32[2,1280]{1,0:T(2,128)S(1)} %get-tuple-element.16), channel_id=1, source_target_pairs={{0,2},{1,3},{2,0},{3,1},{4,6},{5,7},{6,4},{7,5},{8,10},{9,11},{10,... | collective-permute-start | bytes 30728 | tf_op jit(solution)/shard_map/ppermute | solution.py:20
  178.9 3.7 %collective-permute-start.27 = (f32[2,1280]{1,0:T(2,128)S(1)}, f32[2,1280]{1,0:T(2,128)S(1)}, u32[]{:S(2)}, u32[]{:S(2)}) collective-permute-start(f32[2,1280]{1,0:T(2,128)S(1)} %add_add_fusion.1), channel_id=1, source_target_pairs={{0,4},{1,5},{2,6},{3,7},{4,0},{5,1},{6,2},{7,3},{8,12},{9,13},{10,... | collective-permute-start | bytes 30728 | tf_op jit(solution)/shard_map/ppermute | solution.py:20
  185.0 2.1 %collective-permute-done.28 = f32[2,1280]{1,0:T(2,128)S(1)} collective-permute-done((f32[2,1280]{1,0:T(2,128)S(1)}, f32[2,1280]{1,0:T(2,128)S(1)}, u32[]{:S(2)}, u32[]{:S(2)}) %collective-permute-start.28) | collective-permute-done | bytes 10272 | tf_op jit(solution)/shard_map/ppermute | solution.py:20
  187.2 2.3 %collective-permute-done.29 = f32[2,1280]{1,0:T(2,128)S(1)} collective-permute-done((f32[2,1280]{1,0:T(2,128)S(1)}, f32[2,1280]{1,0:T(2,128)S(1)}, u32[]{:S(2)}, u32[]{:S(2)}) %collective-permute-start.29) | collective-permute-done | bytes 10272 | tf_op jit(solution)/shard_map/ppermute | solution.py:20
  (89 shorter events, 39.1 us)
Async XLA Ops:
  0.6 64.5 %collective-permute-start.2 = (bf16[256,3584]{1,0:T(8,128)(2,1)}, bf16[256,3584]{1,0:T(8,128)(2,1)}, u32[]{:S(2)}, u32[]{:S(2)}) collective-permute-start(bf16[256,3584]{1,0:T(8,128)(2,1)} %refs_4_.1), channel_id=1, source_target_pairs={{0,2},{1,3},{2,0},{3,1},{4,6},{5,7},{6,4},{7,5},{8,10},{9,11},{10,... | collective-permute-start | bytes 5505032 | tf_op jit(solution)/shard_map/ppermute | solution.py:20
  6.5 44.3 %collective-permute-start.14 = (bf16[224,640]{1,0:T(8,128)(2,1)S(1)}, bf16[224,640]{1,0:T(8,128)(2,1)S(1)}, u32[]{:S(2)}, u32[]{:S(2)}) collective-permute-start(bf16[224,640]{1,0:T(8,128)(2,1)S(1)} %get-tuple-element.12), channel_id=1, source_target_pairs={{0,2},{1,3},{2,0},{3,1},{4,6},{5,7},{6,4},{7,5},{8,10},{9,11},{10,... | collective-permute-start | bytes 860168 | tf_op jit(solution)/shard_map/ppermute | solution.py:20
  6.7 48.8 %collective-permute-start.15 = (bf16[224,640]{1,0:T(8,128)(2,1)S(1)}, bf16[224,640]{1,0:T(8,128)(2,1)S(1)}, u32[]{:S(2)}, u32[]{:S(2)}) collective-permute-start(bf16[224,640]{1,0:T(8,128)(2,1)S(1)} %get-tuple-element.13), channel_id=1, source_target_pairs={{0,3},{1,2},{2,1},{3,0},{4,7},{5,6},{6,5},{7,4},{8,11},{9,10},{10,... | collective-permute-start | bytes 860168 | tf_op jit(solution)/shard_map/ppermute | solution.py:20
  7.5 50.1 %collective-permute-start.5 = (bf16[224,640]{1,0:T(8,128)(2,1)S(1)}, bf16[224,640]{1,0:T(8,128)(2,1)S(1)}, u32[]{:S(2)}, u32[]{:S(2)}) collective-permute-start(bf16[224,640]{1,0:T(8,128)(2,1)S(1)} %get-tuple-element.11), channel_id=1, source_target_pairs={{0,1},{1,0},{2,3},{3,2},{4,5},{5,4},{6,7},{7,6},{8,9},{9,8},{10,11... | collective-permute-start | bytes 860168 | tf_op jit(solution)/shard_map/ppermute | solution.py:20
  8.8 50.5 %collective-permute-start = (s32[256]{0:T(256)}, s32[256]{0:T(256)S(1)}, u32[]{:S(2)}, u32[]{:S(2)}) collective-permute-start(s32[256]{0:T(256)} %bitcast.21), channel_id=1, source_target_pairs={{0,2},{1,3},{2,0},{3,1},{4,6},{5,7},{6,4},{7,5},{8,10},{9,11},{10,... | collective-permute-start | bytes 3080 | tf_op jit(solution)/shard_map/ppermute | solution.py:20
  55.5 9.7 %collective-permute-start.16 = (bf16[224,640]{1,0:T(8,128)(2,1)S(1)}, bf16[224,640]{1,0:T(8,128)(2,1)S(1)}, u32[]{:S(2)}, u32[]{:S(2)}) collective-permute-start(bf16[224,640]{1,0:T(8,128)(2,1)S(1)} %get-tuple-element.18.refs_18_), channel_id=1, source_target_pairs={{0,4},{1,5},{2,6},{3,7},{4,8},{5,9},{6,10},{7,11},{8,12},{9,13},{1... | collective-permute-start | bytes 860168 | tf_op jit(solution)/shard_map/ppermute | solution.py:30
  57.1 9.6 %collective-permute-start.19 = (bf16[224,640]{1,0:T(8,128)(2,1)S(1)}, bf16[224,640]{1,0:T(8,128)(2,1)S(1)}, u32[]{:S(2)}, u32[]{:S(2)}) collective-permute-start(bf16[224,640]{1,0:T(8,128)(2,1)S(1)} %get-tuple-element.18.refs_18_), channel_id=1, source_target_pairs={{0,16},{1,17},{2,18},{3,19},{4,0},{5,1},{6,2},{7,3},{8,4},{9,5},{1... | collective-permute-start | bytes 860168 | tf_op jit(solution)/shard_map/ppermute | solution.py:30
  57.7 14.9 %collective-permute-start.9 = (bf16[224,640]{1,0:T(8,128)(2,1)S(1)}, bf16[224,640]{1,0:T(8,128)(2,1)S(1)}, u32[]{:S(2)}, u32[]{:S(2)}) collective-permute-start(bf16[224,640]{1,0:T(8,128)(2,1)S(1)} %get-tuple-element.20.refs_8_), channel_id=1, source_target_pairs={{0,16},{1,17},{2,18},{3,19},{4,0},{5,1},{6,2},{7,3},{8,4},{9,5},{1... | collective-permute-start | bytes 860168 | tf_op jit(solution)/shard_map/ppermute | solution.py:30
  60.5 12.4 %collective-permute-start.6 = (bf16[224,640]{1,0:T(8,128)(2,1)S(1)}, bf16[224,640]{1,0:T(8,128)(2,1)S(1)}, u32[]{:S(2)}, u32[]{:S(2)}) collective-permute-start(bf16[224,640]{1,0:T(8,128)(2,1)S(1)} %get-tuple-element.20.refs_8_), channel_id=1, source_target_pairs={{0,4},{1,5},{2,6},{3,7},{4,8},{5,9},{6,10},{7,11},{8,12},{9,13},{1... | collective-permute-start | bytes 860168 | tf_op jit(solution)/shard_map/ppermute | solution.py:30
  65.2 54.3 %collective-permute-start.3 = (bf16[256,3584]{1,0:T(8,128)(2,1)}, bf16[256,3584]{1,0:T(8,128)(2,1)}, u32[]{:S(2)}, u32[]{:S(2)}) collective-permute-start(bf16[256,3584]{1,0:T(8,128)(2,1)} %refs_4_.1), channel_id=1, source_target_pairs={{0,1},{1,0},{2,3},{3,2},{4,5},{5,4},{6,7},{7,6},{8,9},{9,8},{10,11... | collective-permute-start | bytes 5505032 | tf_op jit(solution)/shard_map/ppermute | solution.py:20
  65.2 54.3 %collective-permute-start.4 = (bf16[256,3584]{1,0:T(8,128)(2,1)}, bf16[256,3584]{1,0:T(8,128)(2,1)}, u32[]{:S(2)}, u32[]{:S(2)}) collective-permute-start(bf16[256,3584]{1,0:T(8,128)(2,1)} %collective-permute-done.2.refs_5_), channel_id=1, source_target_pairs={{0,1},{1,0},{2,3},{3,2},{4,5},{5,4},{6,7},{7,6},{8,9},{9,8},{10,11... | collective-permute-start | bytes 5505032 | tf_op jit(solution)/shard_map/ppermute | solution.py:20
  66.7 10.4 %collective-permute-start.17 = (bf16[224,640]{1,0:T(8,128)(2,1)S(1)}, bf16[224,640]{1,0:T(8,128)(2,1)S(1)}, u32[]{:S(2)}, u32[]{:S(2)}) collective-permute-start(bf16[224,640]{1,0:T(8,128)(2,1)S(1)} %collective-permute-done.16.refs_20_), channel_id=1, source_target_pairs={{0,4},{1,5},{2,6},{3,7},{4,8},{5,9},{6,10},{7,11},{8,12},{9,13},{1... | collective-permute-start | bytes 860168 | tf_op jit(solution)/shard_map/ppermute | solution.py:30
  72.5 9.8 %collective-permute-start.20 = (bf16[224,640]{1,0:T(8,128)(2,1)S(1)}, bf16[224,640]{1,0:T(8,128)(2,1)}, u32[]{:S(2)}, u32[]{:S(2)}) collective-permute-start(bf16[224,640]{1,0:T(8,128)(2,1)S(1)} %collective-permute-done.19.refs_23_), channel_id=1, source_target_pairs={{0,16},{1,17},{2,18},{3,19},{4,0},{5,1},{6,2},{7,3},{8,4},{9,5},{1... | collective-permute-start | bytes 860168 | tf_op jit(solution)/shard_map/ppermute | solution.py:30
  72.8 14.3 %collective-permute-start.10 = (bf16[224,640]{1,0:T(8,128)(2,1)S(1)}, bf16[224,640]{1,0:T(8,128)(2,1)S(1)}, u32[]{:S(2)}, u32[]{:S(2)}) collective-permute-start(bf16[224,640]{1,0:T(8,128)(2,1)S(1)} %collective-permute-done.9.refs_13_), channel_id=1, source_target_pairs={{0,16},{1,17},{2,18},{3,19},{4,0},{5,1},{6,2},{7,3},{8,4},{9,5},{1... | collective-permute-start | bytes 860168 | tf_op jit(solution)/shard_map/ppermute | solution.py:30
  77.2 12.2 %collective-permute-start.7 = (bf16[224,640]{1,0:T(8,128)(2,1)S(1)}, bf16[224,640]{1,0:T(8,128)(2,1)S(1)}, u32[]{:S(2)}, u32[]{:S(2)}) collective-permute-start(bf16[224,640]{1,0:T(8,128)(2,1)S(1)} %collective-permute-done.6.refs_10_), channel_id=1, source_target_pairs={{0,4},{1,5},{2,6},{3,7},{4,8},{5,9},{6,10},{7,11},{8,12},{9,13},{1... | collective-permute-start | bytes 860168 | tf_op jit(solution)/shard_map/ppermute | solution.py:30
  82.4 9.7 %collective-permute-start.18 = (bf16[224,640]{1,0:T(8,128)(2,1)S(1)}, bf16[224,640]{1,0:T(8,128)(2,1)S(1)}, u32[]{:S(2)}, u32[]{:S(2)}) collective-permute-start(bf16[224,640]{1,0:T(8,128)(2,1)S(1)} %collective-permute-done.17.refs_21_), channel_id=1, source_target_pairs={{4,8},{5,9},{6,10},{7,11},{8,12},{9,13},{10,14},{11,15},{12,28},{1... | collective-permute-start | bytes 860168 | tf_op jit(solution)/shard_map/ppermute | solution.py:30
  87.2 11.9 %collective-permute-start.21 = (bf16[224,640]{1,0:T(8,128)(2,1)}, bf16[224,640]{1,0:T(8,128)(2,1)S(1)}, u32[]{:S(2)}, u32[]{:S(2)}) collective-permute-start(bf16[224,640]{1,0:T(8,128)(2,1)} %collective-permute-done.20.refs_24_), channel_id=1, source_target_pairs={{0,16},{1,17},{2,18},{3,19},{4,0},{5,1},{6,2},{7,3},{8,4},{9,5},{1... | collective-permute-start | bytes 860168 | tf_op jit(solution)/shard_map/ppermute | solution.py:30
  89.4 13.6 %collective-permute-start.11 = (bf16[224,640]{1,0:T(8,128)(2,1)S(1)}, bf16[224,640]{1,0:T(8,128)(2,1)S(1)}, u32[]{:S(2)}, u32[]{:S(2)}) collective-permute-start(bf16[224,640]{1,0:T(8,128)(2,1)S(1)} %collective-permute-done.10.refs_14_), channel_id=1, source_target_pairs={{0,16},{1,17},{2,18},{3,19},{4,0},{5,1},{6,2},{7,3},{8,4},{9,5},{1... | collective-permute-start | bytes 860168 | tf_op jit(solution)/shard_map/ppermute | solution.py:30
  92.1 12.3 %collective-permute-start.8 = (bf16[224,640]{1,0:T(8,128)(2,1)S(1)}, bf16[224,640]{1,0:T(8,128)(2,1)S(1)}, u32[]{:S(2)}, u32[]{:S(2)}) collective-permute-start(bf16[224,640]{1,0:T(8,128)(2,1)S(1)} %collective-permute-done.7.refs_11_), channel_id=1, source_target_pairs={{4,8},{5,9},{6,10},{7,11},{8,12},{9,13},{10,14},{11,15},{12,28},{1... | collective-permute-start | bytes 860168 | tf_op jit(solution)/shard_map/ppermute | solution.py:30
  99.0 8.4 %collective-permute-start.22 = (bf16[224,640]{1,0:T(8,128)(2,1)S(1)}, bf16[224,640]{1,0:T(8,128)(2,1)S(1)}, u32[]{:S(2)}, u32[]{:S(2)}) collective-permute-start(bf16[224,640]{1,0:T(8,128)(2,1)S(1)} %broadcast_select_fusion.1), channel_id=1, source_target_pairs={{4,20},{5,21},{6,22},{7,23},{8,24},{9,25},{10,26},{11,27},{24,8},{... | collective-permute-start | bytes 860168 | tf_op jit(solution)/shard_map/ppermute | solution.py:30
  103.0 12.1 %collective-permute-start.12 = (bf16[224,640]{1,0:T(8,128)(2,1)}, bf16[224,640]{1,0:T(8,128)(2,1)}, u32[]{:S(2)}, u32[]{:S(2)}) collective-permute-start(bf16[224,640]{1,0:T(8,128)(2,1)} %broadcast_select_fusion.3), channel_id=1, source_target_pairs={{4,20},{5,21},{6,22},{7,23},{8,24},{9,25},{10,26},{11,27},{24,8},{... | collective-permute-start | bytes 860168 | tf_op jit(solution)/shard_map/ppermute | solution.py:30
  104.4 11.7 %collective-permute-start.23 = (bf16[224,640]{1,0:T(8,128)(2,1)}, bf16[224,640]{1,0:T(8,128)(2,1)}, u32[]{:S(2)}, u32[]{:S(2)}) collective-permute-start(bf16[224,640]{1,0:T(8,128)(2,1)} %broadcast_select_fusion), channel_id=1, source_target_pairs={{0,16},{1,17},{2,18},{3,19},{12,28},{13,29},{14,30},{15,31},{28,12... | collective-permute-start | bytes 860168 | tf_op jit(solution)/shard_map/ppermute | solution.py:30
  108.1 11.3 %collective-permute-start.13 = (bf16[224,640]{1,0:T(8,128)(2,1)}, bf16[224,640]{1,0:T(8,128)(2,1)}, u32[]{:S(2)}, u32[]{:S(2)}) collective-permute-start(bf16[224,640]{1,0:T(8,128)(2,1)} %broadcast_select_fusion.2), channel_id=1, source_target_pairs={{0,16},{1,17},{2,18},{3,19},{12,28},{13,29},{14,30},{15,31},{28,12... | collective-permute-start | bytes 860168 | tf_op jit(solution)/shard_map/ppermute | solution.py:30
  136.5 33.7 %all-to-all-start = ((bf16[16,64,640]{2,1,0:T(8,128)(2,1)}), bf16[16,64,640]{2,1,0:T(8,128)(2,1)S(1)}, u32[]{:S(2)}, u32[]{:S(2)}) async-start(bf16[16,64,640]{2,1,0:T(8,128)(2,1)} %bitcast.20), calls=%async_computation | async-start | bytes 2621440 | tf_op jit(solution)/shard_map/all_to_all | solution.py:276
  (22 other events, 221.7 us)

commit v3 on v2

--- a/solution.py
+++ b/solution.py
@@ -10,7 +10,7 @@
 F32 = jnp.float32
 BF16 = jnp.bfloat16
 BOTH = ("groups", "seq")
-BIG = 48 * 1024 * 1024
+BIG = 24 * 1024 * 1024
 VM = pl.BlockSpec(memory_space=pltpu.VMEM)
 SM = pl.BlockSpec(memory_space=pltpu.SMEM)
 ANY = pl.BlockSpec(memory_space=pl.ANY)
@@ -30,20 +30,22 @@
     return lax.ppermute(value, BOTH, pairs)
 
 
-def gather_cycle(block, p, devices):
-    fwd, bwd = [block], [block]
-    for k in (1, 2, 3):
-        up = [(a, (a + 1) % 8) for a in range(8)]
-        down = [(a, (a - 1) % 8) for a in range(8)]
-        if k == 3:
-            up = [(a, b) for a, b in up if (b - k) % 8 != 7 - b]
-            down = [(a, b) for a, b in down if (b + k) % 8 != 7 - b]
-        fwd.append(cycle(fwd[-1], up, devices))
-        bwd.append(cycle(bwd[-1], down, devices))
+def after(value, *others):
+    return lax.optimization_barrier((value,) + others)[0]
+
+
+def step(fwd, bwd, k, devices):
+    up = [(a, (a + 1) % 8) for a in range(8)]
+    down = [(a, (a - 1) % 8) for a in range(8)]
+    if k == 3:
+        up = [(a, b) for a, b in up if (b - k) % 8 != 7 - b]
+        down = [(a, b) for a, b in down if (b + k) % 8 != 7 - b]
+    return cycle(fwd, up, devices), cycle(bwd, down, devices)
+
+
+def swap(fwd, bwd, p, spots, devices):
     first = (p % 4 == 0) | (p % 4 == 1)
-    inner = cycle(jnp.where(first, bwd[1], fwd[1]), [(a, 7 - a) for a in (1, 2, 5, 6)], devices)
-    outer = cycle(jnp.where(first, bwd[3], fwd[3]), [(a, 7 - a) for a in (0, 3, 4, 7)], devices)
-    return fwd[1:] + bwd[1:] + [inner, outer]
+    return cycle(jnp.where(first, bwd, fwd), [(a, 7 - a) for a in spots], devices)
 
 
 def cut(place, a_ref, v_ref, keep, to_core, to_pair, to_both, sems):
@@ -65,65 +67,125 @@
         pltpu.make_async_copy(a_ref.at[:, near], out, sems.at[i]).wait()
 
 
-def one_hot_pack(lhs, w, base_col, base_row, source, out):
+def columns(line, width):
+    return pl.ds(pl.multiple_of(line * (width // 4), 128), width // 4)
+
+
+def line_of(q):
+    return jnp.where(q < 4, q, 7 - q)
+
+
+def load_rows(lhs, lines, buf, sem):
+    rows, width = lhs[0].shape
+    copies = []
+    for j, line in enumerate(lines):
+        for s, ref in enumerate(lhs):
+            to = buf.at[pl.ds(s * rows, rows), pl.ds(j * (width // 4), width // 4)]
+            copies.append(pltpu.make_async_copy(ref.at[:, columns(line, width)], to, sem.at[8 + j * len(lhs) + s]))
+    return copies
+
+
+def second_line(line):
+    return jnp.where((line == 0) | (line == 2), 1, 2)
+
+
+def last_lines(line):
+    return jnp.where(line == 0, 2, 0), jnp.where(line == 3, 1, 3)
+
+
+def near_half(*refs):
+    place = refs[0]
+    parts, lhs = refs[1:15], refs[15:-4]
+    out, buf, w, sems = refs[-4:]
+    deep = parts[0].shape[0]
+    p, x = place[0], place[1]
+    ends = p % 4
+    line = line_of(p)
+    second = second_line(line)
+    copies = load_rows(lhs, (line, second), buf, sems)
+    for c in copies:
+        c.start()
+
+    def move(ref, q, slot, which, i):
+        start = pl.multiple_of(((slot * 2 + which) * 2 + q // 4) * deep, 16)
+        return pltpu.make_async_copy(ref, w.at[pl.ds(start, deep)], sems.at[slot * 4 + i])
+
+    for chain in range(2):
+        own, pair, f1, b1, f2, b2, inner = parts[chain * 7 : chain * 7 + 7]
+        which = jnp.where(chain == 0, x, 1 - x)
+        move(own, p, 0, which, 2 * chain).start()
+        move(pair, 7 - p, 0, which, 2 * chain + 1).start()
+        for case, one, two in ((0, (b1, 1), (f2, 6)), (1, (b1, 1), (inner, 4)), (2, (f1, 7), (inner, 4)), (3, (f1, 7), (b2, 2))):
+
+            @pl.when(ends == case)
+            def _():
+                for i, (ref, step) in enumerate((one, two)):
+                    move(ref, (p + step) % 8, 1, which, 2 * chain + i).start()
+
+    acc = None
+    for slot in range(2):
+        for c in copies[slot * len(lhs) : (slot + 1) * len(lhs)]:
+            c.wait()
+        for i in range(4):
+            move(parts[0], p, slot, x, i).wait()
+        span = slice(slot * 4 * deep, (slot + 1) * 4 * deep)
+        part = jnp.dot(buf[:, span], w[span, :], preferred_element_type=F32)
+        acc = part if acc is None else acc + part
+    out[...] = acc
+
+
+def far_half(*refs):
+    place, source, base_col, base_row, acc_near, acc_far = refs[:6]
+    parts, lhs = refs[6:20], refs[20:24]
+    out, buf, w, sems = refs[24:]
+    deep = parts[0].shape[0]
     rows = lhs[0].shape[0]
     devices, sources, cap, half = out.shape
+    p, x = place[0], place[1]
+    ends = p % 4
+    line = line_of(p)
+    third, fourth = last_lines(line)
+    copies = load_rows(lhs, (third, fourth), buf, sems)
+    for c in copies:
+        c.start()
+
+    def move(ref, q, which, i):
+        slot = jnp.where(line_of(q) == third, 0, 1)
+        start = pl.multiple_of(((slot * 2 + which) * 2 + q // 4) * deep, 16)
+        return pltpu.make_async_copy(ref, w.at[pl.ds(start, deep)], sems.at[i])
+
+    for chain in range(2):
+        f1, f2, f3, b1, b2, b3, outer = parts[chain * 7 : chain * 7 + 7]
+        which = jnp.where(chain == 0, x, 1 - x)
+        f1, f2, f3, b1, b2, b3 = (f1, 7), (f2, 6), (f3, 5), (b1, 1), (b2, 2), (b3, 3)
+        outer = (outer, 4)
+        for case, takes in enumerate(((b2, f3, b3, outer), (f1, f2, b2, b3), (f2, f3, b1, b2), (f2, f3, b3, outer))):
+
+            @pl.when(ends == case)
+            def _():
+                for i, (ref, step) in enumerate(takes):
+                    move(ref, (p + step) % 8, which, 4 * chain + i).start()
+
     first = lax.broadcasted_iota(jnp.int32, (rows, rows), 0)
-    second = lax.broadcasted_iota(jnp.int32, (rows, rows), 1)
+    later = lax.broadcasted_iota(jnp.int32, (rows, rows), 1)
     slots = lax.broadcasted_iota(jnp.int32, (devices * cap, rows), 0)
+    picks = []
     for s in range(4):
         col = base_col[s * rows : (s + 1) * rows, :]
         row = base_row[:, s * rows : (s + 1) * rows]
-        same = jnp.logical_and(col == row, first < second)
+        same = jnp.logical_and(col == row, first < later)
         count = jnp.sum(same.astype(F32), axis=0, keepdims=True).astype(jnp.int32)
-        pick = (slots == row + count).astype(F32).astype(BF16)
-        up = jnp.dot(lhs[s][...], w[...], preferred_element_type=F32).astype(BF16)
-        packed = jnp.dot(pick, up, preferred_element_type=F32).astype(BF16)
+        picks.append((slots == row + count).astype(F32).astype(BF16))
+    for c in copies:
+        c.wait()
+    for i in range(8):
+        move(parts[0], p, x, i).wait()
+    for s in range(4):
+        acc = acc_near if s % 2 == 0 else acc_far
+        at = slice((s // 2) * rows, (s // 2 + 1) * rows)
+        up = acc[at, :] + jnp.dot(buf[s * rows : (s + 1) * rows, :], w[...], preferred_element_type=F32)
+        packed = jnp.dot(picks[s], up.astype(BF16), preferred_element_type=F32).astype(BF16)
         out[:, source[s]] = packed.reshape(devices, cap, half)
-
-
-def product_cycle(*refs):
-    place, source, base_col, base_row = refs[:4]
-    lhs, parts = refs[4:8], refs[8:28]
-    out, w, sems = refs[28:]
-    deep = parts[0].shape[0]
-    p, x = place[0], place[1]
-
-    def spread(op):
-        for chain in range(2):
-            own, pair, f1, f2, f3, b1, b2, b3, inner, outer = parts[chain * 10 : chain * 10 + 10]
-            which = jnp.where(chain == 0, x, 1 - x)
-
-            def move(ref, q, i):
-                group = q // 4
-                line = jnp.where(group == 0, q, 7 - q)
-                start = pl.multiple_of(((line * 2 + which) * 2 + group) * deep, 16)
-                op(pltpu.make_async_copy(ref, w.at[pl.ds(start, deep)], sems.at[chain * 8 + i]))
-
-            move(own, p, 0)
-            move(pair, 7 - p, 1)
-            far = (p + 4) % 8
-            ends = p % 4
-            for i, (ref, step) in enumerate(((f1, 7), (f2, 6), (f3, 5), (b1, 1), (b2, 2), (b3, 3))):
-                q = (p + step) % 8
-
-                @pl.when(q != 7 - p)
-                def _():
-                    move(ref, q, 2 + i if i < 5 else 7)
-
-            spare = jnp.where(ends == 0, 2, jnp.where(ends == 1, 4, jnp.where(ends == 2, 7, 5)))
-
-            @pl.when((ends == 0) | (ends == 3))
-            def _():
-                move(outer, far, spare)
-
-            @pl.when((ends == 1) | (ends == 2))
-            def _():
-                move(inner, far, spare)
-
-    spread(lambda c: c.start())
-    spread(lambda c: c.wait())
-    one_hot_pack(lhs, w, base_col, base_row, source, out)
 
 
 def product_plain(base_col, base_row, l0, l1, l2, l3, w, out):
@@ -232,7 +294,7 @@
     from_pair = flip(to_pair, 2, devices)
     from_both = flip(to_both, 3, devices)
 
-    r_pair = flip(grad_rows, 2, devices)
+    r_pair = flip(after(grad_rows, from_pair, from_both), 2, devices)
     r_core = flip(grad_rows, 1, devices)
     r_both = flip(r_pair, 1, devices)
     ids = route_ids[:, 0]
@@ -249,17 +311,41 @@
         straight = core == group
         block1 = jnp.where(straight, keep, from_core)
         mirror1 = jnp.where(straight, from_core, keep)
+        f1, b1 = step(block1, block1, 1, devices)
+        from_pair, from_both = after((from_pair, from_both), f1)
         block2 = jnp.where(straight, from_pair, from_both)
         mirror2 = jnp.where(straight, from_both, from_pair)
-        parts1 = [block1, mirror1] + gather_cycle(block1, p, devices)
-        parts2 = [block2, mirror2] + gather_cycle(block2, p, devices)
+        chains = []
+        for block, mirror, got in ((block1, mirror1, (f1, b1)), (block2, mirror2, None)):
+            f1, b1 = got or step(block, block, 1, devices)
+            f2, b2 = step(f1, b1, 2, devices)
+            inner = swap(f1, b1, p, (1, 2, 5, 6), devices)
+            f3, b3 = step(f2, b2, 3, devices)
+            outer = swap(f3, b3, p, (0, 3, 4, 7), devices)
+            chains.append((block, mirror, f1, b1, f2, b2, f3, b3, inner, outer))
+        early = [v for c in chains for v in (c[0], c[1], c[2], c[3], c[4], c[5], c[8])]
+        late = [v for c in chains for v in (c[2], c[4], c[6], c[3], c[5], c[7], c[9])]
+        spots = jnp.stack([p, pair])
+        acc = jax.ShapeDtypeStruct((2 * rows, half), F32)
+
+        def scratch(n):
+            return [
+                pltpu.VMEM((n * rows, width // 2), BF16),
+                pltpu.VMEM((width // 2, half), BF16),
+                pltpu.SemaphoreType.DMA((16,)),
+            ]
+
+        near = [
+            call(near_half, acc, [SM] + [ANY] * 16, scratch(2))(spots, *early, *pair_of)
+            for pair_of in ((lhs[0], lhs[2]), (lhs[1], lhs[3]))
+        ]
         base = jnp.where(named, all_ids % devices * cap, -(2 * rows))
         packed = call(
-            product_cycle,
+            far_half,
             jax.ShapeDtypeStruct((devices, 4, cap, half), BF16),
-            [SM, SM] + [VM] * 6 + [ANY] * 20,
-            [pltpu.VMEM((width, half), BF16), pltpu.SemaphoreType.DMA((16,))],
-        )(jnp.stack([p, pair]), source, base[:, None], base[None, :], *lhs, *parts1, *parts2)
+            [SM, SM] + [VM] * 4 + [ANY] * 18,
+            scratch(4),
+        )(spots, source, base[:, None], base[None, :], *near, *late, *lhs)
         packed = packed.reshape(devices, 4 * cap, half)
     else:
         straight = jnp.stack([keep, from_pair, from_core, from_both])

time: 191 us -> 181 us (0.948)
  waiting for transfers between devices: 114 us -> 91 us
  starting transfers between devices: 45.4 us -> 49.5 us
  other arithmetic: 5.72 us -> 9.63 us
  Pallas kernels: 16.4 us -> 19.1 us
  local copies, waits for them, and re-layouts: 7.75 us -> 9.9 us
    ppermute x16, waiting for transfers between devices: 31.3 us -> 16.1 us  [cycle(): return lax.ppermute(value, BOTH, pairs)]
    ppermute x14, waiting for transfers between devices: 55.2 us -> 47.5 us  [flip(): return lax.ppermute(value, 'seq', [(i, i ^ bits) for i in range(devices)])]
    ppermute x16, starting transfers between devices: 24 us -> 28.2 us  [cycle(): return lax.ppermute(value, BOTH, pairs)]
    pallas_call x1 -> x3, Pallas kernels: 13.2 us -> 16 us  [the longest x2 8.26 us: on_device(): call(near_half, acc, [SM] + [ANY] * 16, scratch(2))(spots, *early, *pair_of)]
    unnamed x30 -> x64, local copies, waits for them, and re-layouts: 6.72 us -> 8.18 us
  transfers between devices with their start and end apart: 31 -> 31, of which waited for: 19 -> 17; matrix products, arithmetic and copies ran while one was open for 3% -> 6% of each run, Pallas kernels for 0% -> 5%
where the time goes in v3:
time: 181 us; the launch traced here: 180 us
  waiting for transfers between devices  91 us (50%)
  starting transfers between devices  49.5 us (27%)
  Pallas kernels  19.1 us (11%)
  local copies, waits for them, and re-layouts  9.9 us (5%)
  other arithmetic  9.63 us (5%)
    ppermute x14, waiting for transfers between devices, flip(): return lax.ppermute(value, 'seq', [(i, i ^ bits) for i in range(devices)])  47.5 us
    ppermute x16, starting transfers between devices, cycle(): return lax.ppermute(value, BOTH, pairs)  28.2 us
    all_to_all x1, waiting for transfers between devices, on_device(): arrived = lax.all_to_all(packed, 'seq', 0, 0, tiled=True)  27.4 us
    ppermute x16, waiting for transfers between devices, cycle(): return lax.ppermute(value, BOTH, pairs)  16.1 us
    ppermute x14, starting transfers between devices, flip(): return lax.ppermute(value, 'seq', [(i, i ^ bits) for i in range(devices)])  15.1 us
    pallas_call x2, Pallas kernels, on_device(): call(near_half, acc, [SM] + [ANY] * 16, scratch(2))(spots, *early, *pair_of)  8.26 us
    unnamed x64, local copies, waits for them, and re-layouts  8.18 us
    pallas_call x1, Pallas kernels, on_device(): call(far_half, jax.ShapeDtypeStruct((devices, 4, cap, half), BF16), [SM,...  7.69 us
  transfers between devices with their start and end apart: 31, of which 17 were waited for; matrix products, arithmetic and copies ran while one was open for 6% of the time, Pallas kernels for 5%

profile of v3, /device:TPU:0, one launch (start us, length us, event | category | flops | bytes accessed | tf_op | source)
XLA Modules:
  0.0 180.3 jit_solution(16408946457548982139)
XLA Ops:
  3.7 3.0 %collective-permute-start.8 = (bf16[224,640]{1,0:T(8,128)(2,1)S(1)}, bf16[224,640]{1,0:T(8,128)(2,1)S(1)}, u32[]{:S(2)}, u32[]{:S(2)}) collective-permute-start(bf16[224,640]{1,0:T(8,128)(2,1)S(1)} %get-tuple-element.15), channel_id=1, source_target_pairs={{0,2},{1,3},{2,0},{3,1},{4,6},{5,7},{6,4},{7,5},{8,10},{9,11},{10,... | collective-permute-start | bytes 860168 | tf_op jit(solution)/shard_map/ppermute | solution.py:20
  6.7 7.7 %collective-permute-done.8 = bf16[224,640]{1,0:T(8,128)(2,1)S(1)} collective-permute-done((bf16[224,640]{1,0:T(8,128)(2,1)S(1)}, bf16[224,640]{1,0:T(8,128)(2,1)S(1)}, u32[]{:S(2)}, u32[]{:S(2)}) %collective-permute-start.8) | collective-permute-done | bytes 286752 | tf_op jit(solution)/shard_map/ppermute | solution.py:20
  14.4 4.6 %collective-permute-done.9 = bf16[224,640]{1,0:T(8,128)(2,1)S(1)} collective-permute-done((bf16[224,640]{1,0:T(8,128)(2,1)S(1)}, bf16[224,640]{1,0:T(8,128)(2,1)S(1)}, u32[]{:S(2)}, u32[]{:S(2)}) %collective-permute-start.9) | collective-permute-done | bytes 286752 | tf_op jit(solution)/shard_map/ppermute | solution.py:20
  26.0 7.1 %collective-permute-done.3.refs_3_.refs_6_ = bf16[224,640]{1,0:T(8,128)(2,1)S(1)} collective-permute-done((bf16[224,640]{1,0:T(8,128)(2,1)S(1)}, bf16[224,640]{1,0:T(8,128)(2,1)S(1)}, u32[]{:S(2)}, u32[]{:S(2)}) %collective-permute-start.3) | collective-permute-done | bytes 286752 | tf_op jit(solution)/shard_map/ppermute | solution.py:30
  36.3 25.5 %collective-permute-done = s32[256]{0:T(256)S(1)} collective-permute-done((s32[256]{0:T(256)S(1)}, s32[256]{0:T(256)S(1)}, u32[]{:S(2)}, u32[]{:S(2)}) %collective-permute-start) | collective-permute-done | bytes 1056 | tf_op jit(solution)/shard_map/ppermute | solution.py:20
  63.5 1.8 %collective-permute-start.5 = (bf16[224,640]{1,0:T(8,128)(2,1)S(1)}, bf16[224,640]{1,0:T(8,128)(2,1)}, u32[]{:S(2)}, u32[]{:S(2)}) collective-permute-start(bf16[224,640]{1,0:T(8,128)(2,1)S(1)} %collective-permute-done.3.refs_3_.refs_6_), channel_id=1, source_target_pairs={{0,4},{1,5},{2,6},{3,7},{4,8},{5,9},{6,10},{7,11},{8,12},{9,13},{1... | collective-permute-start | bytes 860168 | tf_op jit(solution)/shard_map/ppermute | solution.py:30
  65.6 1.9 %collective-permute-start.12 = (bf16[224,640]{1,0:T(8,128)(2,1)S(1)}, bf16[224,640]{1,0:T(8,128)(2,1)S(1)}, u32[]{:S(2)}, u32[]{:S(2)}) collective-permute-start(bf16[224,640]{1,0:T(8,128)(2,1)S(1)} %collective-permute-done.10.refs_10_.refs_13_), channel_id=1, source_target_pairs={{0,4},{1,5},{2,6},{3,7},{4,8},{5,9},{6,10},{7,11},{8,12},{9,13},{1... | collective-permute-start | bytes 860168 | tf_op jit(solution)/shard_map/ppermute | solution.py:30
  68.7 4.5 %collective-permute-done.5.refs_5_.refs_7_ = bf16[224,640]{1,0:T(8,128)(2,1)} collective-permute-done((bf16[224,640]{1,0:T(8,128)(2,1)S(1)}, bf16[224,640]{1,0:T(8,128)(2,1)}, u32[]{:S(2)}, u32[]{:S(2)}) %collective-permute-start.5) | collective-permute-done | bytes 286752 | tf_op jit(solution)/shard_map/ppermute | solution.py:30
  73.3 1.8 collective-permute-start.13
  79.1 3.8 %collective-permute-start.19 = (bf16[224,640]{1,0:T(8,128)(2,1)}, bf16[224,640]{1,0:T(8,128)(2,1)S(1)}, u32[]{:S(2)}, u32[]{:S(2)}) collective-permute-start(bf16[224,640]{1,0:T(8,128)(2,1)} %collective-permute-done.6.refs_6_.refs_10_), channel_id=1, source_target_pairs={{0,16},{1,17},{2,18},{3,19},{4,0},{5,1},{6,2},{7,3},{8,4},{9,5},{1... | collective-permute-start | bytes 860168 | tf_op jit(solution)/shard_map/ppermute | solution.py:30
  84.7 4.1 %collective-permute-start.22 = (bf16[224,640]{1,0:T(8,128)(2,1)S(1)}, bf16[224,640]{1,0:T(8,128)(2,1)S(1)}, u32[]{:S(2)}, u32[]{:S(2)}) collective-permute-start(bf16[224,640]{1,0:T(8,128)(2,1)S(1)} %collective-permute-done.13.refs_13_.refs_17_), channel_id=1, source_target_pairs={{0,16},{1,17},{2,18},{3,19},{4,0},{5,1},{6,2},{7,3},{8,4},{9,5},{1... | collective-permute-start | bytes 860168 | tf_op jit(solution)/shard_map/ppermute | solution.py:30
  95.0 3.6 %collective-permute-start.20 = (bf16[224,640]{1,0:T(8,128)(2,1)}, bf16[224,640]{1,0:T(8,128)(2,1)}, u32[]{:S(2)}, u32[]{:S(2)}) collective-permute-start(bf16[224,640]{1,0:T(8,128)(2,1)} %broadcast_select_fusion.1), channel_id=1, source_target_pairs={{0,16},{1,17},{2,18},{3,19},{12,28},{13,29},{14,30},{15,31},{28,12... | collective-permute-start | bytes 860168 | tf_op jit(solution)/shard_map/ppermute | solution.py:30
  100.1 2.2 %collective-permute-start.23 = (bf16[224,640]{1,0:T(8,128)(2,1)}, bf16[224,640]{1,0:T(8,128)(2,1)}, u32[]{:S(2)}, u32[]{:S(2)}) collective-permute-start(bf16[224,640]{1,0:T(8,128)(2,1)} %broadcast_select_fusion), channel_id=1, source_target_pairs={{0,16},{1,17},{2,18},{3,19},{12,28},{13,29},{14,30},{15,31},{28,12... | collective-permute-start | bytes 860168 | tf_op jit(solution)/shard_map/ppermute | solution.py:30
  103.0 1.7 copy.15
  110.7 4.0 %shard_map.104.refs_4_ = f32[512,640]{1,0:T(8,128)S(1)} custom-call(s32[2]{0:T(128)S(1)} %copy-done.21, bf16[224,640]{1,0:T(8,128)(2,1)S(1)} %get-tuple-element.26.refs_1_, bf16[224,640]{1,0:T(8,128)(2,1)S(1)} %get-tuple-element.25.refs_2_, bf16[224,640]{1,0:T(8,128)(2,1)S(1)} %collective-permute-done.3.refs_3_.refs_6_, ...), custom_call_target="tpu_custom_call" | custom-call | tf_op jit(solution)/shard_map/pallas_call | solution.py:339
  114.8 4.3 %shard_map.105.refs_5_ = f32[512,640]{1,0:T(8,128)S(1)} custom-call(s32[2]{0:T(128)S(1)} %copy-done.21, bf16[224,640]{1,0:T(8,128)(2,1)S(1)} %get-tuple-element.26.refs_1_, bf16[224,640]{1,0:T(8,128)(2,1)S(1)} %get-tuple-element.25.refs_2_, bf16[224,640]{1,0:T(8,128)(2,1)S(1)} %collective-permute-done.3.refs_3_.refs_6_, ...), custom_call_target="tpu_custom_call" | custom-call | tf_op jit(solution)/shard_map/pallas_call | solution.py:339
  119.1 7.7 %shard_map.106 = bf16[16,4,16,640]{3,2,1,0:T(8,128)(2,1)} custom-call(s32[2]{0:T(128)S(1)} %copy-done.21, s32[4]{0:T(128)S(1)} %copy-done.22, s32[1024,1]{1,0:T(8,128)S(1)} %fusion.2.refs_2_, s32[1,1024]{1,0:T(1,128)S(1)} %copy-done.20, f32[512,640]{1,0:T(8,128)S(1)} %shard_map.104.refs_4_, f32[512,640]{1,0:T(8,128)S(1)} %shard_map.105.refs_5_, ...), custom_call_target="tpu_custom_call" | custom-call | tf_op jit(solution)/shard_map/pallas_call | solution.py:343
  126.9 6.2 %all-to-all-start = ((bf16[16,64,640]{2,1,0:T(8,128)(2,1)}), bf16[16,64,640]{2,1,0:T(8,128)(2,1)S(1)}, u32[]{:S(2)}, u32[]{:S(2)}) async-start(bf16[16,64,640]{2,1,0:T(8,128)(2,1)} %bitcast.15), calls=%async_computation | async-start | bytes 2621440 | tf_op jit(solution)/shard_map/all_to_all | solution.py:362
  133.1 27.4 %all-to-all-done = bf16[16,64,640]{2,1,0:T(8,128)(2,1)S(1)} async-done(((bf16[16,64,640]{2,1,0:T(8,128)(2,1)}), bf16[16,64,640]{2,1,0:T(8,128)(2,1)S(1)}, u32[]{:S(2)}, u32[]{:S(2)}) %all-to-all-start) | async-done | bytes 1310752 | tf_op jit(solution)/shard_map/all_to_all | solution.py:362
  160.5 2.5 %shard_map.107 = (bf16[256,1280]{1,0:T(8,128)(2,1)}, bf16[256,1280]{1,0:T(8,128)(2,1)}, f32[2,1280]{1,0:T(2,128)S(1)}) custom-call(bf16[4,2,2,4,16,640]{5,4,3,2,1,0:T(8,128)(2,1)S(1)} %bitcast.17, bf16[256,1280]{1,0:T(8,128)(2,1)S(1)} %copy-done.16, bf16[256,1280]{1,0:T(8,128)(2,1)S(1)} %copy-done.17, f32[1,1280]{1,0:T(1,128)S(1)} %broadcast_in_dim.16.a_gain, ...), custom_call_target="tpu_custom_call" | custom-call | tf_op jit(solution)/shard_map/pallas_call | solution.py:367
  163.7 2.3 %collective-permute-start.25 = (f32[2,1280]{1,0:T(2,128)S(1)}, f32[2,1280]{1,0:T(2,128)S(1)}, u32[]{:S(2)}, u32[]{:S(2)}) collective-permute-start(f32[2,1280]{1,0:T(2,128)S(1)} %get-tuple-element.22), channel_id=1, source_target_pairs={{0,2},{1,3},{2,0},{3,1},{4,6},{5,7},{6,4},{7,5},{8,10},{9,11},{10,... | collective-permute-start | bytes 30728 | tf_op jit(solution)/shard_map/ppermute | solution.py:20
  169.2 3.7 %collective-permute-start.27 = (f32[2,1280]{1,0:T(2,128)S(1)}, f32[2,1280]{1,0:T(2,128)S(1)}, u32[]{:S(2)}, u32[]{:S(2)}) collective-permute-start(f32[2,1280]{1,0:T(2,128)S(1)} %add_add_fusion.1), channel_id=1, source_target_pairs={{0,4},{1,5},{2,6},{3,7},{4,0},{5,1},{6,2},{7,3},{8,12},{9,13},{10,... | collective-permute-start | bytes 30728 | tf_op jit(solution)/shard_map/ppermute | solution.py:20
  175.3 2.1 %collective-permute-done.28 = f32[2,1280]{1,0:T(2,128)S(1)} collective-permute-done((f32[2,1280]{1,0:T(2,128)S(1)}, f32[2,1280]{1,0:T(2,128)S(1)}, u32[]{:S(2)}, u32[]{:S(2)}) %collective-permute-start.28) | collective-permute-done | bytes 10272 | tf_op jit(solution)/shard_map/ppermute | solution.py:20
  177.4 2.3 %collective-permute-done.29 = f32[2,1280]{1,0:T(2,128)S(1)} collective-permute-done((f32[2,1280]{1,0:T(2,128)S(1)}, f32[2,1280]{1,0:T(2,128)S(1)}, u32[]{:S(2)}, u32[]{:S(2)}) %collective-permute-start.29) | collective-permute-done | bytes 10272 | tf_op jit(solution)/shard_map/ppermute | solution.py:20
  (125 shorter events, 43.6 us)
Async XLA Ops:
  3.7 10.7 %collective-permute-start.8 = (bf16[224,640]{1,0:T(8,128)(2,1)S(1)}, bf16[224,640]{1,0:T(8,128)(2,1)S(1)}, u32[]{:S(2)}, u32[]{:S(2)}) collective-permute-start(bf16[224,640]{1,0:T(8,128)(2,1)S(1)} %get-tuple-element.15), channel_id=1, source_target_pairs={{0,2},{1,3},{2,0},{3,1},{4,6},{5,7},{6,4},{7,5},{8,10},{9,11},{10,... | collective-permute-start | bytes 860168 | tf_op jit(solution)/shard_map/ppermute | solution.py:20
  6.7 12.2 %collective-permute-start.9 = (bf16[224,640]{1,0:T(8,128)(2,1)S(1)}, bf16[224,640]{1,0:T(8,128)(2,1)S(1)}, u32[]{:S(2)}, u32[]{:S(2)}) collective-permute-start(bf16[224,640]{1,0:T(8,128)(2,1)S(1)} %get-tuple-element.16), channel_id=1, source_target_pairs={{0,3},{1,2},{2,1},{3,0},{4,7},{5,6},{6,5},{7,4},{8,11},{9,10},{10,... | collective-permute-start | bytes 860168 | tf_op jit(solution)/shard_map/ppermute | solution.py:20
  18.9 44.2 %collective-permute-start.16 = (bf16[256,3584]{1,0:T(8,128)(2,1)}, bf16[256,3584]{1,0:T(8,128)(2,1)}, u32[]{:S(2)}, u32[]{:S(2)}) collective-permute-start(bf16[256,3584]{1,0:T(8,128)(2,1)} %refs_20_.1), channel_id=1, source_target_pairs={{0,2},{1,3},{2,0},{3,1},{4,6},{5,7},{6,4},{7,5},{8,10},{9,11},{10,... | collective-permute-start | bytes 5505032 | tf_op jit(solution)/shard_map/ppermute | solution.py:20
  23.9 9.2 %collective-permute-start.3 = (bf16[224,640]{1,0:T(8,128)(2,1)S(1)}, bf16[224,640]{1,0:T(8,128)(2,1)S(1)}, u32[]{:S(2)}, u32[]{:S(2)}) collective-permute-start(bf16[224,640]{1,0:T(8,128)(2,1)S(1)} %get-tuple-element.26.refs_1_), channel_id=1, source_target_pairs={{0,4},{1,5},{2,6},{3,7},{4,8},{5,9},{6,10},{7,11},{8,12},{9,13},{1... | collective-permute-start | bytes 860168 | tf_op jit(solution)/shard_map/ppermute | solution.py:30
  25.5 38.0 %collective-permute-start.4 = (bf16[224,640]{1,0:T(8,128)(2,1)S(1)}, bf16[224,640]{1,0:T(8,128)(2,1)S(1)}, u32[]{:S(2)}, u32[]{:S(2)}) collective-permute-start(bf16[224,640]{1,0:T(8,128)(2,1)S(1)} %get-tuple-element.26.refs_1_), channel_id=1, source_target_pairs={{0,16},{1,17},{2,18},{3,19},{4,0},{5,1},{6,2},{7,3},{8,4},{9,5},{1... | collective-permute-start | bytes 860168 | tf_op jit(solution)/shard_map/ppermute | solution.py:30
  33.9 31.4 %collective-permute-start.10 = (bf16[224,640]{1,0:T(8,128)(2,1)}, bf16[224,640]{1,0:T(8,128)(2,1)S(1)}, u32[]{:S(2)}, u32[]{:S(2)}) collective-permute-start(bf16[224,640]{1,0:T(8,128)(2,1)} %get-tuple-element.24.refs_8_), channel_id=1, source_target_pairs={{0,4},{1,5},{2,6},{3,7},{4,8},{5,9},{6,10},{7,11},{8,12},{9,13},{1... | collective-permute-start | bytes 860168 | tf_op jit(solution)/shard_map/ppermute | solution.py:30
  35.5 30.1 %collective-permute-start.11 = (bf16[224,640]{1,0:T(8,128)(2,1)}, bf16[224,640]{1,0:T(8,128)(2,1)S(1)}, u32[]{:S(2)}, u32[]{:S(2)}) collective-permute-start(bf16[224,640]{1,0:T(8,128)(2,1)} %get-tuple-element.24.refs_8_), channel_id=1, source_target_pairs={{0,16},{1,17},{2,18},{3,19},{4,0},{5,1},{6,2},{7,3},{8,4},{9,5},{1... | collective-permute-start | bytes 860168 | tf_op jit(solution)/shard_map/ppermute | solution.py:30
  36.0 25.8 %collective-permute-start = (s32[256]{0:T(256)S(1)}, s32[256]{0:T(256)S(1)}, u32[]{:S(2)}, u32[]{:S(2)}) collective-permute-start(s32[256]{0:T(256)S(1)} %bitcast.20), channel_id=1, source_target_pairs={{0,2},{1,3},{2,0},{3,1},{4,6},{5,7},{6,4},{7,5},{8,10},{9,11},{10,... | collective-permute-start | bytes 3080 | tf_op jit(solution)/shard_map/ppermute | solution.py:20
  63.0 43.2 %collective-permute-start.15 = (bf16[256,3584]{1,0:T(8,128)(2,1)S(1)}, bf16[256,3584]{1,0:T(8,128)(2,1)}, u32[]{:S(2)}, u32[]{:S(2)}) collective-permute-start(bf16[256,3584]{1,0:T(8,128)(2,1)S(1)} %copy-done), channel_id=1, source_target_pairs={{0,1},{1,0},{2,3},{3,2},{4,5},{5,4},{6,7},{7,6},{8,9},{9,8},{10,11... | collective-permute-start | bytes 5505032 | tf_op jit(solution)/shard_map/ppermute | solution.py:20
  63.2 51.6 %collective-permute-start.17 = (bf16[256,3584]{1,0:T(8,128)(2,1)}, bf16[256,3584]{1,0:T(8,128)(2,1)}, u32[]{:S(2)}, u32[]{:S(2)}) collective-permute-start(bf16[256,3584]{1,0:T(8,128)(2,1)} %collective-permute-done.16.refs_15_.refs_21_), channel_id=1, source_target_pairs={{0,1},{1,0},{2,3},{3,2},{4,5},{5,4},{6,7},{7,6},{8,9},{9,8},{10,11... | collective-permute-start | bytes 5505032 | tf_op jit(solution)/shard_map/ppermute | solution.py:20
  63.5 9.8 %collective-permute-start.5 = (bf16[224,640]{1,0:T(8,128)(2,1)S(1)}, bf16[224,640]{1,0:T(8,128)(2,1)}, u32[]{:S(2)}, u32[]{:S(2)}) collective-permute-start(bf16[224,640]{1,0:T(8,128)(2,1)S(1)} %collective-permute-done.3.refs_3_.refs_6_), channel_id=1, source_target_pairs={{0,4},{1,5},{2,6},{3,7},{4,8},{5,9},{6,10},{7,11},{8,12},{9,13},{1... | collective-permute-start | bytes 860168 | tf_op jit(solution)/shard_map/ppermute | solution.py:30
  65.3 9.7 %collective-permute-start.6 = (bf16[224,640]{1,0:T(8,128)(2,1)S(1)}, bf16[224,640]{1,0:T(8,128)(2,1)}, u32[]{:S(2)}, u32[]{:S(2)}) collective-permute-start(bf16[224,640]{1,0:T(8,128)(2,1)S(1)} %collective-permute-done.4.refs_4_.refs_9_), channel_id=1, source_target_pairs={{0,16},{1,17},{2,18},{3,19},{4,0},{5,1},{6,2},{7,3},{8,4},{9,5},{1... | collective-permute-start | bytes 860168 | tf_op jit(solution)/shard_map/ppermute | solution.py:30
  65.6 13.5 %collective-permute-start.12 = (bf16[224,640]{1,0:T(8,128)(2,1)S(1)}, bf16[224,640]{1,0:T(8,128)(2,1)S(1)}, u32[]{:S(2)}, u32[]{:S(2)}) collective-permute-start(bf16[224,640]{1,0:T(8,128)(2,1)S(1)} %collective-permute-done.10.refs_10_.refs_13_), channel_id=1, source_target_pairs={{0,4},{1,5},{2,6},{3,7},{4,8},{5,9},{6,10},{7,11},{8,12},{9,13},{1... | collective-permute-start | bytes 860168 | tf_op jit(solution)/shard_map/ppermute | solution.py:30
  73.3 9.6 %collective-permute-start.13 = (bf16[224,640]{1,0:T(8,128)(2,1)S(1)}, bf16[224,640]{1,0:T(8,128)(2,1)S(1)}, u32[]{:S(2)}, u32[]{:S(2)}) collective-permute-start(bf16[224,640]{1,0:T(8,128)(2,1)S(1)} %collective-permute-done.11.refs_11_.refs_16_), channel_id=1, source_target_pairs={{0,16},{1,17},{2,18},{3,19},{4,0},{5,1},{6,2},{7,3},{8,4},{9,5},{1... | collective-permute-start | bytes 860168 | tf_op jit(solution)/shard_map/ppermute | solution.py:30
  75.0 9.7 %collective-permute-start.18 = (bf16[224,640]{1,0:T(8,128)(2,1)}, bf16[224,640]{1,0:T(8,128)(2,1)S(1)}, u32[]{:S(2)}, u32[]{:S(2)}) collective-permute-start(bf16[224,640]{1,0:T(8,128)(2,1)} %collective-permute-done.5.refs_5_.refs_7_), channel_id=1, source_target_pairs={{4,8},{5,9},{6,10},{7,11},{8,12},{9,13},{10,14},{11,15},{12,28},{1... | collective-permute-start | bytes 860168 | tf_op jit(solution)/shard_map/ppermute | solution.py:30
  79.1 10.6 %collective-permute-start.19 = (bf16[224,640]{1,0:T(8,128)(2,1)}, bf16[224,640]{1,0:T(8,128)(2,1)S(1)}, u32[]{:S(2)}, u32[]{:S(2)}) collective-permute-start(bf16[224,640]{1,0:T(8,128)(2,1)} %collective-permute-done.6.refs_6_.refs_10_), channel_id=1, source_target_pairs={{0,16},{1,17},{2,18},{3,19},{4,0},{5,1},{6,2},{7,3},{8,4},{9,5},{1... | collective-permute-start | bytes 860168 | tf_op jit(solution)/shard_map/ppermute | solution.py:30
  82.9 9.1 %collective-permute-start.21 = (bf16[224,640]{1,0:T(8,128)(2,1)S(1)}, bf16[224,640]{1,0:T(8,128)(2,1)S(1)}, u32[]{:S(2)}, u32[]{:S(2)}) collective-permute-start(bf16[224,640]{1,0:T(8,128)(2,1)S(1)} %collective-permute-done.12.refs_12_.refs_14_), channel_id=1, source_target_pairs={{4,8},{5,9},{6,10},{7,11},{8,12},{9,13},{10,14},{11,15},{12,28},{1... | collective-permute-start | bytes 860168 | tf_op jit(solution)/shard_map/ppermute | solution.py:30
  84.7 10.2 %collective-permute-start.22 = (bf16[224,640]{1,0:T(8,128)(2,1)S(1)}, bf16[224,640]{1,0:T(8,128)(2,1)S(1)}, u32[]{:S(2)}, u32[]{:S(2)}) collective-permute-start(bf16[224,640]{1,0:T(8,128)(2,1)S(1)} %collective-permute-done.13.refs_13_.refs_17_), channel_id=1, source_target_pairs={{0,16},{1,17},{2,18},{3,19},{4,0},{5,1},{6,2},{7,3},{8,4},{9,5},{1... | collective-permute-start | bytes 860168 | tf_op jit(solution)/shard_map/ppermute | solution.py:30
  89.7 9.6 %collective-permute-start.7 = (bf16[224,640]{1,0:T(8,128)(2,1)S(1)}, bf16[224,640]{1,0:T(8,128)(2,1)S(1)}, u32[]{:S(2)}, u32[]{:S(2)}) collective-permute-start(bf16[224,640]{1,0:T(8,128)(2,1)S(1)} %broadcast_select_fusion.3), channel_id=1, source_target_pairs={{4,20},{5,21},{6,22},{7,23},{8,24},{9,25},{10,26},{11,27},{24,8},{... | collective-permute-start | bytes 860168 | tf_op jit(solution)/shard_map/ppermute | solution.py:30
  92.0 14.2 %collective-permute-start.14 = (bf16[224,640]{1,0:T(8,128)(2,1)}, bf16[224,640]{1,0:T(8,128)(2,1)}, u32[]{:S(2)}, u32[]{:S(2)}) collective-permute-start(bf16[224,640]{1,0:T(8,128)(2,1)} %broadcast_select_fusion.2), channel_id=1, source_target_pairs={{4,20},{5,21},{6,22},{7,23},{8,24},{9,25},{10,26},{11,27},{24,8},{... | collective-permute-start | bytes 860168 | tf_op jit(solution)/shard_map/ppermute | solution.py:30
  95.0 24.1 %collective-permute-start.20 = (bf16[224,640]{1,0:T(8,128)(2,1)}, bf16[224,640]{1,0:T(8,128)(2,1)}, u32[]{:S(2)}, u32[]{:S(2)}) collective-permute-start(bf16[224,640]{1,0:T(8,128)(2,1)} %broadcast_select_fusion.1), channel_id=1, source_target_pairs={{0,16},{1,17},{2,18},{3,19},{12,28},{13,29},{14,30},{15,31},{28,12... | collective-permute-start | bytes 860168 | tf_op jit(solution)/shard_map/ppermute | solution.py:30
  100.1 19.0 %collective-permute-start.23 = (bf16[224,640]{1,0:T(8,128)(2,1)}, bf16[224,640]{1,0:T(8,128)(2,1)}, u32[]{:S(2)}, u32[]{:S(2)}) collective-permute-start(bf16[224,640]{1,0:T(8,128)(2,1)} %broadcast_select_fusion), channel_id=1, source_target_pairs={{0,16},{1,17},{2,18},{3,19},{12,28},{13,29},{14,30},{15,31},{28,12... | collective-permute-start | bytes 860168 | tf_op jit(solution)/shard_map/ppermute | solution.py:30
  126.9 33.6 %all-to-all-start = ((bf16[16,64,640]{2,1,0:T(8,128)(2,1)}), bf16[16,64,640]{2,1,0:T(8,128)(2,1)S(1)}, u32[]{:S(2)}, u32[]{:S(2)}) async-start(bf16[16,64,640]{2,1,0:T(8,128)(2,1)} %bitcast.15), calls=%async_computation | async-start | bytes 2621440 | tf_op jit(solution)/shard_map/all_to_all | solution.py:362
  169.2 6.1 %collective-permute-start.27 = (f32[2,1280]{1,0:T(2,128)S(1)}, f32[2,1280]{1,0:T(2,128)S(1)}, u32[]{:S(2)}, u32[]{:S(2)}) collective-permute-start(f32[2,1280]{1,0:T(2,128)S(1)} %add_add_fusion.1), channel_id=1, source_target_pairs={{0,4},{1,5},{2,6},{3,7},{4,0},{5,1},{6,2},{7,3},{8,12},{9,13},{10,... | collective-permute-start | bytes 30728 | tf_op jit(solution)/shard_map/ppermute | solution.py:20
  (39 other events, 374.6 us)

commit v4 on v3

--- a/solution.py
+++ b/solution.py
@@ -11,6 +11,7 @@
 BF16 = jnp.bfloat16
 BOTH = ("groups", "seq")
 BIG = 24 * 1024 * 1024
+WHOLE = 60 * 1024 * 1024
 VM = pl.BlockSpec(memory_space=pltpu.VMEM)
 SM = pl.BlockSpec(memory_space=pltpu.SMEM)
 ANY = pl.BlockSpec(memory_space=pl.ANY)
@@ -18,6 +19,11 @@
 
 def flip(value, bits, devices):
     return lax.ppermute(value, "seq", [(i, i ^ bits) for i in range(devices)])
+
+
+def cross(value, bits, devices):
+    pairs = [(g * devices + i, g * devices + (i ^ bits)) for g in range(2) for i in range(g, devices, 2)]
+    return lax.ppermute(value, BOTH, pairs)
 
 
 def spot(p, low, devices):
@@ -81,7 +87,7 @@
     for j, line in enumerate(lines):
         for s, ref in enumerate(lhs):
             to = buf.at[pl.ds(s * rows, rows), pl.ds(j * (width // 4), width // 4)]
-            copies.append(pltpu.make_async_copy(ref.at[:, columns(line, width)], to, sem.at[8 + j * len(lhs) + s]))
+            copies.append(pltpu.make_async_copy(ref.at[:, columns(line, width)], to, sem.at[16 + j * len(lhs) + s]))
     return copies
 
 
@@ -93,78 +99,50 @@
     return jnp.where(line == 0, 2, 0), jnp.where(line == 3, 1, 3)
 
 
-def near_half(*refs):
-    place = refs[0]
-    parts, lhs = refs[1:15], refs[15:-4]
-    out, buf, w, sems = refs[-4:]
-    deep = parts[0].shape[0]
-    p, x = place[0], place[1]
-    ends = p % 4
-    line = line_of(p)
-    second = second_line(line)
-    copies = load_rows(lhs, (line, second), buf, sems)
-    for c in copies:
-        c.start()
-
-    def move(ref, q, slot, which, i):
-        start = pl.multiple_of(((slot * 2 + which) * 2 + q // 4) * deep, 16)
-        return pltpu.make_async_copy(ref, w.at[pl.ds(start, deep)], sems.at[slot * 4 + i])
-
-    for chain in range(2):
-        own, pair, f1, b1, f2, b2, inner = parts[chain * 7 : chain * 7 + 7]
-        which = jnp.where(chain == 0, x, 1 - x)
-        move(own, p, 0, which, 2 * chain).start()
-        move(pair, 7 - p, 0, which, 2 * chain + 1).start()
-        for case, one, two in ((0, (b1, 1), (f2, 6)), (1, (b1, 1), (inner, 4)), (2, (f1, 7), (inner, 4)), (3, (f1, 7), (b2, 2))):
-
-            @pl.when(ends == case)
-            def _():
-                for i, (ref, step) in enumerate((one, two)):
-                    move(ref, (p + step) % 8, 1, which, 2 * chain + i).start()
-
-    acc = None
-    for slot in range(2):
-        for c in copies[slot * len(lhs) : (slot + 1) * len(lhs)]:
-            c.wait()
-        for i in range(4):
-            move(parts[0], p, slot, x, i).wait()
-        span = slice(slot * 4 * deep, (slot + 1) * 4 * deep)
-        part = jnp.dot(buf[:, span], w[span, :], preferred_element_type=F32)
-        acc = part if acc is None else acc + part
-    out[...] = acc
-
-
-def far_half(*refs):
-    place, source, base_col, base_row, acc_near, acc_far = refs[:6]
-    parts, lhs = refs[6:20], refs[20:24]
-    out, buf, w, sems = refs[24:]
+def product_cycle(*refs):
+    place, source, base_col, base_row = refs[:4]
+    parts, lhs = refs[4:24], refs[24:28]
+    out, buf, w, acc, sems = refs[28:]
     deep = parts[0].shape[0]
     rows = lhs[0].shape[0]
     devices, sources, cap, half = out.shape
     p, x = place[0], place[1]
     ends = p % 4
     line = line_of(p)
+    second = second_line(line)
     third, fourth = last_lines(line)
-    copies = load_rows(lhs, (third, fourth), buf, sems)
-    for c in copies:
-        c.start()
-
-    def move(ref, q, which, i):
-        slot = jnp.where(line_of(q) == third, 0, 1)
+    copies = load_rows(lhs, (line, second, third, fourth), buf, sems)
+
+    def move(ref, q, slot, which, i):
         start = pl.multiple_of(((slot * 2 + which) * 2 + q // 4) * deep, 16)
         return pltpu.make_async_copy(ref, w.at[pl.ds(start, deep)], sems.at[i])
 
-    for chain in range(2):
-        f1, f2, f3, b1, b2, b3, outer = parts[chain * 7 : chain * 7 + 7]
-        which = jnp.where(chain == 0, x, 1 - x)
-        f1, f2, f3, b1, b2, b3 = (f1, 7), (f2, 6), (f3, 5), (b1, 1), (b2, 2), (b3, 3)
-        outer = (outer, 4)
-        for case, takes in enumerate(((b2, f3, b3, outer), (f1, f2, b2, b3), (f2, f3, b1, b2), (f2, f3, b3, outer))):
-
-            @pl.when(ends == case)
-            def _():
-                for i, (ref, step) in enumerate(takes):
-                    move(ref, (p + step) % 8, which, 4 * chain + i).start()
+    for j in range(2):
+        for c in copies[8 * j : 8 * j + 8]:
+            c.start()
+        for chain in range(2):
+            own, mirror, f1, f2, f3, b1, b2, b3, inner, outer = parts[chain * 10 : chain * 10 + 10]
+            which = jnp.where(chain == 0, x, 1 - x)
+            f1, f2, f3, b1, b2, b3 = (f1, 7), (f2, 6), (f3, 5), (b1, 1), (b2, 2), (b3, 3)
+            inner, outer = (inner, 4), (outer, 4)
+            if j == 0:
+                move(own, p, 0, which, 4 * chain).start()
+            for case in range(4):
+
+                @pl.when(ends == case)
+                def _():
+                    if j == 0:
+                        ref = mirror if chain == 0 else (f1[0], mirror, mirror, b1[0])[case]
+                        move(ref, 7 - p, 0, which, 4 * chain + 1).start()
+                        takes = ((b1, f2), (b1, inner), (f1, inner), (f1, b2))[case]
+                        for i, (ref, step) in enumerate(takes):
+                            move(ref, (p + step) % 8, 1, which, 4 * chain + 2 + i).start()
+                    else:
+                        takes = ((b2, f3, b3, outer), (f1, f2, b2, b3), (f2, f3, b1, b2), (f2, f3, b3, outer))[case]
+                        for i, (ref, step) in enumerate(takes):
+                            q = (p + step) % 8
+                            slot = jnp.where(line_of(q) == third, 2, 3)
+                            move(ref, q, slot, which, 8 + 4 * chain + i).start()
 
     first = lax.broadcasted_iota(jnp.int32, (rows, rows), 0)
     later = lax.broadcasted_iota(jnp.int32, (rows, rows), 1)
@@ -176,14 +154,17 @@
         same = jnp.logical_and(col == row, first < later)
         count = jnp.sum(same.astype(F32), axis=0, keepdims=True).astype(jnp.int32)
         picks.append((slots == row + count).astype(F32).astype(BF16))
-    for c in copies:
-        c.wait()
-    for i in range(8):
-        move(parts[0], p, x, i).wait()
+    for j in range(2):
+        for c in copies[8 * j : 8 * j + 8]:
+            c.wait()
+        for i in range(8):
+            move(parts[0], p, 0, x, 8 * j + i).wait()
+        span = slice(j * 8 * deep, (j + 1) * 8 * deep)
+        if j == 0:
+            acc[...] = jnp.dot(buf[:, span], w[span, :], preferred_element_type=F32)
     for s in range(4):
-        acc = acc_near if s % 2 == 0 else acc_far
-        at = slice((s // 2) * rows, (s // 2 + 1) * rows)
-        up = acc[at, :] + jnp.dot(buf[s * rows : (s + 1) * rows, :], w[...], preferred_element_type=F32)
+        at = slice(s * rows, (s + 1) * rows)
+        up = acc[at, :] + jnp.dot(buf[at, span], w[span, :], preferred_element_type=F32)
         packed = jnp.dot(picks[s], up.astype(BF16), preferred_element_type=F32).astype(BF16)
         out[:, source[s]] = packed.reshape(devices, cap, half)
 
@@ -249,14 +230,14 @@
         v_out[:, cols(k)] = (scale * (p - n * (pn * inv))).astype(BF16)
 
 
-def call(body, outs, specs, scratch=(), out_spec=VM):
+def call(body, outs, specs, scratch=(), out_spec=VM, limit=BIG):
     return pl.pallas_call(
         body,
         out_shape=outs,
         in_specs=specs,
         out_specs=jax.tree.map(lambda _: out_spec, outs),
         scratch_shapes=list(scratch),
-        compiler_params=pltpu.CompilerParams(vmem_limit_bytes=BIG),
+        compiler_params=pltpu.CompilerParams(vmem_limit_bytes=limit),
     )
 
 
@@ -283,25 +264,36 @@
     block = jax.ShapeDtypeStruct((k, half), BF16)
     if lines == 4:
         keep, to_core, to_pair, to_both = call(
-            cut, (block,) * 4, [SM, ANY, ANY], [pltpu.SemaphoreType.DMA((4,))], ANY
+            cut, (block,) * 4, [SM, ANY, ANY], [pltpu.SemaphoreType.DMA((4,))], VM, WHOLE
         )(jnp.stack([pair, core]), audio_proj.T, vision_proj.T)
     else:
         both = jnp.stack([audio_proj.T, vision_proj.T]).reshape(2, k, 2, half)
         pick = lambda m, h: both[m, :, h]
         keep, to_core = pick(core, pair), pick(1 - core, pair)
         to_pair, to_both = pick(core, 1 - pair), pick(1 - core, 1 - pair)
-    from_core = flip(to_core, 1, devices)
-    from_pair = flip(to_pair, 2, devices)
-    from_both = flip(to_both, 3, devices)
-
-    r_pair = flip(after(grad_rows, from_pair, from_both), 2, devices)
-    r_core = flip(grad_rows, 1, devices)
-    r_both = flip(r_pair, 1, devices)
     ids = route_ids[:, 0]
     i_pair = flip(ids, 2, devices)
     i_far = flip(jnp.concatenate([ids, i_pair]), 1, devices)
     all_ids = jnp.concatenate([ids, i_pair, i_far])
-    lhs = (grad_rows, r_pair, r_core, r_both)
+    from_core = flip(to_core, 1, devices)
+    if lines == 4:
+        to_pair, to_both = after((to_pair, to_both), i_pair)
+        from_pair = cross(to_pair, 2, devices)
+        from_both = cross(to_both, 3, devices)
+        straight = core == group
+        block1 = jnp.where(straight, keep, from_core)
+        mirror1 = jnp.where(straight, from_core, keep)
+        f11, b11 = step(block1, block1, 1, devices)
+        from_pair, from_both, rows_ready = after((from_pair, from_both, grad_rows), f11, b11)
+        rows_ready = after(rows_ready, from_pair, from_both)
+        core_ready = after(grad_rows, f11, b11)
+    else:
+        from_pair = flip(to_pair, 2, devices)
+        from_both = flip(to_both, 3, devices)
+        rows_ready = core_ready = grad_rows
+
+    r_pair = flip(rows_ready, 2, devices)
+    r_core = flip(core_ready, 1, devices)
     low = me % 4
     source = jnp.stack([low, low ^ 2, low ^ 1, low ^ 3])
     named = all_ids // devices == core
@@ -311,43 +303,39 @@
         straight = core == group
         block1 = jnp.where(straight, keep, from_core)
         mirror1 = jnp.where(straight, from_core, keep)
-        f1, b1 = step(block1, block1, 1, devices)
-        from_pair, from_both = after((from_pair, from_both), f1)
+        spots = jnp.stack([p, pair])
+        ends, mids = (0, 3, 4, 7), (1, 2, 5, 6)
         block2 = jnp.where(straight, from_pair, from_both)
-        mirror2 = jnp.where(straight, from_both, from_pair)
-        chains = []
-        for block, mirror, got in ((block1, mirror1, (f1, b1)), (block2, mirror2, None)):
-            f1, b1 = got or step(block, block, 1, devices)
-            f2, b2 = step(f1, b1, 2, devices)
-            inner = swap(f1, b1, p, (1, 2, 5, 6), devices)
-            f3, b3 = step(f2, b2, 3, devices)
-            outer = swap(f3, b3, p, (0, 3, 4, 7), devices)
-            chains.append((block, mirror, f1, b1, f2, b2, f3, b3, inner, outer))
-        early = [v for c in chains for v in (c[0], c[1], c[2], c[3], c[4], c[5], c[8])]
-        late = [v for c in chains for v in (c[2], c[4], c[6], c[3], c[5], c[7], c[9])]
-        spots = jnp.stack([p, pair])
-        acc = jax.ShapeDtypeStruct((2 * rows, half), F32)
-
-        def scratch(n):
-            return [
-                pltpu.VMEM((n * rows, width // 2), BF16),
-                pltpu.VMEM((width // 2, half), BF16),
-                pltpu.SemaphoreType.DMA((16,)),
-            ]
-
-        near = [
-            call(near_half, acc, [SM] + [ANY] * 16, scratch(2))(spots, *early, *pair_of)
-            for pair_of in ((lhs[0], lhs[2]), (lhs[1], lhs[3]))
-        ]
+        f12, b12 = step(f11, b11, 2, devices)
+        f21, b21 = step(block2, block2, 1, devices)
+        inner1 = swap(f11, b11, p, mids, devices)
+        f22, b22 = step(*after((f21, b21), f12, b12), 2, devices)
+        f13, b13 = step(*after((f12, b12), f21, b21), 3, devices)
+        inner2 = swap(f21, b21, p, mids, devices)
+        mirror2 = cycle(block2, [(a, 7 - a) for a in mids], devices)
+        outer1 = swap(f13, b13, p, ends, devices)
+        f23, b23 = step(*after((f22, b22), f13, b13), 3, devices)
+        r_both = flip(after(r_pair, f23, b23), 1, devices)
+        lhs = (grad_rows, r_pair, r_core, r_both)
+        outer2 = swap(f23, b23, p, ends, devices)
+        chain1 = (block1, mirror1, f11, f12, f13, b11, b12, b13, inner1, outer1)
+        chain2 = (block2, mirror2, f21, f22, f23, b21, b22, b23, inner2, outer2)
         base = jnp.where(named, all_ids % devices * cap, -(2 * rows))
         packed = call(
-            far_half,
+            product_cycle,
             jax.ShapeDtypeStruct((devices, 4, cap, half), BF16),
-            [SM, SM] + [VM] * 4 + [ANY] * 18,
-            scratch(4),
-        )(spots, source, base[:, None], base[None, :], *near, *late, *lhs)
+            [SM, SM] + [VM] * 2 + [ANY] * 24,
+            [
+                pltpu.VMEM((4 * rows, width), BF16),
+                pltpu.VMEM((width, half), BF16),
+                pltpu.VMEM((4 * rows, half), F32),
+                pltpu.SemaphoreType.DMA((32,)),
+            ],
+            limit=WHOLE,
+        )(spots, source, base[:, None], base[None, :], *chain1, *chain2, *lhs)
         packed = packed.reshape(devices, 4 * cap, half)
     else:
+        lhs = (grad_rows, r_pair, r_core, flip(r_pair, 1, devices))
         straight = jnp.stack([keep, from_pair, from_core, from_both])
         plane = jnp.zeros_like(straight).at[source].set(straight)
         ranks = [[a * 4 + w for a in range(lines)] for w in range(4)]

time: 181 us -> 160 us (0.88)
  waiting for transfers between devices: 91 us -> 76.9 us
  local copies, waits for them, and re-layouts: 9.9 us -> 1.72 us
  starting transfers between devices: 49.5 us -> 54.2 us
    ppermute x14 -> x12, waiting for transfers between devices: 47.5 us -> 11.3 us  [flip(): return lax.ppermute(value, 'seq', [(i, i ^ bits) for i in range(devices)])]
    ppermute x16 -> x17, waiting for transfers between devices: 16.1 us -> 35.8 us  [cycle(): return lax.ppermute(value, BOTH, pairs)]
    unnamed x64 -> x56, local copies, waits for them, and re-layouts: 8.18 us -> 1.49 us
    ppermute x0 -> x2, starting transfers between devices: none -> 5.22 us  [cross(): return lax.ppermute(value, BOTH, pairs)]
    pallas_call x3 -> x1, Pallas kernels: 16 us -> 12.1 us  [on_device(): call(product_cycle, jax.ShapeDtypeStruct((devices, 4, cap, half), BF16),...]
    ppermute x0 -> x2, waiting for transfers between devices: none -> 2.44 us  [cross(): return lax.ppermute(value, BOTH, pairs)]
    pallas_call x1, Pallas kernels: 0.7 us -> 2.92 us  [on_device(): call(cut, (block,) * 4, [SM, ANY, ANY], [pltpu.SemaphoreType.DMA((4,))],...]
    ppermute x14 -> x12, starting transfers between devices: 15.1 us -> 13.5 us  [flip(): return lax.ppermute(value, 'seq', [(i, i ^ bits) for i in range(devices)])]
  transfers between devices with their start and end apart: 31 -> 32, of which waited for: 17 -> 20; matrix products, arithmetic and copies ran while one was open for 6% -> 5% of each run, Pallas kernels for 5% -> 0%
where the time goes in v4:
time: 160 us
  waiting for transfers between devices  76.9 us (48%)
  starting transfers between devices  54.2 us (34%)
  Pallas kernels  17.5 us (11%)
  other arithmetic  8.38 us (5%)
  local copies, waits for them, and re-layouts  1.72 us (1%)
    ppermute x17, waiting for transfers between devices, cycle(): return lax.ppermute(value, BOTH, pairs)  35.8 us
    ppermute x17, starting transfers between devices, cycle(): return lax.ppermute(value, BOTH, pairs)  28.7 us
    all_to_all x1, waiting for transfers between devices, on_device(): arrived = lax.all_to_all(packed, 'seq', 0, 0, tiled=True)  27.4 us
    ppermute x12, starting transfers between devices, flip(): return lax.ppermute(value, 'seq', [(i, i ^ bits) for i in range(devices)])  13.5 us
    pallas_call x1, Pallas kernels, on_device(): call(product_cycle, jax.ShapeDtypeStruct((devices, 4, cap, half), BF16),...  12.1 us
    ppermute x12, waiting for transfers between devices, flip(): return lax.ppermute(value, 'seq', [(i, i ^ bits) for i in range(devices)])  11.3 us
    all_to_all x1, starting transfers between devices, on_device(): arrived = lax.all_to_all(packed, 'seq', 0, 0, tiled=True)  6.81 us
    ppermute x2, starting transfers between devices, cross(): return lax.ppermute(value, BOTH, pairs)  5.22 us
  transfers between devices with their start and end apart: 32, of which 20 were waited for; matrix products, arithmetic and copies ran while one was open for 5% of the time, Pallas kernels for 0%

profile of v4, /device:TPU:0, one launch (start us, length us, event | category | flops | bytes accessed | tf_op | source)
XLA Modules:
  0.0 159.7 jit_solution(46881953974728633)
XLA Ops:
  1.2 2.9 %shard_map.103 = (bf16[224,640]{1,0:T(8,128)(2,1)}, bf16[224,640]{1,0:T(8,128)(2,1)}, bf16[224,640]{1,0:T(8,128)(2,1)}, bf16[224,640]{1,0:T(8,128)(2,1)}) custom-call(s32[2]{0:T(128)} %pad_add_fusion.5.place, bf16[224,1280]{1,0:T(8,128)(2,1)} %bitcast.19, bf16[224,1280]{1,0:T(8,128)(2,1)} %bitcast.20), custom_call_target="tpu_custom_call" | custom-call | tf_op jit(solution)/shard_map/pallas_call | solution.py:266
  4.7 2.6 %collective-permute-start = (s32[256]{0:T(256)}, s32[256]{0:T(256)S(1)}, u32[]{:S(2)}, u32[]{:S(2)}) collective-permute-start(s32[256]{0:T(256)} %bitcast.21), channel_id=1, source_target_pairs={{0,2},{1,3},{2,0},{3,1},{4,6},{5,7},{6,4},{7,5},{8,10},{9,11},{10,... | collective-permute-start | bytes 3080 | tf_op jit(solution)/shard_map/ppermute | solution.py:21
  9.0 3.9 %collective-permute-start.7 = (bf16[224,640]{1,0:T(8,128)(2,1)}, bf16[224,640]{1,0:T(8,128)(2,1)S(1)}, u32[]{:S(2)}, u32[]{:S(2)}) collective-permute-start(bf16[224,640]{1,0:T(8,128)(2,1)} %get-tuple-element.28), channel_id=1, source_target_pairs={{0,2},{2,0},{4,6},{6,4},{8,10},{10,8},{12,14},{14,12},{17,19},{19,... | collective-permute-start | bytes 860168 | tf_op jit(solution)/shard_map/ppermute | solution.py:26
  18.0 2.4 %collective-permute-done.8 = bf16[224,640]{1,0:T(8,128)(2,1)S(1)} collective-permute-done((bf16[224,640]{1,0:T(8,128)(2,1)}, bf16[224,640]{1,0:T(8,128)(2,1)S(1)}, u32[]{:S(2)}, u32[]{:S(2)}) %collective-permute-start.8) | collective-permute-done | bytes 286752 | tf_op jit(solution)/shard_map/ppermute | solution.py:26
  20.5 3.6 %collective-permute-done.3.refs_6_ = bf16[224,640]{1,0:T(8,128)(2,1)S(1)} collective-permute-done((bf16[224,640]{1,0:T(8,128)(2,1)S(1)}, bf16[224,640]{1,0:T(8,128)(2,1)S(1)}, u32[]{:S(2)}, u32[]{:S(2)}) %collective-permute-start.3) | collective-permute-done | bytes 286752 | tf_op jit(solution)/shard_map/ppermute | solution.py:36
  26.9 2.3 %collective-permute-start.4 = (bf16[224,640]{1,0:T(8,128)(2,1)S(1)}, bf16[224,640]{1,0:T(8,128)(2,1)S(1)}, u32[]{:S(2)}, u32[]{:S(2)}) collective-permute-start(bf16[224,640]{1,0:T(8,128)(2,1)S(1)} %collective-permute-done.3.refs_6_), channel_id=1, source_target_pairs={{0,4},{1,5},{2,6},{3,7},{4,8},{5,9},{6,10},{7,11},{8,12},{9,13},{1... | collective-permute-start | bytes 860168 | tf_op jit(solution)/shard_map/ppermute | solution.py:36
  29.2 4.5 %collective-permute-done.10.refs_19_ = bf16[224,640]{1,0:T(8,128)(2,1)S(1)} collective-permute-done((bf16[224,640]{1,0:T(8,128)(2,1)S(1)}, bf16[224,640]{1,0:T(8,128)(2,1)S(1)}, u32[]{:S(2)}, u32[]{:S(2)}) %collective-permute-start.10) | collective-permute-done | bytes 286752 | tf_op jit(solution)/shard_map/ppermute | solution.py:36
  33.7 2.5 %collective-permute-done.9.refs_16_ = bf16[224,640]{1,0:T(8,128)(2,1)S(1)} collective-permute-done((bf16[224,640]{1,0:T(8,128)(2,1)S(1)}, bf16[224,640]{1,0:T(8,128)(2,1)S(1)}, u32[]{:S(2)}, u32[]{:S(2)}) %collective-permute-start.9) | collective-permute-done | bytes 286752 | tf_op jit(solution)/shard_map/ppermute | solution.py:36
  36.2 4.6 %collective-permute-done.4.refs_7_ = bf16[224,640]{1,0:T(8,128)(2,1)S(1)} collective-permute-done((bf16[224,640]{1,0:T(8,128)(2,1)S(1)}, bf16[224,640]{1,0:T(8,128)(2,1)S(1)}, u32[]{:S(2)}, u32[]{:S(2)}) %collective-permute-start.4) | collective-permute-done | bytes 286752 | tf_op jit(solution)/shard_map/ppermute | solution.py:36
  44.1 4.6 %collective-permute-start.12 = (bf16[224,640]{1,0:T(8,128)(2,1)S(1)}, bf16[224,640]{1,0:T(8,128)(2,1)S(1)}, u32[]{:S(2)}, u32[]{:S(2)}) collective-permute-start(bf16[224,640]{1,0:T(8,128)(2,1)S(1)} %collective-permute-done.6.refs_10_), channel_id=1, source_target_pairs={{0,16},{1,17},{2,18},{3,19},{4,0},{5,1},{6,2},{7,3},{8,4},{9,5},{1... | collective-permute-start | bytes 860168 | tf_op jit(solution)/shard_map/ppermute | solution.py:36
  50.6 3.9 %collective-permute-done.11.refs_8_ = bf16[224,640]{1,0:T(8,128)(2,1)S(1)} collective-permute-done((bf16[224,640]{1,0:T(8,128)(2,1)S(1)}, bf16[224,640]{1,0:T(8,128)(2,1)S(1)}, u32[]{:S(2)}, u32[]{:S(2)}) %collective-permute-start.11) | collective-permute-done | bytes 286752 | tf_op jit(solution)/shard_map/ppermute | solution.py:36
  56.5 4.6 %collective-permute-start.19 = (bf16[224,640]{1,0:T(8,128)(2,1)S(1)}, bf16[224,640]{1,0:T(8,128)(2,1)S(1)}, u32[]{:S(2)}, u32[]{:S(2)}) collective-permute-start(bf16[224,640]{1,0:T(8,128)(2,1)S(1)} %collective-permute-done.17.refs_20_), channel_id=1, source_target_pairs={{0,16},{1,17},{2,18},{3,19},{4,0},{5,1},{6,2},{7,3},{8,4},{9,5},{1... | collective-permute-start | bytes 860168 | tf_op jit(solution)/shard_map/ppermute | solution.py:36
  61.2 3.0 %collective-permute-done.18.refs_18_ = bf16[224,640]{1,0:T(8,128)(2,1)S(1)} collective-permute-done((bf16[224,640]{1,0:T(8,128)(2,1)S(1)}, bf16[224,640]{1,0:T(8,128)(2,1)S(1)}, u32[]{:S(2)}, u32[]{:S(2)}) %collective-permute-start.18) | collective-permute-done | bytes 286752 | tf_op jit(solution)/shard_map/ppermute | solution.py:36
  75.4 3.9 %collective-permute-start.14 = (bf16[224,640]{1,0:T(8,128)(2,1)}, bf16[224,640]{1,0:T(8,128)(2,1)S(1)}, u32[]{:S(2)}, u32[]{:S(2)}) collective-permute-start(bf16[224,640]{1,0:T(8,128)(2,1)} %broadcast_select_fusion.2), channel_id=1, source_target_pairs={{0,16},{1,17},{2,18},{3,19},{12,28},{13,29},{14,30},{15,31},{28,12... | collective-permute-start | bytes 860168 | tf_op jit(solution)/shard_map/ppermute | solution.py:36
  83.5 3.7 %collective-permute-done.14.refs_13_ = bf16[224,640]{1,0:T(8,128)(2,1)S(1)} collective-permute-done((bf16[224,640]{1,0:T(8,128)(2,1)}, bf16[224,640]{1,0:T(8,128)(2,1)S(1)}, u32[]{:S(2)}, u32[]{:S(2)}) %collective-permute-start.14) | collective-permute-done | bytes 286752 | tf_op jit(solution)/shard_map/ppermute | solution.py:36
  87.2 5.6 %collective-permute-done.21.refs_23_ = bf16[224,640]{1,0:T(8,128)(2,1)S(1)} collective-permute-done((bf16[224,640]{1,0:T(8,128)(2,1)}, bf16[224,640]{1,0:T(8,128)(2,1)S(1)}, u32[]{:S(2)}, u32[]{:S(2)}) %collective-permute-start.21) | collective-permute-done | bytes 286752 | tf_op jit(solution)/shard_map/ppermute | solution.py:36
  93.6 12.1 %shard_map.104 = bf16[16,4,16,640]{3,2,1,0:T(8,128)(2,1)} custom-call(s32[2]{0:T(128)} %pad_add_fusion.3.refs_0_, s32[4]{0:T(128)} %pad_add_fusion.4.refs_1_, s32[1024,1]{1,0:T(8,128)} %fusion.2.refs_2_, s32[1,1024]{1,0:T(1,128)} %compare_select_fusion.refs_3_, bf16[224,640]{1,0:T(8,128)(2,1)} %copy-done.16, bf16[224,640]{1,0:T(8,128)(2,1)} %get-tuple-element.45.refs_5_, ...), custom_call_target="tpu_custom_call" | custom-call | tf_op jit(solution)/shard_map/pallas_call | solution.py:324
  105.7 6.8 %all-to-all-start = ((bf16[16,64,640]{2,1,0:T(8,128)(2,1)}), bf16[16,64,640]{2,1,0:T(8,128)(2,1)S(1)}, u32[]{:S(2)}, u32[]{:S(2)}) async-start(bf16[16,64,640]{2,1,0:T(8,128)(2,1)} %bitcast.18), calls=%async_computation | async-start | bytes 2621440 | tf_op jit(solution)/shard_map/all_to_all | solution.py:350
  112.5 27.4 %all-to-all-done = bf16[16,64,640]{2,1,0:T(8,128)(2,1)S(1)} async-done(((bf16[16,64,640]{2,1,0:T(8,128)(2,1)}), bf16[16,64,640]{2,1,0:T(8,128)(2,1)S(1)}, u32[]{:S(2)}, u32[]{:S(2)}) %all-to-all-start) | async-done | bytes 1310752 | tf_op jit(solution)/shard_map/all_to_all | solution.py:350
  139.9 2.5 %shard_map.105 = (bf16[256,1280]{1,0:T(8,128)(2,1)}, bf16[256,1280]{1,0:T(8,128)(2,1)}, f32[2,1280]{1,0:T(2,128)S(1)}) custom-call(bf16[4,2,2,4,16,640]{5,4,3,2,1,0:T(8,128)(2,1)S(1)} %bitcast.17, bf16[256,1280]{1,0:T(8,128)(2,1)S(1)} %copy-done, bf16[256,1280]{1,0:T(8,128)(2,1)S(1)} %copy-done.1, f32[1,1280]{1,0:T(1,128)S(1)} %broadcast_in_dim.16.a_gain, ...), custom_call_target="tpu_custom_call" | custom-call | tf_op jit(solution)/shard_map/pallas_call | solution.py:355
  143.2 2.3 %collective-permute-start.26 = (f32[2,1280]{1,0:T(2,128)S(1)}, f32[2,1280]{1,0:T(2,128)S(1)}, u32[]{:S(2)}, u32[]{:S(2)}) collective-permute-start(f32[2,1280]{1,0:T(2,128)S(1)} %get-tuple-element.44), channel_id=1, source_target_pairs={{0,2},{1,3},{2,0},{3,1},{4,6},{5,7},{6,4},{7,5},{8,10},{9,11},{10,... | collective-permute-start | bytes 30728 | tf_op jit(solution)/shard_map/ppermute | solution.py:21
  148.6 3.7 %collective-permute-start.28 = (f32[2,1280]{1,0:T(2,128)S(1)}, f32[2,1280]{1,0:T(2,128)S(1)}, u32[]{:S(2)}, u32[]{:S(2)}) collective-permute-start(f32[2,1280]{1,0:T(2,128)S(1)} %add_add_fusion.1), channel_id=1, source_target_pairs={{0,4},{1,5},{2,6},{3,7},{4,0},{5,1},{6,2},{7,3},{8,12},{9,13},{10,... | collective-permute-start | bytes 30728 | tf_op jit(solution)/shard_map/ppermute | solution.py:21
  154.7 2.1 %collective-permute-done.29 = f32[2,1280]{1,0:T(2,128)S(1)} collective-permute-done((f32[2,1280]{1,0:T(2,128)S(1)}, f32[2,1280]{1,0:T(2,128)S(1)}, u32[]{:S(2)}, u32[]{:S(2)}) %collective-permute-start.29) | collective-permute-done | bytes 10272 | tf_op jit(solution)/shard_map/ppermute | solution.py:21
  156.8 2.3 %collective-permute-done.30 = f32[2,1280]{1,0:T(2,128)S(1)} collective-permute-done((f32[2,1280]{1,0:T(2,128)S(1)}, f32[2,1280]{1,0:T(2,128)S(1)}, u32[]{:S(2)}, u32[]{:S(2)}) %collective-permute-start.30) | collective-permute-done | bytes 10272 | tf_op jit(solution)/shard_map/ppermute | solution.py:21
  (117 shorter events, 41.2 us)
Async XLA Ops:
  4.2 10.1 %collective-permute-start.2 = (bf16[224,640]{1,0:T(8,128)(2,1)}, bf16[224,640]{1,0:T(8,128)(2,1)S(1)}, u32[]{:S(2)}, u32[]{:S(2)}) collective-permute-start(bf16[224,640]{1,0:T(8,128)(2,1)} %get-tuple-element.25), channel_id=1, source_target_pairs={{0,1},{1,0},{2,3},{3,2},{4,5},{5,4},{6,7},{7,6},{8,9},{9,8},{10,11... | collective-permute-start | bytes 860168 | tf_op jit(solution)/shard_map/ppermute | solution.py:21
  9.0 9.0 %collective-permute-start.7 = (bf16[224,640]{1,0:T(8,128)(2,1)}, bf16[224,640]{1,0:T(8,128)(2,1)S(1)}, u32[]{:S(2)}, u32[]{:S(2)}) collective-permute-start(bf16[224,640]{1,0:T(8,128)(2,1)} %get-tuple-element.28), channel_id=1, source_target_pairs={{0,2},{2,0},{4,6},{6,4},{8,10},{10,8},{12,14},{14,12},{17,19},{19,... | collective-permute-start | bytes 860168 | tf_op jit(solution)/shard_map/ppermute | solution.py:26
  12.9 7.5 %collective-permute-start.8 = (bf16[224,640]{1,0:T(8,128)(2,1)}, bf16[224,640]{1,0:T(8,128)(2,1)S(1)}, u32[]{:S(2)}, u32[]{:S(2)}) collective-permute-start(bf16[224,640]{1,0:T(8,128)(2,1)} %get-tuple-element.29), channel_id=1, source_target_pairs={{0,3},{2,1},{4,7},{6,5},{8,11},{10,9},{12,15},{14,13},{17,18},{19,... | collective-permute-start | bytes 860168 | tf_op jit(solution)/shard_map/ppermute | solution.py:26
  16.0 8.0 %collective-permute-start.3 = (bf16[224,640]{1,0:T(8,128)(2,1)S(1)}, bf16[224,640]{1,0:T(8,128)(2,1)S(1)}, u32[]{:S(2)}, u32[]{:S(2)}) collective-permute-start(bf16[224,640]{1,0:T(8,128)(2,1)S(1)} %get-tuple-element.46.refs_4_), channel_id=1, source_target_pairs={{0,4},{1,5},{2,6},{3,7},{4,8},{5,9},{6,10},{7,11},{8,12},{9,13},{1... | collective-permute-start | bytes 860168 | tf_op jit(solution)/shard_map/ppermute | solution.py:36
  17.6 6.6 %collective-permute-start.5 = (bf16[224,640]{1,0:T(8,128)(2,1)S(1)}, bf16[224,640]{1,0:T(8,128)(2,1)S(1)}, u32[]{:S(2)}, u32[]{:S(2)}) collective-permute-start(bf16[224,640]{1,0:T(8,128)(2,1)S(1)} %get-tuple-element.46.refs_4_), channel_id=1, source_target_pairs={{0,16},{1,17},{2,18},{3,19},{4,0},{5,1},{6,2},{7,3},{8,4},{9,5},{1... | collective-permute-start | bytes 860168 | tf_op jit(solution)/shard_map/ppermute | solution.py:36
  24.2 41.6 %collective-permute-start.22 = (bf16[256,3584]{1,0:T(8,128)(2,1)S(1)}, bf16[256,3584]{1,0:T(8,128)(2,1)}, u32[]{:S(2)}, u32[]{:S(2)}) collective-permute-start(bf16[256,3584]{1,0:T(8,128)(2,1)S(1)} %copy-done.2), channel_id=1, source_target_pairs={{0,2},{1,3},{2,0},{3,1},{4,6},{5,7},{6,4},{7,5},{8,10},{9,11},{10,... | collective-permute-start | bytes 5505032 | tf_op jit(solution)/shard_map/ppermute | solution.py:21
  24.8 8.9 %collective-permute-start.10 = (bf16[224,640]{1,0:T(8,128)(2,1)S(1)}, bf16[224,640]{1,0:T(8,128)(2,1)S(1)}, u32[]{:S(2)}, u32[]{:S(2)}) collective-permute-start(bf16[224,640]{1,0:T(8,128)(2,1)S(1)} %broadcast_select_fusion.4.refs_14_), channel_id=1, source_target_pairs={{0,16},{1,17},{2,18},{3,19},{4,0},{5,1},{6,2},{7,3},{8,4},{9,5},{1... | collective-permute-start | bytes 860168 | tf_op jit(solution)/shard_map/ppermute | solution.py:36
  26.4 9.8 %collective-permute-start.9 = (bf16[224,640]{1,0:T(8,128)(2,1)S(1)}, bf16[224,640]{1,0:T(8,128)(2,1)S(1)}, u32[]{:S(2)}, u32[]{:S(2)}) collective-permute-start(bf16[224,640]{1,0:T(8,128)(2,1)S(1)} %broadcast_select_fusion.4.refs_14_), channel_id=1, source_target_pairs={{0,4},{1,5},{2,6},{3,7},{4,8},{5,9},{6,10},{7,11},{8,12},{9,13},{1... | collective-permute-start | bytes 860168 | tf_op jit(solution)/shard_map/ppermute | solution.py:36
  26.9 13.9 %collective-permute-start.4 = (bf16[224,640]{1,0:T(8,128)(2,1)S(1)}, bf16[224,640]{1,0:T(8,128)(2,1)S(1)}, u32[]{:S(2)}, u32[]{:S(2)}) collective-permute-start(bf16[224,640]{1,0:T(8,128)(2,1)S(1)} %collective-permute-done.3.refs_6_), channel_id=1, source_target_pairs={{0,4},{1,5},{2,6},{3,7},{4,8},{5,9},{6,10},{7,11},{8,12},{9,13},{1... | collective-permute-start | bytes 860168 | tf_op jit(solution)/shard_map/ppermute | solution.py:36
  29.2 11.6 %collective-permute-start.6 = (bf16[224,640]{1,0:T(8,128)(2,1)S(1)}, bf16[224,640]{1,0:T(8,128)(2,1)S(1)}, u32[]{:S(2)}, u32[]{:S(2)}) collective-permute-start(bf16[224,640]{1,0:T(8,128)(2,1)S(1)} %collective-permute-done.5.refs_9_), channel_id=1, source_target_pairs={{0,16},{1,17},{2,18},{3,19},{4,0},{5,1},{6,2},{7,3},{8,4},{9,5},{1... | collective-permute-start | bytes 860168 | tf_op jit(solution)/shard_map/ppermute | solution.py:36
  40.8 9.8 %collective-permute-start.16 = (bf16[224,640]{1,0:T(8,128)(2,1)S(1)}, bf16[224,640]{1,0:T(8,128)(2,1)S(1)}, u32[]{:S(2)}, u32[]{:S(2)}) collective-permute-start(bf16[224,640]{1,0:T(8,128)(2,1)S(1)} %collective-permute-done.9.refs_16_), channel_id=1, source_target_pairs={{0,4},{1,5},{2,6},{3,7},{4,8},{5,9},{6,10},{7,11},{8,12},{9,13},{1... | collective-permute-start | bytes 860168 | tf_op jit(solution)/shard_map/ppermute | solution.py:36
  40.9 9.7 %collective-permute-start.17 = (bf16[224,640]{1,0:T(8,128)(2,1)S(1)}, bf16[224,640]{1,0:T(8,128)(2,1)S(1)}, u32[]{:S(2)}, u32[]{:S(2)}) collective-permute-start(bf16[224,640]{1,0:T(8,128)(2,1)S(1)} %collective-permute-done.10.refs_19_), channel_id=1, source_target_pairs={{0,16},{1,17},{2,18},{3,19},{4,0},{5,1},{6,2},{7,3},{8,4},{9,5},{1... | collective-permute-start | bytes 860168 | tf_op jit(solution)/shard_map/ppermute | solution.py:36
  42.9 11.6 %collective-permute-start.11 = (bf16[224,640]{1,0:T(8,128)(2,1)S(1)}, bf16[224,640]{1,0:T(8,128)(2,1)S(1)}, u32[]{:S(2)}, u32[]{:S(2)}) collective-permute-start(bf16[224,640]{1,0:T(8,128)(2,1)S(1)} %collective-permute-done.4.refs_7_), channel_id=1, source_target_pairs={{4,8},{5,9},{6,10},{7,11},{8,12},{9,13},{10,14},{11,15},{12,28},{1... | collective-permute-start | bytes 860168 | tf_op jit(solution)/shard_map/ppermute | solution.py:36
  44.1 11.1 %collective-permute-start.12 = (bf16[224,640]{1,0:T(8,128)(2,1)S(1)}, bf16[224,640]{1,0:T(8,128)(2,1)S(1)}, u32[]{:S(2)}, u32[]{:S(2)}) collective-permute-start(bf16[224,640]{1,0:T(8,128)(2,1)S(1)} %collective-permute-done.6.refs_10_), channel_id=1, source_target_pairs={{0,16},{1,17},{2,18},{3,19},{4,0},{5,1},{6,2},{7,3},{8,4},{9,5},{1... | collective-permute-start | bytes 860168 | tf_op jit(solution)/shard_map/ppermute | solution.py:36
  55.3 8.9 %collective-permute-start.18 = (bf16[224,640]{1,0:T(8,128)(2,1)S(1)}, bf16[224,640]{1,0:T(8,128)(2,1)S(1)}, u32[]{:S(2)}, u32[]{:S(2)}) collective-permute-start(bf16[224,640]{1,0:T(8,128)(2,1)S(1)} %collective-permute-done.16.refs_17_), channel_id=1, source_target_pairs={{4,8},{5,9},{6,10},{7,11},{8,12},{9,13},{10,14},{11,15},{12,28},{1... | collective-permute-start | bytes 860168 | tf_op jit(solution)/shard_map/ppermute | solution.py:36
  56.5 9.3 %collective-permute-start.19 = (bf16[224,640]{1,0:T(8,128)(2,1)S(1)}, bf16[224,640]{1,0:T(8,128)(2,1)S(1)}, u32[]{:S(2)}, u32[]{:S(2)}) collective-permute-start(bf16[224,640]{1,0:T(8,128)(2,1)S(1)} %collective-permute-done.17.refs_20_), channel_id=1, source_target_pairs={{0,16},{1,17},{2,18},{3,19},{4,0},{5,1},{6,2},{7,3},{8,4},{9,5},{1... | collective-permute-start | bytes 860168 | tf_op jit(solution)/shard_map/ppermute | solution.py:36
  61.1 31.7 %collective-permute-start.23 = (bf16[256,3584]{1,0:T(8,128)(2,1)S(1)}, bf16[256,3584]{1,0:T(8,128)(2,1)}, u32[]{:S(2)}, u32[]{:S(2)}) collective-permute-start(bf16[256,3584]{1,0:T(8,128)(2,1)S(1)} %copy-done.2), channel_id=1, source_target_pairs={{0,1},{1,0},{2,3},{3,2},{4,5},{5,4},{6,7},{7,6},{8,9},{9,8},{10,11... | collective-permute-start | bytes 5505032 | tf_op jit(solution)/shard_map/ppermute | solution.py:21
  66.5 26.3 %collective-permute-start.24 = (bf16[256,3584]{1,0:T(8,128)(2,1)}, bf16[256,3584]{1,0:T(8,128)(2,1)}, u32[]{:S(2)}, u32[]{:S(2)}) collective-permute-start(bf16[256,3584]{1,0:T(8,128)(2,1)} %collective-permute-done.22.refs_25_), channel_id=1, source_target_pairs={{0,1},{1,0},{2,3},{3,2},{4,5},{5,4},{6,7},{7,6},{8,9},{9,8},{10,11... | collective-permute-start | bytes 5505032 | tf_op jit(solution)/shard_map/ppermute | solution.py:21
  70.3 9.0 %collective-permute-start.15 = (bf16[224,640]{1,0:T(8,128)(2,1)S(1)}, bf16[224,640]{1,0:T(8,128)(2,1)S(1)}, u32[]{:S(2)}, u32[]{:S(2)}) collective-permute-start(bf16[224,640]{1,0:T(8,128)(2,1)S(1)} %broadcast_select_fusion.4.refs_14_), channel_id=1, source_target_pairs={{4,20},{5,21},{6,22},{7,23},{8,24},{9,25},{10,26},{11,27},{24,8},{... | collective-permute-start | bytes 860168 | tf_op jit(solution)/shard_map/ppermute | solution.py:36
  72.5 11.0 %collective-permute-start.20 = (bf16[224,640]{1,0:T(8,128)(2,1)}, bf16[224,640]{1,0:T(8,128)(2,1)}, u32[]{:S(2)}, u32[]{:S(2)}) collective-permute-start(bf16[224,640]{1,0:T(8,128)(2,1)} %broadcast_select_fusion.1), channel_id=1, source_target_pairs={{4,20},{5,21},{6,22},{7,23},{8,24},{9,25},{10,26},{11,27},{24,8},{... | collective-permute-start | bytes 860168 | tf_op jit(solution)/shard_map/ppermute | solution.py:36
  75.4 11.8 %collective-permute-start.14 = (bf16[224,640]{1,0:T(8,128)(2,1)}, bf16[224,640]{1,0:T(8,128)(2,1)S(1)}, u32[]{:S(2)}, u32[]{:S(2)}) collective-permute-start(bf16[224,640]{1,0:T(8,128)(2,1)} %broadcast_select_fusion.2), channel_id=1, source_target_pairs={{0,16},{1,17},{2,18},{3,19},{12,28},{13,29},{14,30},{15,31},{28,12... | collective-permute-start | bytes 860168 | tf_op jit(solution)/shard_map/ppermute | solution.py:36
  79.4 13.5 %collective-permute-start.21 = (bf16[224,640]{1,0:T(8,128)(2,1)}, bf16[224,640]{1,0:T(8,128)(2,1)S(1)}, u32[]{:S(2)}, u32[]{:S(2)}) collective-permute-start(bf16[224,640]{1,0:T(8,128)(2,1)} %broadcast_select_fusion), channel_id=1, source_target_pairs={{0,16},{1,17},{2,18},{3,19},{12,28},{13,29},{14,30},{15,31},{28,12... | collective-permute-start | bytes 860168 | tf_op jit(solution)/shard_map/ppermute | solution.py:36
  105.7 34.2 %all-to-all-start = ((bf16[16,64,640]{2,1,0:T(8,128)(2,1)}), bf16[16,64,640]{2,1,0:T(8,128)(2,1)S(1)}, u32[]{:S(2)}, u32[]{:S(2)}) async-start(bf16[16,64,640]{2,1,0:T(8,128)(2,1)} %bitcast.18), calls=%async_computation | async-start | bytes 2621440 | tf_op jit(solution)/shard_map/all_to_all | solution.py:350
  148.6 6.1 %collective-permute-start.28 = (f32[2,1280]{1,0:T(2,128)S(1)}, f32[2,1280]{1,0:T(2,128)S(1)}, u32[]{:S(2)}, u32[]{:S(2)}) collective-permute-start(f32[2,1280]{1,0:T(2,128)S(1)} %add_add_fusion.1), channel_id=1, source_target_pairs={{0,4},{1,5},{2,6},{3,7},{4,0},{5,1},{6,2},{7,3},{8,12},{9,13},{10,... | collective-permute-start | bytes 30728 | tf_op jit(solution)/shard_map/ppermute | solution.py:21
  (36 other events, 629.1 us)

commit v5 on v4

--- a/solution.py
+++ b/solution.py
@@ -13,7 +13,6 @@
 BIG = 24 * 1024 * 1024
 WHOLE = 60 * 1024 * 1024
 VM = pl.BlockSpec(memory_space=pltpu.VMEM)
-SM = pl.BlockSpec(memory_space=pltpu.SMEM)
 ANY = pl.BlockSpec(memory_space=pl.ANY)
 
 
@@ -21,14 +20,9 @@
     return lax.ppermute(value, "seq", [(i, i ^ bits) for i in range(devices)])
 
 
-def cross(value, bits, devices):
-    pairs = [(g * devices + i, g * devices + (i ^ bits)) for g in range(2) for i in range(g, devices, 2)]
-    return lax.ppermute(value, BOTH, pairs)
-
-
 def spot(p, low, devices):
     group, line = (0, p) if p < 4 else (1, 7 - p)
-    return group * devices + line * 4 + low
+    return group * devices + line * 4 + (low ^ group)
 
 
 def cycle(value, moves, devices):
@@ -54,22 +48,26 @@
     return cycle(jnp.where(first, bwd, fwd), [(a, 7 - a) for a in spots], devices)
 
 
-def cut(place, a_ref, v_ref, keep, to_core, to_pair, to_both, sems):
-    pair, core = place[0], place[1]
+def seat():
+    me = lax.axis_index("seq")
+    return lax.axis_index("groups"), me // 4, lax.rem(me // 2, 2), lax.rem(me, 2)
+
+
+def cut(a_ref, v_ref, keep, to_pair, to_core, sems):
+    group, _, pair, core = seat()
     half = keep.shape[1]
     near = pl.ds(pl.multiple_of(pair * half, 128), half)
     away = pl.ds(pl.multiple_of((1 - pair) * half, 128), half)
-    for here in range(2):
-        mine, other = (a_ref, v_ref) if here == 0 else (v_ref, a_ref)
-
-        @pl.when(core == here)
+    for same in (True, False):
+        mine, other = (a_ref, v_ref) if same else (v_ref, a_ref)
+
+        @pl.when((core == group) == same)
         def _():
-            pltpu.make_async_copy(other.at[:, near], to_core, sems.at[0]).start()
-            pltpu.make_async_copy(mine.at[:, near], keep, sems.at[1]).start()
-            pltpu.make_async_copy(mine.at[:, away], to_pair, sems.at[2]).start()
-            pltpu.make_async_copy(other.at[:, away], to_both, sems.at[3]).start()
-
-    for i, out in enumerate((to_core, keep, to_pair, to_both)):
+            pltpu.make_async_copy(mine.at[:, near], keep, sems.at[0]).start()
+            pltpu.make_async_copy(mine.at[:, away], to_pair, sems.at[1]).start()
+            pltpu.make_async_copy(other.at[:, near], to_core, sems.at[2]).start()
+
+    for i, out in enumerate((keep, to_pair, to_core)):
         pltpu.make_async_copy(a_ref.at[:, near], out, sems.at[i]).wait()
 
 
@@ -100,21 +98,22 @@
 
 
 def product_cycle(*refs):
-    place, source, base_col, base_row = refs[:4]
+    ids = refs[:4]
     parts, lhs = refs[4:24], refs[24:28]
     out, buf, w, acc, sems = refs[28:]
     deep = parts[0].shape[0]
     rows = lhs[0].shape[0]
     devices, sources, cap, half = out.shape
-    p, x = place[0], place[1]
-    ends = p % 4
-    line = line_of(p)
+    group, line, x, core = seat()
+    modality = lax.rem(core + group, 2)
+    p = jnp.where(group == 0, line, 7 - line)
+    ends = lax.rem(p, 4)
     second = second_line(line)
     third, fourth = last_lines(line)
     copies = load_rows(lhs, (line, second, third, fourth), buf, sems)
 
     def move(ref, q, slot, which, i):
-        start = pl.multiple_of(((slot * 2 + which) * 2 + q // 4) * deep, 16)
+        start = pl.multiple_of(((slot * 2 + which) * 2 + lax.rem(q // 4 + modality, 2)) * deep, 16)
         return pltpu.make_async_copy(ref, w.at[pl.ds(start, deep)], sems.at[i])
 
     for j in range(2):
@@ -136,24 +135,28 @@
                         move(ref, 7 - p, 0, which, 4 * chain + 1).start()
                         takes = ((b1, f2), (b1, inner), (f1, inner), (f1, b2))[case]
                         for i, (ref, step) in enumerate(takes):
-                            move(ref, (p + step) % 8, 1, which, 4 * chain + 2 + i).start()
+                            move(ref, lax.rem(p + step, 8), 1, which, 4 * chain + 2 + i).start()
                     else:
                         takes = ((b2, f3, b3, outer), (f1, f2, b2, b3), (f2, f3, b1, b2), (f2, f3, b3, outer))[case]
                         for i, (ref, step) in enumerate(takes):
-                            q = (p + step) % 8
+                            q = lax.rem(p + step, 8)
                             slot = jnp.where(line_of(q) == third, 2, 3)
                             move(ref, q, slot, which, 8 + 4 * chain + i).start()
 
-    first = lax.broadcasted_iota(jnp.int32, (rows, rows), 0)
-    later = lax.broadcasted_iota(jnp.int32, (rows, rows), 1)
+    earlier = lax.broadcasted_iota(jnp.int32, (rows, rows), 0) < lax.broadcasted_iota(jnp.int32, (rows, rows), 1)
+    earlier = earlier.astype(F32).astype(BF16)
+    kinds = lax.broadcasted_iota(jnp.int32, (devices, rows), 0) + modality * devices
     slots = lax.broadcasted_iota(jnp.int32, (devices * cap, rows), 0)
     picks = []
-    for s in range(4):
-        col = base_col[s * rows : (s + 1) * rows, :]
-        row = base_row[:, s * rows : (s + 1) * rows]
-        same = jnp.logical_and(col == row, first < later)
-        count = jnp.sum(same.astype(F32), axis=0, keepdims=True).astype(jnp.int32)
-        picks.append((slots == row + count).astype(F32).astype(BF16))
+    for id_ref in ids:
+        named_by = id_ref[...]
+        named = (kinds == named_by).astype(F32)
+        before = jnp.dot(named.astype(BF16), earlier, preferred_element_type=F32)
+        count = jnp.sum(named * before, axis=0, keepdims=True).astype(jnp.int32)
+        slot = (named_by - modality * devices) * cap + count
+        picks.append((slots == slot).astype(F32).astype(BF16))
+    low = x * 2 + core
+    source = (low, (1 - x) * 2 + core, x * 2 + 1 - core, (1 - x) * 2 + 1 - core)
     for j in range(2):
         for c in copies[8 * j : 8 * j + 8]:
             c.wait()
@@ -186,12 +189,13 @@
 
 
 def norms(recv, a_states, v_states, a_gain, v_gain, a_out, v_out, gains):
+    group = lax.axis_index("groups")
     rows, width = a_states.shape
     half = width // 2
     inv = 1.0 / width
 
     def upstream(h, m):
-        return recv[:, h, m].reshape(rows, half).astype(F32)
+        return recv[:, h, lax.rem(m + group, 2)].reshape(rows, half).astype(F32)
 
     def cols(h):
         return slice(h * half, (h + 1) * half)
@@ -261,70 +265,43 @@
     me = lax.axis_index("seq")
     line, pair, core = me // 4, (me // 2) % 2, me % 2
 
-    block = jax.ShapeDtypeStruct((k, half), BF16)
+    modality = (core + group) % 2
+    ids = route_ids.reshape(1, rows)
+
     if lines == 4:
-        keep, to_core, to_pair, to_both = call(
-            cut, (block,) * 4, [SM, ANY, ANY], [pltpu.SemaphoreType.DMA((4,))], VM, WHOLE
-        )(jnp.stack([pair, core]), audio_proj.T, vision_proj.T)
-    else:
-        both = jnp.stack([audio_proj.T, vision_proj.T]).reshape(2, k, 2, half)
-        pick = lambda m, h: both[m, :, h]
-        keep, to_core = pick(core, pair), pick(1 - core, pair)
-        to_pair, to_both = pick(core, 1 - pair), pick(1 - core, 1 - pair)
-    ids = route_ids[:, 0]
-    i_pair = flip(ids, 2, devices)
-    i_far = flip(jnp.concatenate([ids, i_pair]), 1, devices)
-    all_ids = jnp.concatenate([ids, i_pair, i_far])
-    from_core = flip(to_core, 1, devices)
-    if lines == 4:
-        to_pair, to_both = after((to_pair, to_both), i_pair)
-        from_pair = cross(to_pair, 2, devices)
-        from_both = cross(to_both, 3, devices)
-        straight = core == group
-        block1 = jnp.where(straight, keep, from_core)
-        mirror1 = jnp.where(straight, from_core, keep)
+        block = jax.ShapeDtypeStruct((k, half), BF16)
+        block1, to_pair, to_core = call(
+            cut, (block,) * 3, [ANY, ANY], [pltpu.SemaphoreType.DMA((3,))], VM, WHOLE
+        )(audio_proj.T, vision_proj.T)
+        from_pair = flip(to_pair, 2, devices)
+        p = jnp.where(group == 0, line, 7 - line)
+        ends, mids = (0, 3, 4, 7), (1, 2, 5, 6)
         f11, b11 = step(block1, block1, 1, devices)
-        from_pair, from_both, rows_ready = after((from_pair, from_both, grad_rows), f11, b11)
-        rows_ready = after(rows_ready, from_pair, from_both)
-        core_ready = after(grad_rows, f11, b11)
-    else:
-        from_pair = flip(to_pair, 2, devices)
-        from_both = flip(to_both, 3, devices)
-        rows_ready = core_ready = grad_rows
-
-    r_pair = flip(rows_ready, 2, devices)
-    r_core = flip(core_ready, 1, devices)
-    low = me % 4
-    source = jnp.stack([low, low ^ 2, low ^ 1, low ^ 3])
-    named = all_ids // devices == core
-
-    if lines == 4:
-        p = jnp.where(group == 0, line, 7 - line)
-        straight = core == group
-        block1 = jnp.where(straight, keep, from_core)
-        mirror1 = jnp.where(straight, from_core, keep)
-        spots = jnp.stack([p, pair])
-        ends, mids = (0, 3, 4, 7), (1, 2, 5, 6)
-        block2 = jnp.where(straight, from_pair, from_both)
+        block2 = after(from_pair, f11, b11)
+        r_pair = flip(after(grad_rows, block2), 2, devices)
+        r_core = flip(after(grad_rows, block2), 1, devices)
+        mirror1 = flip(after(to_core, block2), 1, devices)
+        i_core = flip(after(ids, block2), 1, devices)
+        inner1 = swap(f11, b11, p, mids, devices)
         f12, b12 = step(f11, b11, 2, devices)
         f21, b21 = step(block2, block2, 1, devices)
-        inner1 = swap(f11, b11, p, mids, devices)
+        mirror2 = cycle(block2, [(a, 7 - a) for a in mids], devices)
         f22, b22 = step(*after((f21, b21), f12, b12), 2, devices)
-        f13, b13 = step(*after((f12, b12), f21, b21), 3, devices)
+        f13, b13 = step(*after((f12, b12), f21, b21, inner1), 3, devices)
         inner2 = swap(f21, b21, p, mids, devices)
-        mirror2 = cycle(block2, [(a, 7 - a) for a in mids], devices)
         outer1 = swap(f13, b13, p, ends, devices)
-        f23, b23 = step(*after((f22, b22), f13, b13), 3, devices)
-        r_both = flip(after(r_pair, f23, b23), 1, devices)
-        lhs = (grad_rows, r_pair, r_core, r_both)
+        f23, b23 = step(*after((f22, b22), outer1, inner2, mirror2), 3, devices)
         outer2 = swap(f23, b23, p, ends, devices)
+        r_there = after(r_pair, f23, b23)
+        r_both = flip(r_there, 1, devices)
+        late_ids = after(ids, r_there)
+        i_pair, i_both = flip(late_ids, 2, devices), flip(late_ids, 3, devices)
         chain1 = (block1, mirror1, f11, f12, f13, b11, b12, b13, inner1, outer1)
         chain2 = (block2, mirror2, f21, f22, f23, b21, b22, b23, inner2, outer2)
-        base = jnp.where(named, all_ids % devices * cap, -(2 * rows))
         packed = call(
             product_cycle,
             jax.ShapeDtypeStruct((devices, 4, cap, half), BF16),
-            [SM, SM] + [VM] * 2 + [ANY] * 24,
+            [VM] * 4 + [ANY] * 24,
             [
                 pltpu.VMEM((4 * rows, width), BF16),
                 pltpu.VMEM((width, half), BF16),
@@ -332,21 +309,30 @@
                 pltpu.SemaphoreType.DMA((32,)),
             ],
             limit=WHOLE,
-        )(spots, source, base[:, None], base[None, :], *chain1, *chain2, *lhs)
-        packed = packed.reshape(devices, 4 * cap, half)
+        )(ids, i_pair, i_core, i_both, *chain1, *chain2, grad_rows, r_pair, r_core, r_both)
     else:
-        lhs = (grad_rows, r_pair, r_core, flip(r_pair, 1, devices))
-        straight = jnp.stack([keep, from_pair, from_core, from_both])
-        plane = jnp.zeros_like(straight).at[source].set(straight)
+        both = jnp.stack([audio_proj.T, vision_proj.T]).reshape(2, k, 2, half)
+        plane = [both[modality, :, pair]]
+        plane.append(flip(both[modality, :, 1 - pair], 2, devices))
+        plane.append(flip(both[1 - modality, :, pair], 1, devices))
+        plane.append(flip(both[1 - modality, :, 1 - pair], 3, devices))
+        low = me % 4
+        source = jnp.stack([low, low ^ 2, low ^ 1, low ^ 3])
+        plane = jnp.zeros((4, k, half), BF16).at[source].set(jnp.stack(plane))
         ranks = [[a * 4 + w for a in range(lines)] for w in range(4)]
         w = lax.all_gather(plane.reshape(4 * k, half), "seq", axis=0, tiled=True, axis_index_groups=ranks)
-        where_from = jnp.repeat(source, rows)
-        base = jnp.where(named, (all_ids % devices * 4 + where_from) * cap, -(8 * rows))
+        i_pair = flip(ids, 2, devices)
+        i_far = flip(jnp.concatenate([ids, i_pair], axis=1), 1, devices)
+        r_pair = flip(grad_rows, 2, devices)
+        lhs = (grad_rows, r_pair, flip(grad_rows, 1, devices), flip(r_pair, 1, devices))
+        all_ids = jnp.concatenate([ids, i_pair, i_far], axis=1)
+        base = (all_ids % devices * 4 + jnp.repeat(source, rows)[None, :]) * cap
+        base = jnp.where(all_ids // devices == modality, base, -(8 * rows))
         packed = call(product_plain, jax.ShapeDtypeStruct((4 * rows, half), BF16), [VM] * 7)(
-            base[:, None], base[None, :], *lhs, w
+            base.reshape(-1, 1), base, *lhs, w
         )
-        packed = packed.reshape(devices, 4 * cap, half)
-
+
+    packed = packed.reshape(devices, 4 * cap, half)
     arrived = lax.all_to_all(packed, "seq", 0, 0, tiled=True)
     arrived = arrived.reshape(lines, 2, 2, 4, cap, half)
     if cap % 16 != 0:
@@ -363,13 +349,8 @@
     )(arrived, audio_states, vision_states, audio_gain[None, :], vision_gain[None, :])
     bit = 1
     while bit < devices:
-        near = flip(gains, bit, devices)
-        if 2 * bit < devices:
-            far = flip(gains, 2 * bit, devices) + flip(gains, 3 * bit, devices)
-            gains = (gains + near) + far
-        else:
-            gains = gains + near
-        bit *= 4
+        gains = gains + flip(gains, bit, devices)
+        bit *= 2
     return (audio_grad, vision_grad, gains)
 
 

time: 160 us -> 152 us (0.950)
  other arithmetic: 8.38 us -> 0.78 us
  waiting for transfers between devices: 76.9 us -> 81.4 us
  starting transfers between devices: 54.2 us -> 49.8 us
    ppermute x17, waiting for transfers between devices: 35.8 us -> 46.6 us  [cycle(): return lax.ppermute(value, BOTH, pairs)]
    ppermute x2 -> x0, starting transfers between devices: 5.22 us -> none  [cross(): return lax.ppermute(value, BOTH, pairs)]
    ppermute x12, waiting for transfers between devices: 11.3 us -> 7.4 us  [flip(): return lax.ppermute(value, 'seq', [(i, i ^ bits) for i in range(devices)])]
    ppermute x12, starting transfers between devices: 13.5 us -> 17.2 us  [flip(): return lax.ppermute(value, 'seq', [(i, i ^ bits) for i in range(devices)])]
    select_n x4 -> x0, other arithmetic: 3.69 us -> none  [the longest x2 1.92 us: on_device(): base = jnp.where(named, all_ids % devices * cap, -(2 * rows))]
    ppermute x2 -> x0, waiting for transfers between devices: 2.44 us -> none  [cross(): return lax.ppermute(value, BOTH, pairs)]
    select_n x4, other arithmetic: 2.32 us -> 0.15 us  [swap(): jnp.where(first, bwd, fwd)]
    all_to_all x1, starting transfers between devices: 6.81 us -> 5 us  [on_device(): arrived = lax.all_to_all(packed, 'seq', 0, 0, tiled=True)]
  transfers between devices with their start and end apart: 32 -> 30, of which waited for: 20 -> 20; matrix products, arithmetic and copies ran while one was open for 5% -> 0% of each run, Pallas kernels for 0% -> 0%
where the time goes in v5:
time: 152 us
  waiting for transfers between devices  81.4 us (54%)
  starting transfers between devices  49.8 us (33%)
  Pallas kernels  16.5 us (11%)
  local copies, waits for them, and re-layouts  2.51 us (2%)
    ppermute x17, waiting for transfers between devices, cycle(): return lax.ppermute(value, BOTH, pairs)  46.6 us
    ppermute x17, starting transfers between devices, cycle(): return lax.ppermute(value, BOTH, pairs)  27.6 us
    all_to_all x1, waiting for transfers between devices, on_device(): arrived = lax.all_to_all(packed, 'seq', 0, 0, tiled=True)  27.4 us
    ppermute x12, starting transfers between devices, flip(): return lax.ppermute(value, 'seq', [(i, i ^ bits) for i in range(devices)])  17.2 us
    pallas_call x1, Pallas kernels, on_device(): call(product_cycle, jax.ShapeDtypeStruct((devices, 4, cap, half), BF16),...  11.8 us
    ppermute x12, waiting for transfers between devices, flip(): return lax.ppermute(value, 'seq', [(i, i ^ bits) for i in range(devices)])  7.4 us
    all_to_all x1, starting transfers between devices, on_device(): arrived = lax.all_to_all(packed, 'seq', 0, 0, tiled=True)  5 us
  transfers between devices with their start and end apart: 30, of which 20 were waited for; matrix products, arithmetic and copies ran while one was open for 0% of the time, Pallas kernels for 0%

profile of v5, /device:TPU:0, one launch (start us, length us, event | category | flops | bytes accessed | tf_op | source)
XLA Modules:
  0.0 151.9 jit_solution(11780263662899936065)
XLA Ops:
  2.9 3.1 %collective-permute-start.1 = (bf16[224,640]{1,0:T(8,128)(2,1)}, bf16[224,640]{1,0:T(8,128)(2,1)S(1)}, u32[]{:S(2)}, u32[]{:S(2)}) collective-permute-start(bf16[224,640]{1,0:T(8,128)(2,1)} %get-tuple-element.22.refs_4_), channel_id=1, source_target_pairs={{0,4},{1,5},{2,6},{3,7},{4,8},{5,9},{6,10},{7,11},{8,12},{9,13},{1... | collective-permute-start | bytes 860168 | tf_op jit(solution)/shard_map/ppermute | solution.py:30
  7.6 4.7 %collective-permute-done.1.refs_6_ = bf16[224,640]{1,0:T(8,128)(2,1)S(1)} collective-permute-done((bf16[224,640]{1,0:T(8,128)(2,1)}, bf16[224,640]{1,0:T(8,128)(2,1)S(1)}, u32[]{:S(2)}, u32[]{:S(2)}) %collective-permute-start.1) | collective-permute-done | bytes 286752 | tf_op jit(solution)/shard_map/ppermute | solution.py:30
  19.0 2.8 %collective-permute-start.6 = (bf16[224,640]{1,0:T(8,128)(2,1)S(1)}, bf16[224,640]{1,0:T(8,128)(2,1)S(1)}, u32[]{:S(2)}, u32[]{:S(2)}) collective-permute-start(bf16[224,640]{1,0:T(8,128)(2,1)S(1)} %collective-permute-done.1.refs_6_), channel_id=1, source_target_pairs={{0,4},{1,5},{2,6},{3,7},{4,8},{5,9},{6,10},{7,11},{8,12},{9,13},{1... | collective-permute-start | bytes 860168 | tf_op jit(solution)/shard_map/ppermute | solution.py:30
  21.7 3.9 %collective-permute-done.4.refs_16_ = bf16[224,640]{1,0:T(8,128)(2,1)S(1)} collective-permute-done((bf16[224,640]{1,0:T(8,128)(2,1)S(1)}, bf16[224,640]{1,0:T(8,128)(2,1)S(1)}, u32[]{:S(2)}, u32[]{:S(2)}) %collective-permute-start.4) | collective-permute-done | bytes 286752 | tf_op jit(solution)/shard_map/ppermute | solution.py:30
  25.7 5.8 %collective-permute-done.6.refs_7_ = bf16[224,640]{1,0:T(8,128)(2,1)S(1)} collective-permute-done((bf16[224,640]{1,0:T(8,128)(2,1)S(1)}, bf16[224,640]{1,0:T(8,128)(2,1)S(1)}, u32[]{:S(2)}, u32[]{:S(2)}) %collective-permute-start.6) | collective-permute-done | bytes 286752 | tf_op jit(solution)/shard_map/ppermute | solution.py:30
  31.5 2.5 %collective-permute-done.7.refs_10_ = bf16[224,640]{1,0:T(8,128)(2,1)S(1)} collective-permute-done((bf16[224,640]{1,0:T(8,128)(2,1)S(1)}, bf16[224,640]{1,0:T(8,128)(2,1)S(1)}, u32[]{:S(2)}, u32[]{:S(2)}) %collective-permute-start.7) | collective-permute-done | bytes 286752 | tf_op jit(solution)/shard_map/ppermute | solution.py:30
  33.9 3.0 %collective-permute-start.11 = (bf16[224,640]{1,0:T(8,128)(2,1)S(1)}, bf16[224,640]{1,0:T(8,128)(2,1)S(1)}, u32[]{:S(2)}, u32[]{:S(2)}) collective-permute-start(bf16[224,640]{1,0:T(8,128)(2,1)S(1)} %collective-permute-done.7.refs_10_), channel_id=1, source_target_pairs={{0,17},{1,16},{2,19},{3,18},{4,0},{5,1},{6,2},{7,3},{8,4},{9,5},{1... | collective-permute-start | bytes 860168 | tf_op jit(solution)/shard_map/ppermute | solution.py:30
  39.7 3.9 %collective-permute-done.11.refs_11_ = bf16[224,640]{1,0:T(8,128)(2,1)S(1)} collective-permute-done((bf16[224,640]{1,0:T(8,128)(2,1)S(1)}, bf16[224,640]{1,0:T(8,128)(2,1)S(1)}, u32[]{:S(2)}, u32[]{:S(2)}) %collective-permute-start.11) | collective-permute-done | bytes 286752 | tf_op jit(solution)/shard_map/ppermute | solution.py:30
  45.3 2.3 %collective-permute-done.12.refs_8_ = bf16[224,640]{1,0:T(8,128)(2,1)S(1)} collective-permute-done((bf16[224,640]{1,0:T(8,128)(2,1)S(1)}, bf16[224,640]{1,0:T(8,128)(2,1)S(1)}, u32[]{:S(2)}, u32[]{:S(2)}) %collective-permute-start.12) | collective-permute-done | bytes 286752 | tf_op jit(solution)/shard_map/ppermute | solution.py:30
  49.7 4.1 %collective-permute-done.8.refs_17_ = bf16[224,640]{1,0:T(8,128)(2,1)S(1)} collective-permute-done((bf16[224,640]{1,0:T(8,128)(2,1)S(1)}, bf16[224,640]{1,0:T(8,128)(2,1)S(1)}, u32[]{:S(2)}, u32[]{:S(2)}) %collective-permute-start.8) | collective-permute-done | bytes 286752 | tf_op jit(solution)/shard_map/ppermute | solution.py:30
  53.8 3.5 %collective-permute-done.9.refs_20_ = bf16[224,640]{1,0:T(8,128)(2,1)S(1)} collective-permute-done((bf16[224,640]{1,0:T(8,128)(2,1)S(1)}, bf16[224,640]{1,0:T(8,128)(2,1)S(1)}, u32[]{:S(2)}, u32[]{:S(2)}) %collective-permute-start.9) | collective-permute-done | bytes 286752 | tf_op jit(solution)/shard_map/ppermute | solution.py:30
  57.3 3.6 %collective-permute-done.13.refs_13_ = bf16[224,640]{1,0:T(8,128)(2,1)S(1)} collective-permute-done((bf16[224,640]{1,0:T(8,128)(2,1)S(1)}, bf16[224,640]{1,0:T(8,128)(2,1)S(1)}, u32[]{:S(2)}, u32[]{:S(2)}) %collective-permute-start.13) | collective-permute-done | bytes 286752 | tf_op jit(solution)/shard_map/ppermute | solution.py:30
  62.2 4.7 %collective-permute-start.17 = (bf16[224,640]{1,0:T(8,128)(2,1)S(1)}, bf16[224,640]{1,0:T(8,128)(2,1)S(1)}, u32[]{:S(2)}, u32[]{:S(2)}) collective-permute-start(bf16[224,640]{1,0:T(8,128)(2,1)S(1)} %collective-permute-done.9.refs_20_), channel_id=1, source_target_pairs={{0,17},{1,16},{2,19},{3,18},{4,0},{5,1},{6,2},{7,3},{8,4},{9,5},{1... | collective-permute-start | bytes 860168 | tf_op jit(solution)/shard_map/ppermute | solution.py:30
  67.6 4.0 %collective-permute-done.16.refs_18_ = bf16[224,640]{1,0:T(8,128)(2,1)S(1)} collective-permute-done((bf16[224,640]{1,0:T(8,128)(2,1)S(1)}, bf16[224,640]{1,0:T(8,128)(2,1)S(1)}, u32[]{:S(2)}, u32[]{:S(2)}) %collective-permute-start.16) | collective-permute-done | bytes 286752 | tf_op jit(solution)/shard_map/ppermute | solution.py:30
  71.6 2.4 %collective-permute-done.17.refs_21_ = bf16[224,640]{1,0:T(8,128)(2,1)S(1)} collective-permute-done((bf16[224,640]{1,0:T(8,128)(2,1)S(1)}, bf16[224,640]{1,0:T(8,128)(2,1)S(1)}, u32[]{:S(2)}, u32[]{:S(2)}) %collective-permute-start.17) | collective-permute-done | bytes 286752 | tf_op jit(solution)/shard_map/ppermute | solution.py:30
  74.6 4.0 %collective-permute-start.22 = (bf16[224,640]{1,0:T(8,128)(2,1)S(1)}, bf16[224,640]{1,0:T(8,128)(2,1)S(1)}, u32[]{:S(2)}, u32[]{:S(2)}) collective-permute-start(bf16[224,640]{1,0:T(8,128)(2,1)S(1)} %broadcast_select_fusion), channel_id=1, source_target_pairs={{0,17},{1,16},{2,19},{3,18},{12,29},{13,28},{14,31},{15,30},{29,12... | collective-permute-start | bytes 860168 | tf_op jit(solution)/shard_map/ppermute | solution.py:30
  81.7 3.7 %collective-permute-done.22.refs_23_ = bf16[224,640]{1,0:T(8,128)(2,1)S(1)} collective-permute-done((bf16[224,640]{1,0:T(8,128)(2,1)S(1)}, bf16[224,640]{1,0:T(8,128)(2,1)S(1)}, u32[]{:S(2)}, u32[]{:S(2)}) %collective-permute-start.22) | collective-permute-done | bytes 286752 | tf_op jit(solution)/shard_map/ppermute | solution.py:30
  88.0 11.8 %shard_map.104 = bf16[16,4,16,640]{3,2,1,0:T(8,128)(2,1)} custom-call(s32[1,256]{1,0:T(1,128)} %bitcast.12, s32[1,256]{1,0:T(1,128)} %copy-done.26, s32[1,256]{1,0:T(1,128)} %copy-done.25, s32[1,256]{1,0:T(1,128)} %copy-done.27, bf16[224,640]{1,0:T(8,128)(2,1)} %get-tuple-element.22.refs_4_, bf16[224,640]{1,0:T(8,128)(2,1)} %copy-done.21, ...), custom_call_target="tpu_custom_call" | custom-call | tf_op jit(solution)/shard_map/pallas_call | solution.py:301
  99.8 5.0 %all-to-all-start = ((bf16[16,64,640]{2,1,0:T(8,128)(2,1)}), bf16[16,64,640]{2,1,0:T(8,128)(2,1)S(1)}, u32[]{:S(2)}, u32[]{:S(2)}) async-start(bf16[16,64,640]{2,1,0:T(8,128)(2,1)} %bitcast.6), calls=%async_computation | async-start | bytes 2621440 | tf_op jit(solution)/shard_map/all_to_all | solution.py:336
  104.9 27.4 %all-to-all-done = bf16[16,64,640]{2,1,0:T(8,128)(2,1)S(1)} async-done(((bf16[16,64,640]{2,1,0:T(8,128)(2,1)}), bf16[16,64,640]{2,1,0:T(8,128)(2,1)S(1)}, u32[]{:S(2)}, u32[]{:S(2)}) %all-to-all-start) | async-done | bytes 1310752 | tf_op jit(solution)/shard_map/all_to_all | solution.py:336
  132.3 2.5 %shard_map.105 = (bf16[256,1280]{1,0:T(8,128)(2,1)}, bf16[256,1280]{1,0:T(8,128)(2,1)}, f32[2,1280]{1,0:T(2,128)S(1)}) custom-call(bf16[4,2,2,4,16,640]{5,4,3,2,1,0:T(8,128)(2,1)S(1)} %bitcast.5, bf16[256,1280]{1,0:T(8,128)(2,1)S(1)} %copy-done, bf16[256,1280]{1,0:T(8,128)(2,1)S(1)} %copy-done.1, f32[1,1280]{1,0:T(1,128)S(1)} %broadcast_in_dim.6.a_gain, ...), custom_call_target="tpu_custom_call" | custom-call | tf_op jit(solution)/shard_map/pallas_call | solution.py:341
  136.3 2.3 %collective-permute-start.26 = (f32[2,1280]{1,0:T(2,128)S(1)}, f32[2,1280]{1,0:T(2,128)S(1)}, u32[]{:S(2)}, u32[]{:S(2)}) collective-permute-start(f32[2,1280]{1,0:T(2,128)S(1)} %add.25), channel_id=1, source_target_pairs={{0,2},{1,3},{2,0},{3,1},{4,6},{5,7},{6,4},{7,5},{8,10},{9,11},{10,... | collective-permute-start | bytes 30728 | tf_op jit(solution)/shard_map/ppermute | solution.py:20
  140.3 3.8 %collective-permute-start.27 = (f32[2,1280]{1,0:T(2,128)S(1)}, f32[2,1280]{1,0:T(2,128)S(1)}, u32[]{:S(2)}, u32[]{:S(2)}) collective-permute-start(f32[2,1280]{1,0:T(2,128)S(1)} %add.26), channel_id=1, source_target_pairs={{0,4},{1,5},{2,6},{3,7},{4,0},{5,1},{6,2},{7,3},{8,12},{9,13},{10,... | collective-permute-start | bytes 30728 | tf_op jit(solution)/shard_map/ppermute | solution.py:20
  145.8 3.8 %collective-permute-start.28 = (f32[2,1280]{1,0:T(2,128)S(1)}, f32[2,1280]{1,0:T(2,128)S(1)}, u32[]{:S(2)}, u32[]{:S(2)}) collective-permute-start(f32[2,1280]{1,0:T(2,128)S(1)} %add.27), channel_id=1, source_target_pairs={{0,8},{1,9},{2,10},{3,11},{4,12},{5,13},{6,14},{7,15},{8,0},{9,1},... | collective-permute-start | bytes 30728 | tf_op jit(solution)/shard_map/ppermute | solution.py:20
  (107 shorter events, 32.2 us)
Async XLA Ops:
  2.9 9.5 %collective-permute-start.1 = (bf16[224,640]{1,0:T(8,128)(2,1)}, bf16[224,640]{1,0:T(8,128)(2,1)S(1)}, u32[]{:S(2)}, u32[]{:S(2)}) collective-permute-start(bf16[224,640]{1,0:T(8,128)(2,1)} %get-tuple-element.22.refs_4_), channel_id=1, source_target_pairs={{0,4},{1,5},{2,6},{3,7},{4,8},{5,9},{6,10},{7,11},{8,12},{9,13},{1... | collective-permute-start | bytes 860168 | tf_op jit(solution)/shard_map/ppermute | solution.py:30
  5.9 8.5 %collective-permute-start.2 = (bf16[224,640]{1,0:T(8,128)(2,1)}, bf16[224,640]{1,0:T(8,128)(2,1)S(1)}, u32[]{:S(2)}, u32[]{:S(2)}) collective-permute-start(bf16[224,640]{1,0:T(8,128)(2,1)} %get-tuple-element.22.refs_4_), channel_id=1, source_target_pairs={{0,17},{1,16},{2,19},{3,18},{4,0},{5,1},{6,2},{7,3},{8,4},{9,5},{1... | collective-permute-start | bytes 860168 | tf_op jit(solution)/shard_map/ppermute | solution.py:30
  5.9 9.1 %collective-permute-start = (bf16[224,640]{1,0:T(8,128)(2,1)}, bf16[224,640]{1,0:T(8,128)(2,1)S(1)}, u32[]{:S(2)}, u32[]{:S(2)}) collective-permute-start(bf16[224,640]{1,0:T(8,128)(2,1)} %get-tuple-element.21), channel_id=1, source_target_pairs={{0,2},{1,3},{2,0},{3,1},{4,6},{5,7},{6,4},{7,5},{8,10},{9,11},{10,... | collective-permute-start | bytes 860168 | tf_op jit(solution)/shard_map/ppermute | solution.py:20
  15.0 59.0 %collective-permute-start.3 = (bf16[256,3584]{1,0:T(8,128)(2,1)}, bf16[256,3584]{1,0:T(8,128)(2,1)}, u32[]{:S(2)}, u32[]{:S(2)}) collective-permute-start(bf16[256,3584]{1,0:T(8,128)(2,1)} %refs_24_.1), channel_id=1, source_target_pairs={{0,2},{1,3},{2,0},{3,1},{4,6},{5,7},{6,4},{7,5},{8,10},{9,11},{10,... | collective-permute-start | bytes 5505032 | tf_op jit(solution)/shard_map/ppermute | solution.py:20
  16.5 9.1 %collective-permute-start.4 = (bf16[224,640]{1,0:T(8,128)(2,1)S(1)}, bf16[224,640]{1,0:T(8,128)(2,1)S(1)}, u32[]{:S(2)}, u32[]{:S(2)}) collective-permute-start(bf16[224,640]{1,0:T(8,128)(2,1)S(1)} %collective-permute-done.refs_14_), channel_id=1, source_target_pairs={{0,4},{1,5},{2,6},{3,7},{4,8},{5,9},{6,10},{7,11},{8,12},{9,13},{1... | collective-permute-start | bytes 860168 | tf_op jit(solution)/shard_map/ppermute | solution.py:30
  17.7 8.0 %collective-permute-start.5 = (bf16[224,640]{1,0:T(8,128)(2,1)S(1)}, bf16[224,640]{1,0:T(8,128)(2,1)S(1)}, u32[]{:S(2)}, u32[]{:S(2)}) collective-permute-start(bf16[224,640]{1,0:T(8,128)(2,1)S(1)} %collective-permute-done.refs_14_), channel_id=1, source_target_pairs={{0,17},{1,16},{2,19},{3,18},{4,0},{5,1},{6,2},{7,3},{8,4},{9,5},{1... | collective-permute-start | bytes 860168 | tf_op jit(solution)/shard_map/ppermute | solution.py:30
  18.3 7.4 %collective-permute-start.10 = (bf16[224,640]{1,0:T(8,128)(2,1)S(1)}, bf16[224,640]{1,0:T(8,128)(2,1)S(1)}, u32[]{:S(2)}, u32[]{:S(2)}) collective-permute-start(bf16[224,640]{1,0:T(8,128)(2,1)S(1)} %broadcast_select_fusion.3), channel_id=1, source_target_pairs={{4,21},{5,20},{6,23},{7,22},{8,25},{9,24},{10,27},{11,26},{25,8},{... | collective-permute-start | bytes 860168 | tf_op jit(solution)/shard_map/ppermute | solution.py:30
  19.0 12.5 %collective-permute-start.6 = (bf16[224,640]{1,0:T(8,128)(2,1)S(1)}, bf16[224,640]{1,0:T(8,128)(2,1)S(1)}, u32[]{:S(2)}, u32[]{:S(2)}) collective-permute-start(bf16[224,640]{1,0:T(8,128)(2,1)S(1)} %collective-permute-done.1.refs_6_), channel_id=1, source_target_pairs={{0,4},{1,5},{2,6},{3,7},{4,8},{5,9},{6,10},{7,11},{8,12},{9,13},{1... | collective-permute-start | bytes 860168 | tf_op jit(solution)/shard_map/ppermute | solution.py:30
  25.7 8.3 %collective-permute-start.7 = (bf16[224,640]{1,0:T(8,128)(2,1)S(1)}, bf16[224,640]{1,0:T(8,128)(2,1)S(1)}, u32[]{:S(2)}, u32[]{:S(2)}) collective-permute-start(bf16[224,640]{1,0:T(8,128)(2,1)S(1)} %collective-permute-done.2.refs_9_), channel_id=1, source_target_pairs={{0,17},{1,16},{2,19},{3,18},{4,0},{5,1},{6,2},{7,3},{8,4},{9,5},{1... | collective-permute-start | bytes 860168 | tf_op jit(solution)/shard_map/ppermute | solution.py:30
  33.9 9.7 %collective-permute-start.11 = (bf16[224,640]{1,0:T(8,128)(2,1)S(1)}, bf16[224,640]{1,0:T(8,128)(2,1)S(1)}, u32[]{:S(2)}, u32[]{:S(2)}) collective-permute-start(bf16[224,640]{1,0:T(8,128)(2,1)S(1)} %collective-permute-done.7.refs_10_), channel_id=1, source_target_pairs={{0,17},{1,16},{2,19},{3,18},{4,0},{5,1},{6,2},{7,3},{8,4},{9,5},{1... | collective-permute-start | bytes 860168 | tf_op jit(solution)/shard_map/ppermute | solution.py:30
  36.9 10.7 %collective-permute-start.12 = (bf16[224,640]{1,0:T(8,128)(2,1)S(1)}, bf16[224,640]{1,0:T(8,128)(2,1)S(1)}, u32[]{:S(2)}, u32[]{:S(2)}) collective-permute-start(bf16[224,640]{1,0:T(8,128)(2,1)S(1)} %collective-permute-done.6.refs_7_), channel_id=1, source_target_pairs={{4,8},{5,9},{6,10},{7,11},{8,12},{9,13},{10,14},{11,15},{12,29},{1... | collective-permute-start | bytes 860168 | tf_op jit(solution)/shard_map/ppermute | solution.py:30
  38.2 9.5 %collective-permute-start.15 = (bf16[224,640]{1,0:T(8,128)(2,1)S(1)}, bf16[224,640]{1,0:T(8,128)(2,1)S(1)}, u32[]{:S(2)}, u32[]{:S(2)}) collective-permute-start(bf16[224,640]{1,0:T(8,128)(2,1)S(1)} %collective-permute-done.refs_14_), channel_id=1, source_target_pairs={{4,21},{5,20},{6,23},{7,22},{8,25},{9,24},{10,27},{11,26},{25,8},{... | collective-permute-start | bytes 860168 | tf_op jit(solution)/shard_map/ppermute | solution.py:30
  39.0 10.7 %collective-permute-start.14 = (bf16[224,640]{1,0:T(8,128)(2,1)S(1)}, bf16[224,640]{1,0:T(8,128)(2,1)S(1)}, u32[]{:S(2)}, u32[]{:S(2)}) collective-permute-start(bf16[224,640]{1,0:T(8,128)(2,1)S(1)} %broadcast_select_fusion.1), channel_id=1, source_target_pairs={{4,21},{5,20},{6,23},{7,22},{8,25},{9,24},{10,27},{11,26},{25,8},{... | collective-permute-start | bytes 860168 | tf_op jit(solution)/shard_map/ppermute | solution.py:30
  43.6 10.2 %collective-permute-start.8 = (bf16[224,640]{1,0:T(8,128)(2,1)S(1)}, bf16[224,640]{1,0:T(8,128)(2,1)S(1)}, u32[]{:S(2)}, u32[]{:S(2)}) collective-permute-start(bf16[224,640]{1,0:T(8,128)(2,1)S(1)} %collective-permute-done.4.refs_16_), channel_id=1, source_target_pairs={{0,4},{1,5},{2,6},{3,7},{4,8},{5,9},{6,10},{7,11},{8,12},{9,13},{1... | collective-permute-start | bytes 860168 | tf_op jit(solution)/shard_map/ppermute | solution.py:30
  47.6 9.6 %collective-permute-start.9 = (bf16[224,640]{1,0:T(8,128)(2,1)S(1)}, bf16[224,640]{1,0:T(8,128)(2,1)S(1)}, u32[]{:S(2)}, u32[]{:S(2)}) collective-permute-start(bf16[224,640]{1,0:T(8,128)(2,1)S(1)} %collective-permute-done.5.refs_19_), channel_id=1, source_target_pairs={{0,17},{1,16},{2,19},{3,18},{4,0},{5,1},{6,2},{7,3},{8,4},{9,5},{1... | collective-permute-start | bytes 860168 | tf_op jit(solution)/shard_map/ppermute | solution.py:30
  47.7 13.1 %collective-permute-start.13 = (bf16[224,640]{1,0:T(8,128)(2,1)S(1)}, bf16[224,640]{1,0:T(8,128)(2,1)S(1)}, u32[]{:S(2)}, u32[]{:S(2)}) collective-permute-start(bf16[224,640]{1,0:T(8,128)(2,1)S(1)} %broadcast_select_fusion.2), channel_id=1, source_target_pairs={{0,17},{1,16},{2,19},{3,18},{12,29},{13,28},{14,31},{15,30},{29,12... | collective-permute-start | bytes 860168 | tf_op jit(solution)/shard_map/ppermute | solution.py:30
  60.8 10.8 %collective-permute-start.16 = (bf16[224,640]{1,0:T(8,128)(2,1)S(1)}, bf16[224,640]{1,0:T(8,128)(2,1)S(1)}, u32[]{:S(2)}, u32[]{:S(2)}) collective-permute-start(bf16[224,640]{1,0:T(8,128)(2,1)S(1)} %collective-permute-done.8.refs_17_), channel_id=1, source_target_pairs={{4,8},{5,9},{6,10},{7,11},{8,12},{9,13},{10,14},{11,15},{12,29},{1... | collective-permute-start | bytes 860168 | tf_op jit(solution)/shard_map/ppermute | solution.py:30
  62.2 11.8 %collective-permute-start.17 = (bf16[224,640]{1,0:T(8,128)(2,1)S(1)}, bf16[224,640]{1,0:T(8,128)(2,1)S(1)}, u32[]{:S(2)}, u32[]{:S(2)}) collective-permute-start(bf16[224,640]{1,0:T(8,128)(2,1)S(1)} %collective-permute-done.9.refs_20_), channel_id=1, source_target_pairs={{0,17},{1,16},{2,19},{3,18},{4,0},{5,1},{6,2},{7,3},{8,4},{9,5},{1... | collective-permute-start | bytes 860168 | tf_op jit(solution)/shard_map/ppermute | solution.py:30
  66.9 18.6 %collective-permute-start.23 = (bf16[256,3584]{1,0:T(8,128)(2,1)S(1)}, bf16[256,3584]{1,0:T(8,128)(2,1)S(1)}, u32[]{:S(2)}, u32[]{:S(2)}) collective-permute-start(bf16[256,3584]{1,0:T(8,128)(2,1)S(1)} %copy-done.2), channel_id=1, source_target_pairs={{0,1},{1,0},{2,3},{3,2},{4,5},{5,4},{6,7},{7,6},{8,9},{9,8},{10,11... | collective-permute-start | bytes 5505032 | tf_op jit(solution)/shard_map/ppermute | solution.py:20
  74.0 13.9 %collective-permute-start.24 = (bf16[256,3584]{1,0:T(8,128)(2,1)}, bf16[256,3584]{1,0:T(8,128)(2,1)}, u32[]{:S(2)}, u32[]{:S(2)}) collective-permute-start(bf16[256,3584]{1,0:T(8,128)(2,1)} %collective-permute-done.3.refs_25_), channel_id=1, source_target_pairs={{0,1},{1,0},{2,3},{3,2},{4,5},{5,4},{6,7},{7,6},{8,9},{9,8},{10,11... | collective-permute-start | bytes 5505032 | tf_op jit(solution)/shard_map/ppermute | solution.py:20
  74.0 6.6 %collective-permute-start.21 = (bf16[224,640]{1,0:T(8,128)(2,1)S(1)}, bf16[224,640]{1,0:T(8,128)(2,1)S(1)}, u32[]{:S(2)}, u32[]{:S(2)}) collective-permute-start(bf16[224,640]{1,0:T(8,128)(2,1)S(1)} %copy-done.28), channel_id=1, source_target_pairs={{0,1},{1,0},{2,3},{3,2},{4,5},{5,4},{6,7},{7,6},{8,9},{9,8},{10,11... | collective-permute-start | bytes 860168 | tf_op jit(solution)/shard_map/ppermute | solution.py:20
  74.6 10.9 %collective-permute-start.22 = (bf16[224,640]{1,0:T(8,128)(2,1)S(1)}, bf16[224,640]{1,0:T(8,128)(2,1)S(1)}, u32[]{:S(2)}, u32[]{:S(2)}) collective-permute-start(bf16[224,640]{1,0:T(8,128)(2,1)S(1)} %broadcast_select_fusion), channel_id=1, source_target_pairs={{0,17},{1,16},{2,19},{3,18},{12,29},{13,28},{14,31},{15,30},{29,12... | collective-permute-start | bytes 860168 | tf_op jit(solution)/shard_map/ppermute | solution.py:30
  80.1 6.7 %collective-permute-start.18 = (s32[1,256]{1,0:T(1,128)}, s32[1,256]{1,0:T(1,128)S(1)}, u32[]{:S(2)}, u32[]{:S(2)}) collective-permute-start(s32[1,256]{1,0:T(1,128)} %bitcast.10), channel_id=1, source_target_pairs={{0,2},{1,3},{2,0},{3,1},{4,6},{5,7},{6,4},{7,5},{8,10},{9,11},{10,... | collective-permute-start | bytes 3080 | tf_op jit(solution)/shard_map/ppermute | solution.py:20
  99.8 32.4 %all-to-all-start = ((bf16[16,64,640]{2,1,0:T(8,128)(2,1)}), bf16[16,64,640]{2,1,0:T(8,128)(2,1)S(1)}, u32[]{:S(2)}, u32[]{:S(2)}) async-start(bf16[16,64,640]{2,1,0:T(8,128)(2,1)} %bitcast.6), calls=%async_computation | async-start | bytes 2621440 | tf_op jit(solution)/shard_map/all_to_all | solution.py:336
  (35 other events, 800.1 us)

commit v6 on v5

--- a/solution.py
+++ b/solution.py
@@ -11,7 +11,7 @@
 BF16 = jnp.bfloat16
 BOTH = ("groups", "seq")
 BIG = 24 * 1024 * 1024
-WHOLE = 60 * 1024 * 1024
+WHOLE = 125 * 512 * 1024
 VM = pl.BlockSpec(memory_space=pltpu.VMEM)
 ANY = pl.BlockSpec(memory_space=pl.ANY)
 
@@ -89,18 +89,10 @@
     return copies
 
 
-def second_line(line):
-    return jnp.where((line == 0) | (line == 2), 1, 2)
-
-
-def last_lines(line):
-    return jnp.where(line == 0, 2, 0), jnp.where(line == 3, 1, 3)
-
-
 def product_cycle(*refs):
     ids = refs[:4]
     parts, lhs = refs[4:24], refs[24:28]
-    out, buf, w, acc, sems = refs[28:]
+    out, buf, w, acc, named, sems = refs[28:]
     deep = parts[0].shape[0]
     rows = lhs[0].shape[0]
     devices, sources, cap, half = out.shape
@@ -108,63 +100,78 @@
     modality = lax.rem(core + group, 2)
     p = jnp.where(group == 0, line, 7 - line)
     ends = lax.rem(p, 4)
-    second = second_line(line)
-    third, fourth = last_lines(line)
-    copies = load_rows(lhs, (line, second, third, fourth), buf, sems)
-
-    def move(ref, q, slot, which, i):
+
+    def pick(values):
+        return jnp.where(ends == 0, values[0], jnp.where(ends == 1, values[1], jnp.where(ends == 2, values[2], values[3])))
+
+    lines = [line_of(lax.rem(p + pick(far), 8)) for far in ((0, 0, 0, 0), (1, 1, 7, 7), (2, 7, 6, 6), (3, 2, 1, 5))]
+    row_copies = load_rows(lhs, lines, buf, sems)
+
+    def move(ref, far, slot, chain, i):
+        q = lax.rem(p + far, 8)
+        which = lax.rem(x + chain, 2)
         start = pl.multiple_of(((slot * 2 + which) * 2 + lax.rem(q // 4 + modality, 2)) * deep, 16)
-        return pltpu.make_async_copy(ref, w.at[pl.ds(start, deep)], sems.at[i])
-
-    for j in range(2):
-        for c in copies[8 * j : 8 * j + 8]:
+        return pltpu.make_async_copy(ref, w.at[pl.ds(start, deep)], sems.at[4 * slot + 2 * chain + i])
+
+    def start(slot):
+        for c in row_copies[4 * slot : 4 * slot + 4]:
             c.start()
         for chain in range(2):
             own, mirror, f1, f2, f3, b1, b2, b3, inner, outer = parts[chain * 10 : chain * 10 + 10]
-            which = jnp.where(chain == 0, x, 1 - x)
+            behind = mirror if chain == 0 else f1
+            ahead = mirror if chain == 0 else b1
+            turn = 7 + 6 * p
             f1, f2, f3, b1, b2, b3 = (f1, 7), (f2, 6), (f3, 5), (b1, 1), (b2, 2), (b3, 3)
-            inner, outer = (inner, 4), (outer, 4)
-            if j == 0:
-                move(own, p, 0, which, 4 * chain).start()
+            inner, outer, own = (inner, 4), (outer, 4), (own, 0)
+            takes = (
+                ((own, (behind, turn)), (own, (mirror, turn)), (own, (mirror, turn)), (own, (ahead, turn))),
+                ((b1, f2), (b1, inner), (f1, inner), (f1, b2)),
+                ((b2, f3), (f1, f2), (f2, f3), (f2, b3)),
+                ((b3, outer), (b2, b3), (b1, b2), (f3, outer)),
+            )[slot]
             for case in range(4):
 
                 @pl.when(ends == case)
                 def _():
-                    if j == 0:
-                        ref = mirror if chain == 0 else (f1[0], mirror, mirror, b1[0])[case]
-                        move(ref, 7 - p, 0, which, 4 * chain + 1).start()
-                        takes = ((b1, f2), (b1, inner), (f1, inner), (f1, b2))[case]
-                        for i, (ref, step) in enumerate(takes):
-                            move(ref, lax.rem(p + step, 8), 1, which, 4 * chain + 2 + i).start()
-                    else:
-                        takes = ((b2, f3, b3, outer), (f1, f2, b2, b3), (f2, f3, b1, b2), (f2, f3, b3, outer))[case]
-                        for i, (ref, step) in enumerate(takes):
-                            q = lax.rem(p + step, 8)
-                            slot = jnp.where(line_of(q) == third, 2, 3)
-                            move(ref, q, slot, which, 8 + 4 * chain + i).start()
-
+                    for i, (ref, far) in enumerate(takes[case]):
+                        move(ref, far, slot, chain, i).start()
+
+    def wait(slot):
+        for c in row_copies[4 * slot : 4 * slot + 4]:
+            c.wait()
+        for i in range(4):
+            move(parts[0], 0, slot, i // 2, i % 2).wait()
+
+    id_copies = [pltpu.make_async_copy(ref, named.at[s], sems.at[32 + s]) for s, ref in enumerate(ids)]
+    for c in id_copies:
+        c.start()
+    start(0)
+    start(1)
     earlier = lax.broadcasted_iota(jnp.int32, (rows, rows), 0) < lax.broadcasted_iota(jnp.int32, (rows, rows), 1)
     earlier = earlier.astype(F32).astype(BF16)
     kinds = lax.broadcasted_iota(jnp.int32, (devices, rows), 0) + modality * devices
     slots = lax.broadcasted_iota(jnp.int32, (devices * cap, rows), 0)
     picks = []
-    for id_ref in ids:
-        named_by = id_ref[...]
-        named = (kinds == named_by).astype(F32)
-        before = jnp.dot(named.astype(BF16), earlier, preferred_element_type=F32)
-        count = jnp.sum(named * before, axis=0, keepdims=True).astype(jnp.int32)
+    for c in id_copies:
+        c.wait()
+    for s in range(4):
+        named_by = named[s]
+        hit = (kinds == named_by).astype(F32)
+        before = jnp.dot(hit.astype(BF16), earlier, preferred_element_type=F32)
+        count = jnp.sum(hit * before, axis=0, keepdims=True).astype(jnp.int32)
         slot = (named_by - modality * devices) * cap + count
         picks.append((slots == slot).astype(F32).astype(BF16))
     low = x * 2 + core
     source = (low, (1 - x) * 2 + core, x * 2 + 1 - core, (1 - x) * 2 + 1 - core)
-    for j in range(2):
-        for c in copies[8 * j : 8 * j + 8]:
-            c.wait()
-        for i in range(8):
-            move(parts[0], p, 0, x, 8 * j + i).wait()
-        span = slice(j * 8 * deep, (j + 1) * 8 * deep)
-        if j == 0:
-            acc[...] = jnp.dot(buf[:, span], w[span, :], preferred_element_type=F32)
+    wait(0)
+    wait(1)
+    start(2)
+    start(3)
+    span = slice(0, 8 * deep)
+    acc[...] = jnp.dot(buf[:, span], w[span, :], preferred_element_type=F32)
+    wait(2)
+    wait(3)
+    span = slice(8 * deep, 16 * deep)
     for s in range(4):
         at = slice(s * rows, (s + 1) * rows)
         up = acc[at, :] + jnp.dot(buf[at, span], w[span, :], preferred_element_type=F32)
@@ -188,50 +195,51 @@
     out[...] = acc.astype(BF16)
 
 
-def norms(recv, a_states, v_states, a_gain, v_gain, a_out, v_out, gains):
-    group = lax.axis_index("groups")
+def statistics(a_states, v_states, a_mean, a_scale, v_scale):
+    inv = 1.0 / a_states.shape[1]
+    h = a_states[...].astype(F32)
+    mean = jnp.sum(h, axis=1, keepdims=True) * inv
+    centred = h - mean
+    a_mean[...] = mean
+    a_scale[...] = lax.rsqrt(jnp.sum(centred * centred, axis=1, keepdims=True) * inv + 1e-5)
+    g = v_states[...].astype(F32)
+    v_scale[...] = lax.rsqrt(jnp.sum(g * g, axis=1, keepdims=True) * inv + 1e-6)
+
+
+def upstream(recv, h, m, rows):
+    column = lax.rem(m + lax.axis_index("groups"), 2)
+    return recv[:, h, column].reshape(rows, recv.shape[-1]).astype(F32)
+
+
+def gain_sums(recv, a_states, v_states, a_mean, a_scale, v_scale, gains):
+    rows, width = a_states.shape
+    half = width // 2
+    sides = ((a_states, a_mean[...], a_scale), (v_states, 0.0, v_scale))
+    for m, (states, mean, scale) in enumerate(sides):
+        for h in range(2):
+            cols = slice(h * half, (h + 1) * half)
+            n = (states[:, cols].astype(F32) - mean) * scale[...]
+            gains[m : m + 1, cols] = jnp.sum(upstream(recv, h, m, rows) * n, axis=0, keepdims=True)
+
+
+def norms(recv, a_states, v_states, a_mean, a_scale, v_scale, a_gain, v_gain, a_out, v_out):
     rows, width = a_states.shape
     half = width // 2
     inv = 1.0 / width
-
-    def upstream(h, m):
-        return recv[:, h, lax.rem(m + group, 2)].reshape(rows, half).astype(F32)
-
-    def cols(h):
-        return slice(h * half, (h + 1) * half)
-
-    h = a_states[...].astype(F32)
-    mu = jnp.sum(h, axis=1, keepdims=True) * inv
-    centred = h - mu
-    scale = lax.rsqrt(jnp.sum(centred * centred, axis=1, keepdims=True) * inv + 1e-5)
-    normed = centred * scale
-    ps, pn, parts = 0.0, 0.0, []
-    for k in range(2):
-        u = upstream(k, 0)
-        n = normed[:, cols(k)]
-        p = u * a_gain[:, cols(k)]
-        ps = ps + jnp.sum(p, axis=1, keepdims=True)
-        pn = pn + jnp.sum(p * n, axis=1, keepdims=True)
-        gains[0:1, cols(k)] = jnp.sum(u * n, axis=0, keepdims=True)
-        parts.append((p, n))
-    for k in range(2):
-        p, n = parts[k]
-        a_out[:, cols(k)] = (scale * (p - ps * inv - n * (pn * inv))).astype(BF16)
-
-    h = v_states[...].astype(F32)
-    scale = lax.rsqrt(jnp.sum(h * h, axis=1, keepdims=True) * inv + 1e-6)
-    normed = h * scale
-    pn, parts = 0.0, []
-    for k in range(2):
-        u = upstream(k, 1)
-        n = normed[:, cols(k)]
-        p = u * v_gain[:, cols(k)]
-        pn = pn + jnp.sum(p * n, axis=1, keepdims=True)
-        gains[1:2, cols(k)] = jnp.sum(u * n, axis=0, keepdims=True)
-        parts.append((p, n))
-    for k in range(2):
-        p, n = parts[k]
-        v_out[:, cols(k)] = (scale * (p - n * (pn * inv))).astype(BF16)
+    sides = ((a_states, a_mean[...], a_scale, a_gain, a_out), (v_states, 0.0, v_scale, v_gain, v_out))
+    for m, (states, mean, scale, gain, out) in enumerate(sides):
+        ps, pn, parts = 0.0, 0.0, []
+        for h in range(2):
+            cols = slice(h * half, (h + 1) * half)
+            n = (states[:, cols].astype(F32) - mean) * scale[...]
+            p = upstream(recv, h, m, rows) * gain[:, cols]
+            ps = ps + jnp.sum(p, axis=1, keepdims=True)
+            pn = pn + jnp.sum(p * n, axis=1, keepdims=True)
+            parts.append((p, n, cols))
+        for p, n, cols in parts:
+            if m == 0:
+                p = p - ps * inv
+            out[:, cols] = (scale[...] * (p - n * (pn * inv))).astype(BF16)
 
 
 def call(body, outs, specs, scratch=(), out_spec=VM, limit=BIG):
@@ -301,12 +309,13 @@
         packed = call(
             product_cycle,
             jax.ShapeDtypeStruct((devices, 4, cap, half), BF16),
-            [VM] * 4 + [ANY] * 24,
+            [ANY] * 28,
             [
                 pltpu.VMEM((4 * rows, width), BF16),
                 pltpu.VMEM((width, half), BF16),
                 pltpu.VMEM((4 * rows, half), F32),
-                pltpu.SemaphoreType.DMA((32,)),
+                pltpu.VMEM((4, 1, rows), jnp.int32),
+                pltpu.SemaphoreType.DMA((36,)),
             ],
             limit=WHOLE,
         )(ids, i_pair, i_core, i_both, *chain1, *chain2, grad_rows, r_pair, r_core, r_both)
@@ -338,15 +347,14 @@
     if cap % 16 != 0:
         arrived = arrived.transpose(1, 2, 0, 3, 4, 5).reshape(1, 2, 2, 1, rows, half)
 
-    audio_grad, vision_grad, gains = call(
-        norms,
-        (
-            jax.ShapeDtypeStruct((rows, enc), BF16),
-            jax.ShapeDtypeStruct((rows, enc), BF16),
-            jax.ShapeDtypeStruct((2, enc), F32),
-        ),
-        [VM] * 5,
-    )(arrived, audio_states, vision_states, audio_gain[None, :], vision_gain[None, :])
+    thin = jax.ShapeDtypeStruct((rows, 1), F32)
+    states = (audio_states, vision_states)
+    states += tuple(call(statistics, (thin,) * 3, [VM] * 2)(*states))
+    gains = call(gain_sums, jax.ShapeDtypeStruct((2, enc), F32), [VM] * 6)(arrived, *states)
+    grad = jax.ShapeDtypeStruct((rows, enc), BF16)
+    audio_grad, vision_grad = call(norms, (grad, grad), [VM] * 8)(
+        arrived, *states, audio_gain[None, :], vision_gain[None, :]
+    )
     bit = 1
     while bit < devices:
         gains = gains + flip(gains, bit, devices)

time: 152 us -> 150 us (0.987)
  waiting for transfers between devices: 81.4 us -> 79.2 us
    ppermute x12, waiting for transfers between devices: 7.4 us -> 5.54 us  [flip(): return lax.ppermute(value, 'seq', [(i, i ^ bits) for i in range(devices)])]
    pallas_call x1 -> x3, Pallas kernels: 2.48 us -> 3.06 us  [the longest x1 1.99 us: on_device(): call(norms, (grad, grad), [VM] * 8)]
  transfers between devices with their start and end apart: 30 -> 30, of which waited for: 20 -> 19; matrix products, arithmetic and copies ran while one was open for 0% -> 0% of each run, Pallas kernels for 0% -> 2%
where the time goes in v6:
time: 150 us; the launch traced here: 149 us
  waiting for transfers between devices  79.2 us (53%)
  starting transfers between devices  50 us (33%)
  Pallas kernels  16.2 us (11%)
  local copies, waits for them, and re-layouts  2 us (1%)
    ppermute x17, waiting for transfers between devices, cycle(): return lax.ppermute(value, BOTH, pairs)  46.8 us
    ppermute x17, starting transfers between devices, cycle(): return lax.ppermute(value, BOTH, pairs)  27.7 us
    all_to_all x1, waiting for transfers between devices, on_device(): arrived = lax.all_to_all(packed, 'seq', 0, 0, tiled=True)  26.9 us
    ppermute x12, starting transfers between devices, flip(): return lax.ppermute(value, 'seq', [(i, i ^ bits) for i in range(devices)])  17.3 us
    pallas_call x1, Pallas kernels, on_device(): call(product_cycle, jax.ShapeDtypeStruct((devices, 4, cap, half), BF16),...  11.1 us
    ppermute x12, waiting for transfers between devices, flip(): return lax.ppermute(value, 'seq', [(i, i ^ bits) for i in range(devices)])  5.54 us
    all_to_all x1, starting transfers between devices, on_device(): arrived = lax.all_to_all(packed, 'seq', 0, 0, tiled=True)  5.06 us
  transfers between devices with their start and end apart: 30, of which 19 were waited for; matrix products, arithmetic and copies ran while one was open for 0% of the time, Pallas kernels for 2%

profile of v6, /device:TPU:0, one launch (start us, length us, event | category | flops | bytes accessed | tf_op | source)
XLA Modules:
  0.0 149.3 jit_solution(11498535806215967294)
XLA Ops:
  2.7 3.1 %collective-permute-start.1 = (bf16[224,640]{1,0:T(8,128)(2,1)}, bf16[224,640]{1,0:T(8,128)(2,1)S(1)}, u32[]{:S(2)}, u32[]{:S(2)}) collective-permute-start(bf16[224,640]{1,0:T(8,128)(2,1)} %get-tuple-element.24.refs_4_), channel_id=1, source_target_pairs={{0,4},{1,5},{2,6},{3,7},{4,8},{5,9},{6,10},{7,11},{8,12},{9,13},{1... | collective-permute-start | bytes 860168 | tf_op jit(solution)/shard_map/ppermute | solution.py:30
  7.5 4.7 %collective-permute-done.1.refs_6_ = bf16[224,640]{1,0:T(8,128)(2,1)S(1)} collective-permute-done((bf16[224,640]{1,0:T(8,128)(2,1)}, bf16[224,640]{1,0:T(8,128)(2,1)S(1)}, u32[]{:S(2)}, u32[]{:S(2)}) %collective-permute-start.1) | collective-permute-done | bytes 286752 | tf_op jit(solution)/shard_map/ppermute | solution.py:30
  12.2 2.1 %collective-permute-done.2.refs_9_ = bf16[224,640]{1,0:T(8,128)(2,1)S(1)} collective-permute-done((bf16[224,640]{1,0:T(8,128)(2,1)}, bf16[224,640]{1,0:T(8,128)(2,1)S(1)}, u32[]{:S(2)}, u32[]{:S(2)}) %collective-permute-start.2) | collective-permute-done | bytes 286752 | tf_op jit(solution)/shard_map/ppermute | solution.py:30
  18.9 2.8 %collective-permute-start.6 = (bf16[224,640]{1,0:T(8,128)(2,1)S(1)}, bf16[224,640]{1,0:T(8,128)(2,1)S(1)}, u32[]{:S(2)}, u32[]{:S(2)}) collective-permute-start(bf16[224,640]{1,0:T(8,128)(2,1)S(1)} %collective-permute-done.1.refs_6_), channel_id=1, source_target_pairs={{0,4},{1,5},{2,6},{3,7},{4,8},{5,9},{6,10},{7,11},{8,12},{9,13},{1... | collective-permute-start | bytes 860168 | tf_op jit(solution)/shard_map/ppermute | solution.py:30
  21.6 3.9 %collective-permute-done.4.refs_16_ = bf16[224,640]{1,0:T(8,128)(2,1)S(1)} collective-permute-done((bf16[224,640]{1,0:T(8,128)(2,1)S(1)}, bf16[224,640]{1,0:T(8,128)(2,1)S(1)}, u32[]{:S(2)}, u32[]{:S(2)}) %collective-permute-start.4) | collective-permute-done | bytes 286752 | tf_op jit(solution)/shard_map/ppermute | solution.py:30
  25.6 5.8 %collective-permute-done.6.refs_7_ = bf16[224,640]{1,0:T(8,128)(2,1)S(1)} collective-permute-done((bf16[224,640]{1,0:T(8,128)(2,1)S(1)}, bf16[224,640]{1,0:T(8,128)(2,1)S(1)}, u32[]{:S(2)}, u32[]{:S(2)}) %collective-permute-start.6) | collective-permute-done | bytes 286752 | tf_op jit(solution)/shard_map/ppermute | solution.py:30
  31.3 2.5 %collective-permute-done.7.refs_10_ = bf16[224,640]{1,0:T(8,128)(2,1)S(1)} collective-permute-done((bf16[224,640]{1,0:T(8,128)(2,1)S(1)}, bf16[224,640]{1,0:T(8,128)(2,1)S(1)}, u32[]{:S(2)}, u32[]{:S(2)}) %collective-permute-start.7) | collective-permute-done | bytes 286752 | tf_op jit(solution)/shard_map/ppermute | solution.py:30
  33.8 3.0 %collective-permute-start.11 = (bf16[224,640]{1,0:T(8,128)(2,1)S(1)}, bf16[224,640]{1,0:T(8,128)(2,1)S(1)}, u32[]{:S(2)}, u32[]{:S(2)}) collective-permute-start(bf16[224,640]{1,0:T(8,128)(2,1)S(1)} %collective-permute-done.7.refs_10_), channel_id=1, source_target_pairs={{0,17},{1,16},{2,19},{3,18},{4,0},{5,1},{6,2},{7,3},{8,4},{9,5},{1... | collective-permute-start | bytes 860168 | tf_op jit(solution)/shard_map/ppermute | solution.py:30
  39.5 3.9 %collective-permute-done.11.refs_11_ = bf16[224,640]{1,0:T(8,128)(2,1)S(1)} collective-permute-done((bf16[224,640]{1,0:T(8,128)(2,1)S(1)}, bf16[224,640]{1,0:T(8,128)(2,1)S(1)}, u32[]{:S(2)}, u32[]{:S(2)}) %collective-permute-start.11) | collective-permute-done | bytes 286752 | tf_op jit(solution)/shard_map/ppermute | solution.py:30
  45.2 2.3 %collective-permute-done.12.refs_8_ = bf16[224,640]{1,0:T(8,128)(2,1)S(1)} collective-permute-done((bf16[224,640]{1,0:T(8,128)(2,1)S(1)}, bf16[224,640]{1,0:T(8,128)(2,1)S(1)}, u32[]{:S(2)}, u32[]{:S(2)}) %collective-permute-start.12) | collective-permute-done | bytes 286752 | tf_op jit(solution)/shard_map/ppermute | solution.py:30
  49.5 4.1 %collective-permute-done.8.refs_17_ = bf16[224,640]{1,0:T(8,128)(2,1)S(1)} collective-permute-done((bf16[224,640]{1,0:T(8,128)(2,1)S(1)}, bf16[224,640]{1,0:T(8,128)(2,1)S(1)}, u32[]{:S(2)}, u32[]{:S(2)}) %collective-permute-start.8) | collective-permute-done | bytes 286752 | tf_op jit(solution)/shard_map/ppermute | solution.py:30
  53.7 3.5 %collective-permute-done.9.refs_20_ = bf16[224,640]{1,0:T(8,128)(2,1)S(1)} collective-permute-done((bf16[224,640]{1,0:T(8,128)(2,1)S(1)}, bf16[224,640]{1,0:T(8,128)(2,1)S(1)}, u32[]{:S(2)}, u32[]{:S(2)}) %collective-permute-start.9) | collective-permute-done | bytes 286752 | tf_op jit(solution)/shard_map/ppermute | solution.py:30
  57.1 3.6 %collective-permute-done.13.refs_13_ = bf16[224,640]{1,0:T(8,128)(2,1)} collective-permute-done((bf16[224,640]{1,0:T(8,128)(2,1)S(1)}, bf16[224,640]{1,0:T(8,128)(2,1)}, u32[]{:S(2)}, u32[]{:S(2)}) %collective-permute-start.13) | collective-permute-done | bytes 286752 | tf_op jit(solution)/shard_map/ppermute | solution.py:30
  62.0 4.8 %collective-permute-start.17 = (bf16[224,640]{1,0:T(8,128)(2,1)S(1)}, bf16[224,640]{1,0:T(8,128)(2,1)S(1)}, u32[]{:S(2)}, u32[]{:S(2)}) collective-permute-start(bf16[224,640]{1,0:T(8,128)(2,1)S(1)} %collective-permute-done.9.refs_20_), channel_id=1, source_target_pairs={{0,17},{1,16},{2,19},{3,18},{4,0},{5,1},{6,2},{7,3},{8,4},{9,5},{1... | collective-permute-start | bytes 860168 | tf_op jit(solution)/shard_map/ppermute | solution.py:30
  67.6 4.0 %collective-permute-done.16.refs_18_ = bf16[224,640]{1,0:T(8,128)(2,1)S(1)} collective-permute-done((bf16[224,640]{1,0:T(8,128)(2,1)S(1)}, bf16[224,640]{1,0:T(8,128)(2,1)S(1)}, u32[]{:S(2)}, u32[]{:S(2)}) %collective-permute-start.16) | collective-permute-done | bytes 286752 | tf_op jit(solution)/shard_map/ppermute | solution.py:30
  71.6 2.4 %collective-permute-done.17.refs_21_ = bf16[224,640]{1,0:T(8,128)(2,1)S(1)} collective-permute-done((bf16[224,640]{1,0:T(8,128)(2,1)S(1)}, bf16[224,640]{1,0:T(8,128)(2,1)S(1)}, u32[]{:S(2)}, u32[]{:S(2)}) %collective-permute-start.17) | collective-permute-done | bytes 286752 | tf_op jit(solution)/shard_map/ppermute | solution.py:30
  74.6 4.0 %collective-permute-start.22 = (bf16[224,640]{1,0:T(8,128)(2,1)S(1)}, bf16[224,640]{1,0:T(8,128)(2,1)S(1)}, u32[]{:S(2)}, u32[]{:S(2)}) collective-permute-start(bf16[224,640]{1,0:T(8,128)(2,1)S(1)} %broadcast_select_fusion), channel_id=1, source_target_pairs={{0,17},{1,16},{2,19},{3,18},{12,29},{13,28},{14,31},{15,30},{29,12... | collective-permute-start | bytes 860168 | tf_op jit(solution)/shard_map/ppermute | solution.py:30
  81.5 3.9 %collective-permute-done.22.refs_23_ = bf16[224,640]{1,0:T(8,128)(2,1)S(1)} collective-permute-done((bf16[224,640]{1,0:T(8,128)(2,1)S(1)}, bf16[224,640]{1,0:T(8,128)(2,1)S(1)}, u32[]{:S(2)}, u32[]{:S(2)}) %collective-permute-start.22) | collective-permute-done | bytes 286752 | tf_op jit(solution)/shard_map/ppermute | solution.py:30
  87.5 11.1 %shard_map.104 = bf16[16,4,16,640]{3,2,1,0:T(8,128)(2,1)} custom-call(s32[1,256]{1,0:T(1,128)} %bitcast.10, s32[1,256]{1,0:T(1,128)} %copy-done.26, s32[1,256]{1,0:T(1,128)} %copy-done.25, s32[1,256]{1,0:T(1,128)} %copy-done.27, bf16[224,640]{1,0:T(8,128)(2,1)} %get-tuple-element.24.refs_4_, bf16[224,640]{1,0:T(8,128)(2,1)} %copy-done.20, ...), custom_call_target="tpu_custom_call" | custom-call | tf_op jit(solution)/shard_map/pallas_call | solution.py:309
  98.6 5.1 %all-to-all-start = ((bf16[16,64,640]{2,1,0:T(8,128)(2,1)}), bf16[16,64,640]{2,1,0:T(8,128)(2,1)S(1)}, u32[]{:S(2)}, u32[]{:S(2)}) async-start(bf16[16,64,640]{2,1,0:T(8,128)(2,1)} %bitcast.7), calls=%async_computation | async-start | bytes 2621440 | tf_op jit(solution)/shard_map/all_to_all | solution.py:345
  104.2 26.9 %all-to-all-done = bf16[16,64,640]{2,1,0:T(8,128)(2,1)S(1)} async-done(((bf16[16,64,640]{2,1,0:T(8,128)(2,1)}), bf16[16,64,640]{2,1,0:T(8,128)(2,1)S(1)}, u32[]{:S(2)}, u32[]{:S(2)}) %all-to-all-start) | async-done | bytes 1310752 | tf_op jit(solution)/shard_map/all_to_all | solution.py:345
  133.3 2.3 %collective-permute-start.26 = (f32[2,1280]{1,0:T(2,128)S(1)}, f32[2,1280]{1,0:T(2,128)S(1)}, u32[]{:S(2)}, u32[]{:S(2)}) collective-permute-start(f32[2,1280]{1,0:T(2,128)S(1)} %add.25), channel_id=1, source_target_pairs={{0,2},{1,3},{2,0},{3,1},{4,6},{5,7},{6,4},{7,5},{8,10},{9,11},{10,... | collective-permute-start | bytes 30728 | tf_op jit(solution)/shard_map/ppermute | solution.py:20
  137.3 3.8 %collective-permute-start.27 = (f32[2,1280]{1,0:T(2,128)S(1)}, f32[2,1280]{1,0:T(2,128)S(1)}, u32[]{:S(2)}, u32[]{:S(2)}) collective-permute-start(f32[2,1280]{1,0:T(2,128)S(1)} %add.26), channel_id=1, source_target_pairs={{0,4},{1,5},{2,6},{3,7},{4,0},{5,1},{6,2},{7,3},{8,12},{9,13},{10,... | collective-permute-start | bytes 30728 | tf_op jit(solution)/shard_map/ppermute | solution.py:20
  142.8 3.8 %collective-permute-start.28 = (f32[2,1280]{1,0:T(2,128)S(1)}, f32[2,1280]{1,0:T(2,128)S(1)}, u32[]{:S(2)}, u32[]{:S(2)}) collective-permute-start(f32[2,1280]{1,0:T(2,128)S(1)} %add.27), channel_id=1, source_target_pairs={{0,8},{1,9},{2,10},{3,11},{4,12},{5,13},{6,14},{7,15},{8,0},{9,1},... | collective-permute-start | bytes 30728 | tf_op jit(solution)/shard_map/ppermute | solution.py:20
  (109 shorter events, 30.8 us)
Async XLA Ops:
  2.7 9.5 %collective-permute-start.1 = (bf16[224,640]{1,0:T(8,128)(2,1)}, bf16[224,640]{1,0:T(8,128)(2,1)S(1)}, u32[]{:S(2)}, u32[]{:S(2)}) collective-permute-start(bf16[224,640]{1,0:T(8,128)(2,1)} %get-tuple-element.24.refs_4_), channel_id=1, source_target_pairs={{0,4},{1,5},{2,6},{3,7},{4,8},{5,9},{6,10},{7,11},{8,12},{9,13},{1... | collective-permute-start | bytes 860168 | tf_op jit(solution)/shard_map/ppermute | solution.py:30
  5.8 8.5 %collective-permute-start.2 = (bf16[224,640]{1,0:T(8,128)(2,1)}, bf16[224,640]{1,0:T(8,128)(2,1)S(1)}, u32[]{:S(2)}, u32[]{:S(2)}) collective-permute-start(bf16[224,640]{1,0:T(8,128)(2,1)} %get-tuple-element.24.refs_4_), channel_id=1, source_target_pairs={{0,17},{1,16},{2,19},{3,18},{4,0},{5,1},{6,2},{7,3},{8,4},{9,5},{1... | collective-permute-start | bytes 860168 | tf_op jit(solution)/shard_map/ppermute | solution.py:30
  5.8 9.1 %collective-permute-start = (bf16[224,640]{1,0:T(8,128)(2,1)}, bf16[224,640]{1,0:T(8,128)(2,1)S(1)}, u32[]{:S(2)}, u32[]{:S(2)}) collective-permute-start(bf16[224,640]{1,0:T(8,128)(2,1)} %get-tuple-element.23), channel_id=1, source_target_pairs={{0,2},{1,3},{2,0},{3,1},{4,6},{5,7},{6,4},{7,5},{8,10},{9,11},{10,... | collective-permute-start | bytes 860168 | tf_op jit(solution)/shard_map/ppermute | solution.py:20
  14.9 59.1 %collective-permute-start.3 = (bf16[256,3584]{1,0:T(8,128)(2,1)}, bf16[256,3584]{1,0:T(8,128)(2,1)}, u32[]{:S(2)}, u32[]{:S(2)}) collective-permute-start(bf16[256,3584]{1,0:T(8,128)(2,1)} %refs_24_.1), channel_id=1, source_target_pairs={{0,2},{1,3},{2,0},{3,1},{4,6},{5,7},{6,4},{7,5},{8,10},{9,11},{10,... | collective-permute-start | bytes 5505032 | tf_op jit(solution)/shard_map/ppermute | solution.py:20
  16.4 9.1 %collective-permute-start.4 = (bf16[224,640]{1,0:T(8,128)(2,1)S(1)}, bf16[224,640]{1,0:T(8,128)(2,1)S(1)}, u32[]{:S(2)}, u32[]{:S(2)}) collective-permute-start(bf16[224,640]{1,0:T(8,128)(2,1)S(1)} %collective-permute-done.refs_14_), channel_id=1, source_target_pairs={{0,4},{1,5},{2,6},{3,7},{4,8},{5,9},{6,10},{7,11},{8,12},{9,13},{1... | collective-permute-start | bytes 860168 | tf_op jit(solution)/shard_map/ppermute | solution.py:30
  17.6 8.0 %collective-permute-start.5 = (bf16[224,640]{1,0:T(8,128)(2,1)S(1)}, bf16[224,640]{1,0:T(8,128)(2,1)S(1)}, u32[]{:S(2)}, u32[]{:S(2)}) collective-permute-start(bf16[224,640]{1,0:T(8,128)(2,1)S(1)} %collective-permute-done.refs_14_), channel_id=1, source_target_pairs={{0,17},{1,16},{2,19},{3,18},{4,0},{5,1},{6,2},{7,3},{8,4},{9,5},{1... | collective-permute-start | bytes 860168 | tf_op jit(solution)/shard_map/ppermute | solution.py:30
  18.2 7.4 %collective-permute-start.10 = (bf16[224,640]{1,0:T(8,128)(2,1)S(1)}, bf16[224,640]{1,0:T(8,128)(2,1)S(1)}, u32[]{:S(2)}, u32[]{:S(2)}) collective-permute-start(bf16[224,640]{1,0:T(8,128)(2,1)S(1)} %broadcast_select_fusion.3), channel_id=1, source_target_pairs={{4,21},{5,20},{6,23},{7,22},{8,25},{9,24},{10,27},{11,26},{25,8},{... | collective-permute-start | bytes 860168 | tf_op jit(solution)/shard_map/ppermute | solution.py:30
  18.9 12.5 %collective-permute-start.6 = (bf16[224,640]{1,0:T(8,128)(2,1)S(1)}, bf16[224,640]{1,0:T(8,128)(2,1)S(1)}, u32[]{:S(2)}, u32[]{:S(2)}) collective-permute-start(bf16[224,640]{1,0:T(8,128)(2,1)S(1)} %collective-permute-done.1.refs_6_), channel_id=1, source_target_pairs={{0,4},{1,5},{2,6},{3,7},{4,8},{5,9},{6,10},{7,11},{8,12},{9,13},{1... | collective-permute-start | bytes 860168 | tf_op jit(solution)/shard_map/ppermute | solution.py:30
  25.5 8.3 %collective-permute-start.7 = (bf16[224,640]{1,0:T(8,128)(2,1)S(1)}, bf16[224,640]{1,0:T(8,128)(2,1)S(1)}, u32[]{:S(2)}, u32[]{:S(2)}) collective-permute-start(bf16[224,640]{1,0:T(8,128)(2,1)S(1)} %collective-permute-done.2.refs_9_), channel_id=1, source_target_pairs={{0,17},{1,16},{2,19},{3,18},{4,0},{5,1},{6,2},{7,3},{8,4},{9,5},{1... | collective-permute-start | bytes 860168 | tf_op jit(solution)/shard_map/ppermute | solution.py:30
  33.8 9.7 %collective-permute-start.11 = (bf16[224,640]{1,0:T(8,128)(2,1)S(1)}, bf16[224,640]{1,0:T(8,128)(2,1)S(1)}, u32[]{:S(2)}, u32[]{:S(2)}) collective-permute-start(bf16[224,640]{1,0:T(8,128)(2,1)S(1)} %collective-permute-done.7.refs_10_), channel_id=1, source_target_pairs={{0,17},{1,16},{2,19},{3,18},{4,0},{5,1},{6,2},{7,3},{8,4},{9,5},{1... | collective-permute-start | bytes 860168 | tf_op jit(solution)/shard_map/ppermute | solution.py:30
  36.8 10.7 %collective-permute-start.12 = (bf16[224,640]{1,0:T(8,128)(2,1)S(1)}, bf16[224,640]{1,0:T(8,128)(2,1)S(1)}, u32[]{:S(2)}, u32[]{:S(2)}) collective-permute-start(bf16[224,640]{1,0:T(8,128)(2,1)S(1)} %collective-permute-done.6.refs_7_), channel_id=1, source_target_pairs={{4,8},{5,9},{6,10},{7,11},{8,12},{9,13},{10,14},{11,15},{12,29},{1... | collective-permute-start | bytes 860168 | tf_op jit(solution)/shard_map/ppermute | solution.py:30
  38.1 9.4 %collective-permute-start.15 = (bf16[224,640]{1,0:T(8,128)(2,1)}, bf16[224,640]{1,0:T(8,128)(2,1)S(1)}, u32[]{:S(2)}, u32[]{:S(2)}) collective-permute-start(bf16[224,640]{1,0:T(8,128)(2,1)} %copy-done.12), channel_id=1, source_target_pairs={{4,21},{5,20},{6,23},{7,22},{8,25},{9,24},{10,27},{11,26},{25,8},{... | collective-permute-start | bytes 860168 | tf_op jit(solution)/shard_map/ppermute | solution.py:30
  38.9 10.7 %collective-permute-start.14 = (bf16[224,640]{1,0:T(8,128)(2,1)S(1)}, bf16[224,640]{1,0:T(8,128)(2,1)S(1)}, u32[]{:S(2)}, u32[]{:S(2)}) collective-permute-start(bf16[224,640]{1,0:T(8,128)(2,1)S(1)} %broadcast_select_fusion.1), channel_id=1, source_target_pairs={{4,21},{5,20},{6,23},{7,22},{8,25},{9,24},{10,27},{11,26},{25,8},{... | collective-permute-start | bytes 860168 | tf_op jit(solution)/shard_map/ppermute | solution.py:30
  43.5 10.2 %collective-permute-start.8 = (bf16[224,640]{1,0:T(8,128)(2,1)S(1)}, bf16[224,640]{1,0:T(8,128)(2,1)S(1)}, u32[]{:S(2)}, u32[]{:S(2)}) collective-permute-start(bf16[224,640]{1,0:T(8,128)(2,1)S(1)} %collective-permute-done.4.refs_16_), channel_id=1, source_target_pairs={{0,4},{1,5},{2,6},{3,7},{4,8},{5,9},{6,10},{7,11},{8,12},{9,13},{1... | collective-permute-start | bytes 860168 | tf_op jit(solution)/shard_map/ppermute | solution.py:30
  47.5 9.6 %collective-permute-start.9 = (bf16[224,640]{1,0:T(8,128)(2,1)S(1)}, bf16[224,640]{1,0:T(8,128)(2,1)S(1)}, u32[]{:S(2)}, u32[]{:S(2)}) collective-permute-start(bf16[224,640]{1,0:T(8,128)(2,1)S(1)} %collective-permute-done.5.refs_19_), channel_id=1, source_target_pairs={{0,17},{1,16},{2,19},{3,18},{4,0},{5,1},{6,2},{7,3},{8,4},{9,5},{1... | collective-permute-start | bytes 860168 | tf_op jit(solution)/shard_map/ppermute | solution.py:30
  47.6 13.1 %collective-permute-start.13 = (bf16[224,640]{1,0:T(8,128)(2,1)S(1)}, bf16[224,640]{1,0:T(8,128)(2,1)}, u32[]{:S(2)}, u32[]{:S(2)}) collective-permute-start(bf16[224,640]{1,0:T(8,128)(2,1)S(1)} %broadcast_select_fusion.2), channel_id=1, source_target_pairs={{0,17},{1,16},{2,19},{3,18},{12,29},{13,28},{14,31},{15,30},{29,12... | collective-permute-start | bytes 860168 | tf_op jit(solution)/shard_map/ppermute | solution.py:30
  60.7 10.9 %collective-permute-start.16 = (bf16[224,640]{1,0:T(8,128)(2,1)S(1)}, bf16[224,640]{1,0:T(8,128)(2,1)S(1)}, u32[]{:S(2)}, u32[]{:S(2)}) collective-permute-start(bf16[224,640]{1,0:T(8,128)(2,1)S(1)} %collective-permute-done.8.refs_17_), channel_id=1, source_target_pairs={{4,8},{5,9},{6,10},{7,11},{8,12},{9,13},{10,14},{11,15},{12,29},{1... | collective-permute-start | bytes 860168 | tf_op jit(solution)/shard_map/ppermute | solution.py:30
  62.0 11.9 %collective-permute-start.17 = (bf16[224,640]{1,0:T(8,128)(2,1)S(1)}, bf16[224,640]{1,0:T(8,128)(2,1)S(1)}, u32[]{:S(2)}, u32[]{:S(2)}) collective-permute-start(bf16[224,640]{1,0:T(8,128)(2,1)S(1)} %collective-permute-done.9.refs_20_), channel_id=1, source_target_pairs={{0,17},{1,16},{2,19},{3,18},{4,0},{5,1},{6,2},{7,3},{8,4},{9,5},{1... | collective-permute-start | bytes 860168 | tf_op jit(solution)/shard_map/ppermute | solution.py:30
  66.9 18.6 %collective-permute-start.23 = (bf16[256,3584]{1,0:T(8,128)(2,1)S(1)}, bf16[256,3584]{1,0:T(8,128)(2,1)S(1)}, u32[]{:S(2)}, u32[]{:S(2)}) collective-permute-start(bf16[256,3584]{1,0:T(8,128)(2,1)S(1)} %copy-done.2), channel_id=1, source_target_pairs={{0,1},{1,0},{2,3},{3,2},{4,5},{5,4},{6,7},{7,6},{8,9},{9,8},{10,11... | collective-permute-start | bytes 5505032 | tf_op jit(solution)/shard_map/ppermute | solution.py:20
  74.0 12.9 %collective-permute-start.24 = (bf16[256,3584]{1,0:T(8,128)(2,1)}, bf16[256,3584]{1,0:T(8,128)(2,1)}, u32[]{:S(2)}, u32[]{:S(2)}) collective-permute-start(bf16[256,3584]{1,0:T(8,128)(2,1)} %collective-permute-done.3.refs_25_), channel_id=1, source_target_pairs={{0,1},{1,0},{2,3},{3,2},{4,5},{5,4},{6,7},{7,6},{8,9},{9,8},{10,11... | collective-permute-start | bytes 5505032 | tf_op jit(solution)/shard_map/ppermute | solution.py:20
  74.0 6.4 %collective-permute-start.21 = (bf16[224,640]{1,0:T(8,128)(2,1)S(1)}, bf16[224,640]{1,0:T(8,128)(2,1)S(1)}, u32[]{:S(2)}, u32[]{:S(2)}) collective-permute-start(bf16[224,640]{1,0:T(8,128)(2,1)S(1)} %copy-done.28), channel_id=1, source_target_pairs={{0,1},{1,0},{2,3},{3,2},{4,5},{5,4},{6,7},{7,6},{8,9},{9,8},{10,11... | collective-permute-start | bytes 860168 | tf_op jit(solution)/shard_map/ppermute | solution.py:20
  74.6 10.9 %collective-permute-start.22 = (bf16[224,640]{1,0:T(8,128)(2,1)S(1)}, bf16[224,640]{1,0:T(8,128)(2,1)S(1)}, u32[]{:S(2)}, u32[]{:S(2)}) collective-permute-start(bf16[224,640]{1,0:T(8,128)(2,1)S(1)} %broadcast_select_fusion), channel_id=1, source_target_pairs={{0,17},{1,16},{2,19},{3,18},{12,29},{13,28},{14,31},{15,30},{29,12... | collective-permute-start | bytes 860168 | tf_op jit(solution)/shard_map/ppermute | solution.py:30
  79.9 6.9 %collective-permute-start.18 = (s32[1,256]{1,0:T(1,128)S(1)}, s32[1,256]{1,0:T(1,128)S(1)}, u32[]{:S(2)}, u32[]{:S(2)}) collective-permute-start(s32[1,256]{1,0:T(1,128)S(1)} %bitcast.12), channel_id=1, source_target_pairs={{0,2},{1,3},{2,0},{3,1},{4,6},{5,7},{6,4},{7,5},{8,10},{9,11},{10,... | collective-permute-start | bytes 3080 | tf_op jit(solution)/shard_map/ppermute | solution.py:20
  98.6 32.5 %all-to-all-start = ((bf16[16,64,640]{2,1,0:T(8,128)(2,1)}), bf16[16,64,640]{2,1,0:T(8,128)(2,1)S(1)}, u32[]{:S(2)}, u32[]{:S(2)}) async-start(bf16[16,64,640]{2,1,0:T(8,128)(2,1)} %bitcast.7), calls=%async_computation | async-start | bytes 2621440 | tf_op jit(solution)/shard_map/all_to_all | solution.py:345
  (35 other events, 839.6 us)

commit v7 on v6

--- a/solution.py
+++ b/solution.py
@@ -53,21 +53,20 @@
     return lax.axis_index("groups"), me // 4, lax.rem(me // 2, 2), lax.rem(me, 2)
 
 
-def cut(a_ref, v_ref, keep, to_pair, to_core, sems):
+def cut(a_ref, v_ref, keep, to_pair, sems):
     group, _, pair, core = seat()
     half = keep.shape[1]
     near = pl.ds(pl.multiple_of(pair * half, 128), half)
     away = pl.ds(pl.multiple_of((1 - pair) * half, 128), half)
     for same in (True, False):
-        mine, other = (a_ref, v_ref) if same else (v_ref, a_ref)
+        mine = a_ref if same else v_ref
 
         @pl.when((core == group) == same)
         def _():
             pltpu.make_async_copy(mine.at[:, near], keep, sems.at[0]).start()
             pltpu.make_async_copy(mine.at[:, away], to_pair, sems.at[1]).start()
-            pltpu.make_async_copy(other.at[:, near], to_core, sems.at[2]).start()
-
-    for i, out in enumerate((keep, to_pair, to_core)):
+
+    for i, out in enumerate((keep, to_pair)):
         pltpu.make_async_copy(a_ref.at[:, near], out, sems.at[i]).wait()
 
 
@@ -91,9 +90,9 @@
 
 def product_cycle(*refs):
     ids = refs[:4]
-    parts, lhs = refs[4:24], refs[24:28]
-    out, buf, w, acc, named, sems = refs[28:]
-    deep = parts[0].shape[0]
+    parts, lhs = refs[4:15], refs[15:19]
+    out, buf, w, acc, named, sems = refs[19:]
+    deep = parts[0].shape[0] // 2
     rows = lhs[0].shape[0]
     devices, sources, cap, half = out.shape
     group, line, x, core = seat()
@@ -107,40 +106,45 @@
     lines = [line_of(lax.rem(p + pick(far), 8)) for far in ((0, 0, 0, 0), (1, 1, 7, 7), (2, 7, 6, 6), (3, 2, 1, 5))]
     row_copies = load_rows(lhs, lines, buf, sems)
 
-    def move(ref, far, slot, chain, i):
-        q = lax.rem(p + far, 8)
-        which = lax.rem(x + chain, 2)
-        start = pl.multiple_of(((slot * 2 + which) * 2 + lax.rem(q // 4 + modality, 2)) * deep, 16)
-        return pltpu.make_async_copy(ref, w.at[pl.ds(start, deep)], sems.at[4 * slot + 2 * chain + i])
+    def move(ref, far, slot, i):
+        core_of = lax.rem(lax.rem(p + far, 8) // 4 + modality, 2)
+        out = []
+        for part in range(2):
+            place = (slot * 2 + lax.rem(x + part, 2)) * 2 + core_of
+            to = w.at[pl.ds(pl.multiple_of(place * deep, 16), deep)]
+            src = ref[part] if isinstance(ref, tuple) else ref.at[pl.ds(part * deep, deep)]
+            out.append(pltpu.make_async_copy(src, to, sems.at[4 * slot + 2 * i + part]))
+        return out
 
     def start(slot):
         for c in row_copies[4 * slot : 4 * slot + 4]:
             c.start()
-        for chain in range(2):
-            own, mirror, f1, f2, f3, b1, b2, b3, inner, outer = parts[chain * 10 : chain * 10 + 10]
-            behind = mirror if chain == 0 else f1
-            ahead = mirror if chain == 0 else b1
-            turn = 7 + 6 * p
-            f1, f2, f3, b1, b2, b3 = (f1, 7), (f2, 6), (f3, 5), (b1, 1), (b2, 2), (b3, 3)
-            inner, outer, own = (inner, 4), (outer, 4), (own, 0)
-            takes = (
-                ((own, (behind, turn)), (own, (mirror, turn)), (own, (mirror, turn)), (own, (ahead, turn))),
-                ((b1, f2), (b1, inner), (f1, inner), (f1, b2)),
-                ((b2, f3), (f1, f2), (f2, f3), (f2, b3)),
-                ((b3, outer), (b2, b3), (b1, b2), (f3, outer)),
-            )[slot]
-            for case in range(4):
-
-                @pl.when(ends == case)
-                def _():
-                    for i, (ref, far) in enumerate(takes[case]):
-                        move(ref, far, slot, chain, i).start()
+        own, mirror, f1, f2, f3, b1, b2, b3, inner = parts[:9]
+        outer = (parts[9], parts[10])
+        turn = 7 + 6 * p
+        behind, ahead = (f1, turn), (b1, turn)
+        f1, f2, f3, b1, b2, b3 = (f1, 7), (f2, 6), (f3, 5), (b1, 1), (b2, 2), (b3, 3)
+        inner, outer, own, mirror = (inner, 4), (outer, 4), (own, 0), (mirror, turn)
+        takes = (
+            ((own, behind), (own, mirror), (own, mirror), (own, ahead)),
+            ((b1, f2), (b1, inner), (f1, inner), (f1, b2)),
+            ((b2, f3), (f1, f2), (f2, f3), (f2, b3)),
+            ((b3, outer), (b2, b3), (b1, b2), (f3, outer)),
+        )[slot]
+        for case in range(4):
+
+            @pl.when(ends == case)
+            def _():
+                for i, (ref, far) in enumerate(takes[case]):
+                    for c in move(ref, far, slot, i):
+                        c.start()
 
     def wait(slot):
         for c in row_copies[4 * slot : 4 * slot + 4]:
             c.wait()
-        for i in range(4):
-            move(parts[0], 0, slot, i // 2, i % 2).wait()
+        for i in range(2):
+            for c in move(parts[0], 0, slot, i):
+                c.wait()
 
     id_copies = [pltpu.make_async_copy(ref, named.at[s], sems.at[32 + s]) for s, ref in enumerate(ids)]
     for c in id_copies:
@@ -278,38 +282,33 @@
 
     if lines == 4:
         block = jax.ShapeDtypeStruct((k, half), BF16)
-        block1, to_pair, to_core = call(
-            cut, (block,) * 3, [ANY, ANY], [pltpu.SemaphoreType.DMA((3,))], VM, WHOLE
-        )(audio_proj.T, vision_proj.T)
+        keep, to_pair = call(cut, (block,) * 2, [ANY, ANY], [pltpu.SemaphoreType.DMA((2,))], VM, WHOLE)(
+            audio_proj.T, vision_proj.T
+        )
         from_pair = flip(to_pair, 2, devices)
+        whole = jnp.concatenate([keep, from_pair])
+        r_pair = flip(after(grad_rows, from_pair), 2, devices)
         p = jnp.where(group == 0, line, 7 - line)
         ends, mids = (0, 3, 4, 7), (1, 2, 5, 6)
-        f11, b11 = step(block1, block1, 1, devices)
-        block2 = after(from_pair, f11, b11)
-        r_pair = flip(after(grad_rows, block2), 2, devices)
-        r_core = flip(after(grad_rows, block2), 1, devices)
-        mirror1 = flip(after(to_core, block2), 1, devices)
-        i_core = flip(after(ids, block2), 1, devices)
-        inner1 = swap(f11, b11, p, mids, devices)
-        f12, b12 = step(f11, b11, 2, devices)
-        f21, b21 = step(block2, block2, 1, devices)
-        mirror2 = cycle(block2, [(a, 7 - a) for a in mids], devices)
-        f22, b22 = step(*after((f21, b21), f12, b12), 2, devices)
-        f13, b13 = step(*after((f12, b12), f21, b21, inner1), 3, devices)
-        inner2 = swap(f21, b21, p, mids, devices)
-        outer1 = swap(f13, b13, p, ends, devices)
-        f23, b23 = step(*after((f22, b22), outer1, inner2, mirror2), 3, devices)
-        outer2 = swap(f23, b23, p, ends, devices)
-        r_there = after(r_pair, f23, b23)
+        f1, b1 = step(whole, whole, 1, devices)
+        r_core = flip(after(grad_rows, f1, b1), 1, devices)
+        i_core = flip(after(ids, f1, b1), 1, devices)
+        mirror = cycle(whole, [(a, 7 - a) for a in mids], devices)
+        f2, b2 = step(f1, b1, 2, devices)
+        inner = swap(f1, b1, p, mids, devices)
+        f3, b3 = step(*after((f2, b2), inner, mirror), 3, devices)
+        opposite = jnp.where(p % 4 < 2, b3, f3)
+        over_y = cycle(opposite[:k], [(a, 7 - a) for a in ends], devices)
+        along_z = cycle(opposite[k:], [(1, 0), (2, 3), (5, 4), (6, 7)], devices)
+        r_there = after(r_pair, f3, b3)
         r_both = flip(r_there, 1, devices)
         late_ids = after(ids, r_there)
         i_pair, i_both = flip(late_ids, 2, devices), flip(late_ids, 3, devices)
-        chain1 = (block1, mirror1, f11, f12, f13, b11, b12, b13, inner1, outer1)
-        chain2 = (block2, mirror2, f21, f22, f23, b21, b22, b23, inner2, outer2)
+        chain = (whole, mirror, f1, f2, f3, b1, b2, b3, inner, over_y, along_z)
         packed = call(
             product_cycle,
             jax.ShapeDtypeStruct((devices, 4, cap, half), BF16),
-            [ANY] * 28,
+            [ANY] * 19,
             [
                 pltpu.VMEM((4 * rows, width), BF16),
                 pltpu.VMEM((width, half), BF16),
@@ -318,7 +317,7 @@
                 pltpu.SemaphoreType.DMA((36,)),
             ],
             limit=WHOLE,
-        )(ids, i_pair, i_core, i_both, *chain1, *chain2, grad_rows, r_pair, r_core, r_both)
+        )(ids, i_pair, i_core, i_both, *chain, grad_rows, r_pair, r_core, r_both)
     else:
         both = jnp.stack([audio_proj.T, vision_proj.T]).reshape(2, k, 2, half)
         plane = [both[modality, :, pair]]

time: 150 us -> 144 us (0.960)
  starting transfers between devices: 50 us -> 40.2 us
  waiting for transfers between devices: 79.2 us -> 84.2 us
    ppermute x17 -> x10, starting transfers between devices: 27.7 us -> 15 us  [cycle(): return lax.ppermute(value, BOTH, pairs)]
    ppermute x12 -> x11, waiting for transfers between devices: 5.54 us -> 15.5 us  [flip(): return lax.ppermute(value, 'seq', [(i, i ^ bits) for i in range(devices)])]
    ppermute x17 -> x10, waiting for transfers between devices: 46.8 us -> 41.7 us  [cycle(): return lax.ppermute(value, BOTH, pairs)]
    all_to_all x1, starting transfers between devices: 5.06 us -> 6.93 us  [on_device(): arrived = lax.all_to_all(packed, 'seq', 0, 0, tiled=True)]
    ppermute x12 -> x11, starting transfers between devices: 17.3 us -> 18.3 us  [flip(): return lax.ppermute(value, 'seq', [(i, i ^ bits) for i in range(devices)])]
  transfers between devices with their start and end apart: 30 -> 22, of which waited for: 19 -> 15; matrix products, arithmetic and copies ran while one was open for 0% -> 1% of each run, Pallas kernels for 2% -> 2%
where the time goes in v7:
time: 144 us
  waiting for transfers between devices  84.2 us (58%)
  starting transfers between devices  40.2 us (28%)
  Pallas kernels  16.1 us (11%)
  local copies, waits for them, and re-layouts  1.81 us (1%)
    ppermute x10, waiting for transfers between devices, cycle(): return lax.ppermute(value, BOTH, pairs)  41.7 us
    all_to_all x1, waiting for transfers between devices, on_device(): arrived = lax.all_to_all(packed, 'seq', 0, 0, tiled=True)  26.9 us
    ppermute x11, starting transfers between devices, flip(): return lax.ppermute(value, 'seq', [(i, i ^ bits) for i in range(devices)])  18.3 us
    ppermute x11, waiting for transfers between devices, flip(): return lax.ppermute(value, 'seq', [(i, i ^ bits) for i in range(devices)])  15.5 us
    ppermute x10, starting transfers between devices, cycle(): return lax.ppermute(value, BOTH, pairs)  15 us
    pallas_call x1, Pallas kernels, on_device(): call(product_cycle, jax.ShapeDtypeStruct((devices, 4, cap, half), BF16),...  11.1 us
    all_to_all x1, starting transfers between devices, on_device(): arrived = lax.all_to_all(packed, 'seq', 0, 0, tiled=True)  6.93 us
  transfers between devices with their start and end apart: 22, of which 15 were waited for; matrix products, arithmetic and copies ran while one was open for 1% of the time, Pallas kernels for 2%

profile of v7, /device:TPU:0, one launch (start us, length us, event | category | flops | bytes accessed | tf_op | source)
XLA Modules:
  0.0 144.0 jit_solution(10630694148765381482)
XLA Ops:
  0.6 1.9 %shard_map.103 = (bf16[224,640]{1,0:T(8,128)(2,1)}, bf16[224,640]{1,0:T(8,128)(2,1)}) custom-call(bf16[224,1280]{1,0:T(8,128)(2,1)} %bitcast.8, bf16[224,1280]{1,0:T(8,128)(2,1)} %bitcast.9), custom_call_target="tpu_custom_call" | custom-call | tf_op jit(solution)/shard_map/pallas_call | solution.py:285
  2.5 3.0 %collective-permute-start = (bf16[224,640]{1,0:T(8,128)(2,1)}, bf16[224,640]{1,0:T(8,128)(2,1)S(1)}, u32[]{:S(2)}, u32[]{:S(2)}) collective-permute-start(bf16[224,640]{1,0:T(8,128)(2,1)} %get-tuple-element.17), channel_id=1, source_target_pairs={{0,2},{1,3},{2,0},{3,1},{4,6},{5,7},{6,4},{7,5},{8,10},{9,11},{10,... | collective-permute-start | bytes 860168 | tf_op jit(solution)/shard_map/ppermute | solution.py:20
  6.5 6.1 %collective-permute-done = bf16[224,640]{1,0:T(8,128)(2,1)S(1)} collective-permute-done((bf16[224,640]{1,0:T(8,128)(2,1)}, bf16[224,640]{1,0:T(8,128)(2,1)S(1)}, u32[]{:S(2)}, u32[]{:S(2)}) %collective-permute-start) | collective-permute-done | bytes 286752 | tf_op jit(solution)/shard_map/ppermute | solution.py:20
  12.6 1.9 %collective-permute-start.2 = (bf16[448,640]{1,0:T(8,128)(2,1)S(1)}, bf16[448,640]{1,0:T(8,128)(2,1)S(1)}, u32[]{:S(2)}, u32[]{:S(2)}) collective-permute-start(bf16[448,640]{1,0:T(8,128)(2,1)S(1)} %constant_dynamic-update-slice_fusion.refs_4_), channel_id=1, source_target_pairs={{0,4},{1,5},{2,6},{3,7},{4,8},{5,9},{6,10},{7,11},{8,12},{9,13},{1... | collective-permute-start | bytes 1720328 | tf_op jit(solution)/shard_map/ppermute | solution.py:30
  14.5 1.7 %collective-permute-start.1 = (bf16[256,3584]{1,0:T(8,128)(2,1)}, bf16[256,3584]{1,0:T(8,128)(2,1)}, u32[]{:S(2)}, u32[]{:S(2)}) collective-permute-start(bf16[256,3584]{1,0:T(8,128)(2,1)} %refs_15_.1), channel_id=1, source_target_pairs={{0,2},{1,3},{2,0},{3,1},{4,6},{5,7},{6,4},{7,5},{8,10},{9,11},{10,... | collective-permute-start | bytes 5505032 | tf_op jit(solution)/shard_map/ppermute | solution.py:20
  16.9 10.8 %collective-permute-done.2.refs_6_ = bf16[448,640]{1,0:T(8,128)(2,1)S(1)} collective-permute-done((bf16[448,640]{1,0:T(8,128)(2,1)S(1)}, bf16[448,640]{1,0:T(8,128)(2,1)S(1)}, u32[]{:S(2)}, u32[]{:S(2)}) %collective-permute-start.2) | collective-permute-done | bytes 573472 | tf_op jit(solution)/shard_map/ppermute | solution.py:30
  29.0 2.9 %collective-permute-start.3 = (bf16[448,640]{1,0:T(8,128)(2,1)S(1)}, bf16[448,640]{1,0:T(8,128)(2,1)S(1)}, u32[]{:S(2)}, u32[]{:S(2)}) collective-permute-start(bf16[448,640]{1,0:T(8,128)(2,1)S(1)} %collective-permute-done.2.refs_6_), channel_id=1, source_target_pairs={{0,4},{1,5},{2,6},{3,7},{4,8},{5,9},{6,10},{7,11},{8,12},{9,13},{1... | collective-permute-start | bytes 1720328 | tf_op jit(solution)/shard_map/ppermute | solution.py:30
  31.9 12.9 %collective-permute-done.3.refs_7_ = bf16[448,640]{1,0:T(8,128)(2,1)S(1)} collective-permute-done((bf16[448,640]{1,0:T(8,128)(2,1)S(1)}, bf16[448,640]{1,0:T(8,128)(2,1)S(1)}, u32[]{:S(2)}, u32[]{:S(2)}) %collective-permute-start.3) | collective-permute-done | bytes 573472 | tf_op jit(solution)/shard_map/ppermute | solution.py:30
  44.7 2.2 %collective-permute-done.5.refs_10_ = bf16[448,640]{1,0:T(8,128)(2,1)S(1)} collective-permute-done((bf16[448,640]{1,0:T(8,128)(2,1)S(1)}, bf16[448,640]{1,0:T(8,128)(2,1)S(1)}, u32[]{:S(2)}, u32[]{:S(2)}) %collective-permute-start.5) | collective-permute-done | bytes 573472 | tf_op jit(solution)/shard_map/ppermute | solution.py:30
  48.2 4.3 %collective-permute-start.9 = (bf16[448,640]{1,0:T(8,128)(2,1)S(1)}, bf16[448,640]{1,0:T(8,128)(2,1)S(1)}, u32[]{:S(2)}, u32[]{:S(2)}) collective-permute-start(bf16[448,640]{1,0:T(8,128)(2,1)S(1)} %collective-permute-done.5.refs_10_), channel_id=1, source_target_pairs={{0,17},{1,16},{2,19},{3,18},{4,0},{5,1},{6,2},{7,3},{8,4},{9,5},{1... | collective-permute-start | bytes 1720328 | tf_op jit(solution)/shard_map/ppermute | solution.py:30
  52.6 10.3 %collective-permute-done.8.refs_8_ = bf16[448,640]{1,0:T(8,128)(2,1)S(1)} collective-permute-done((bf16[448,640]{1,0:T(8,128)(2,1)S(1)}, bf16[448,640]{1,0:T(8,128)(2,1)S(1)}, u32[]{:S(2)}, u32[]{:S(2)}) %collective-permute-start.8) | collective-permute-done | bytes 573472 | tf_op jit(solution)/shard_map/ppermute | solution.py:30
  62.9 3.3 %collective-permute-done.9.refs_11_ = bf16[448,640]{1,0:T(8,128)(2,1)S(1)} collective-permute-done((bf16[448,640]{1,0:T(8,128)(2,1)S(1)}, bf16[448,640]{1,0:T(8,128)(2,1)S(1)}, u32[]{:S(2)}, u32[]{:S(2)}) %collective-permute-start.9) | collective-permute-done | bytes 573472 | tf_op jit(solution)/shard_map/ppermute | solution.py:30
  66.5 1.9 %collective-permute-start.13 = (bf16[224,640]{1,0:T(8,128)(2,1)S(1)}, bf16[224,640]{1,0:T(8,128)(2,1)S(1)}, u32[]{:S(2)}, u32[]{:S(2)}) collective-permute-start(bf16[224,640]{1,0:T(8,128)(2,1)S(1)} %get-tuple-element.32), channel_id=1, source_target_pairs={{0,17},{1,16},{2,19},{3,18},{12,29},{13,28},{14,31},{15,30},{29,12... | collective-permute-start | bytes 860168 | tf_op jit(solution)/shard_map/ppermute | solution.py:30
  72.6 2.1 %collective-permute-done.10.refs_1_ = s32[1,256]{1,0:T(1,128)S(1)} collective-permute-done((s32[1,256]{1,0:T(1,128)S(1)}, s32[1,256]{1,0:T(1,128)S(1)}, u32[]{:S(2)}, u32[]{:S(2)}) %collective-permute-start.10) | collective-permute-done | bytes 1056 | tf_op jit(solution)/shard_map/ppermute | solution.py:20
  75.2 2.4 %collective-permute-done.12.refs_3_ = s32[1,256]{1,0:T(1,128)S(1)} collective-permute-done((s32[1,256]{1,0:T(1,128)S(1)}, s32[1,256]{1,0:T(1,128)S(1)}, u32[]{:S(2)}, u32[]{:S(2)}) %collective-permute-start.12) | collective-permute-done | bytes 1056 | tf_op jit(solution)/shard_map/ppermute | solution.py:20
  77.7 1.9 %collective-permute-done.14.refs_14_ = bf16[224,640]{1,0:T(8,128)(2,1)S(1)} collective-permute-done((bf16[224,640]{1,0:T(8,128)(2,1)S(1)}, bf16[224,640]{1,0:T(8,128)(2,1)S(1)}, u32[]{:S(2)}, u32[]{:S(2)}) %collective-permute-start.14) | collective-permute-done | bytes 286752 | tf_op jit(solution)/shard_map/ppermute | solution.py:30
  80.3 11.1 %shard_map.104 = bf16[16,4,16,640]{3,2,1,0:T(8,128)(2,1)} custom-call(s32[1,256]{1,0:T(1,128)} %bitcast.10, s32[1,256]{1,0:T(1,128)} %copy-done.17, s32[1,256]{1,0:T(1,128)} %copy-done.16, s32[1,256]{1,0:T(1,128)} %copy-done.18, bf16[448,640]{1,0:T(8,128)(2,1)} %copy-done.6, bf16[448,640]{1,0:T(8,128)(2,1)} %copy-done.7, bf16[448,640]{1,0:T(8,128)(2,1)} %copy-done.2, ...), custom_call_target="tpu_custom_call" | custom-call | tf_op jit(solution)/shard_map/pallas_call | solution.py:308
  91.4 6.9 %all-to-all-start = ((bf16[16,64,640]{2,1,0:T(8,128)(2,1)}), bf16[16,64,640]{2,1,0:T(8,128)(2,1)S(1)}, u32[]{:S(2)}, u32[]{:S(2)}) async-start(bf16[16,64,640]{2,1,0:T(8,128)(2,1)} %bitcast.7), calls=%async_computation | async-start | bytes 2621440 | tf_op jit(solution)/shard_map/all_to_all | solution.py:344
  98.9 26.9 %all-to-all-done = bf16[16,64,640]{2,1,0:T(8,128)(2,1)S(1)} async-done(((bf16[16,64,640]{2,1,0:T(8,128)(2,1)}), bf16[16,64,640]{2,1,0:T(8,128)(2,1)S(1)}, u32[]{:S(2)}, u32[]{:S(2)}) %all-to-all-start) | async-done | bytes 1310752 | tf_op jit(solution)/shard_map/all_to_all | solution.py:344
  128.0 2.3 %collective-permute-start.18 = (f32[2,1280]{1,0:T(2,128)S(1)}, f32[2,1280]{1,0:T(2,128)S(1)}, u32[]{:S(2)}, u32[]{:S(2)}) collective-permute-start(f32[2,1280]{1,0:T(2,128)S(1)} %add.20), channel_id=1, source_target_pairs={{0,2},{1,3},{2,0},{3,1},{4,6},{5,7},{6,4},{7,5},{8,10},{9,11},{10,... | collective-permute-start | bytes 30728 | tf_op jit(solution)/shard_map/ppermute | solution.py:20
  132.0 3.8 %collective-permute-start.19 = (f32[2,1280]{1,0:T(2,128)S(1)}, f32[2,1280]{1,0:T(2,128)S(1)}, u32[]{:S(2)}, u32[]{:S(2)}) collective-permute-start(f32[2,1280]{1,0:T(2,128)S(1)} %add.21), channel_id=1, source_target_pairs={{0,4},{1,5},{2,6},{3,7},{4,0},{5,1},{6,2},{7,3},{8,12},{9,13},{10,... | collective-permute-start | bytes 30728 | tf_op jit(solution)/shard_map/ppermute | solution.py:20
  135.8 1.7 %collective-permute-done.19 = f32[2,1280]{1,0:T(2,128)S(1)} collective-permute-done((f32[2,1280]{1,0:T(2,128)S(1)}, f32[2,1280]{1,0:T(2,128)S(1)}, u32[]{:S(2)}, u32[]{:S(2)}) %collective-permute-start.19) | collective-permute-done | bytes 10272 | tf_op jit(solution)/shard_map/ppermute | solution.py:20
  137.5 3.8 %collective-permute-start.20 = (f32[2,1280]{1,0:T(2,128)S(1)}, f32[2,1280]{1,0:T(2,128)S(1)}, u32[]{:S(2)}, u32[]{:S(2)}) collective-permute-start(f32[2,1280]{1,0:T(2,128)S(1)} %add.22), channel_id=1, source_target_pairs={{0,8},{1,9},{2,10},{3,11},{4,12},{5,13},{6,14},{7,15},{8,0},{9,1},... | collective-permute-start | bytes 30728 | tf_op jit(solution)/shard_map/ppermute | solution.py:20
  141.4 2.0 %shard_map.106 = (bf16[256,1280]{1,0:T(8,128)(2,1)}, bf16[256,1280]{1,0:T(8,128)(2,1)}) custom-call(bf16[4,2,2,4,16,640]{5,4,3,2,1,0:T(8,128)(2,1)S(1)} %bitcast.6, bf16[256,1280]{1,0:T(8,128)(2,1)S(1)} %copy-done, bf16[256,1280]{1,0:T(8,128)(2,1)S(1)} %copy-done.1, f32[256,1]{1,0:T(8,128)S(1)} %get-tuple-element.26.a_mean, ...), custom_call_target="tpu_custom_call" | custom-call | tf_op jit(solution)/shard_map/pallas_call | solution.py:354
  (74 shorter events, 15.1 us)
Async XLA Ops:
  2.5 10.0 %collective-permute-start = (bf16[224,640]{1,0:T(8,128)(2,1)}, bf16[224,640]{1,0:T(8,128)(2,1)S(1)}, u32[]{:S(2)}, u32[]{:S(2)}) collective-permute-start(bf16[224,640]{1,0:T(8,128)(2,1)} %get-tuple-element.17), channel_id=1, source_target_pairs={{0,2},{1,3},{2,0},{3,1},{4,6},{5,7},{6,4},{7,5},{8,10},{9,11},{10,... | collective-permute-start | bytes 860168 | tf_op jit(solution)/shard_map/ppermute | solution.py:20
  12.6 53.8 %copy-start.6 = (bf16[448,640]{1,0:T(8,128)(2,1)}, bf16[448,640]{1,0:T(8,128)(2,1)S(1)}, u32[]{:S(2)}) copy-start(bf16[448,640]{1,0:T(8,128)(2,1)S(1)} %constant_dynamic-update-slice_fusion.refs_4_) | copy-start | bytes 1720324
  12.6 15.0 %collective-permute-start.2 = (bf16[448,640]{1,0:T(8,128)(2,1)S(1)}, bf16[448,640]{1,0:T(8,128)(2,1)S(1)}, u32[]{:S(2)}, u32[]{:S(2)}) collective-permute-start(bf16[448,640]{1,0:T(8,128)(2,1)S(1)} %constant_dynamic-update-slice_fusion.refs_4_), channel_id=1, source_target_pairs={{0,4},{1,5},{2,6},{3,7},{4,8},{5,9},{6,10},{7,11},{8,12},{9,13},{1... | collective-permute-start | bytes 1720328 | tf_op jit(solution)/shard_map/ppermute | solution.py:30
  14.5 13.6 %collective-permute-start.4 = (bf16[448,640]{1,0:T(8,128)(2,1)S(1)}, bf16[448,640]{1,0:T(8,128)(2,1)S(1)}, u32[]{:S(2)}, u32[]{:S(2)}) collective-permute-start(bf16[448,640]{1,0:T(8,128)(2,1)S(1)} %constant_dynamic-update-slice_fusion.refs_4_), channel_id=1, source_target_pairs={{0,17},{1,16},{2,19},{3,18},{4,0},{5,1},{6,2},{7,3},{8,4},{9,5},{1... | collective-permute-start | bytes 1720328 | tf_op jit(solution)/shard_map/ppermute | solution.py:30
  14.5 51.7 %collective-permute-start.1 = (bf16[256,3584]{1,0:T(8,128)(2,1)}, bf16[256,3584]{1,0:T(8,128)(2,1)}, u32[]{:S(2)}, u32[]{:S(2)}) collective-permute-start(bf16[256,3584]{1,0:T(8,128)(2,1)} %refs_15_.1), channel_id=1, source_target_pairs={{0,2},{1,3},{2,0},{3,1},{4,6},{5,7},{6,4},{7,5},{8,10},{9,11},{10,... | collective-permute-start | bytes 5505032 | tf_op jit(solution)/shard_map/ppermute | solution.py:20
  16.2 15.7 %collective-permute-start.7 = (bf16[448,640]{1,0:T(8,128)(2,1)S(1)}, bf16[448,640]{1,0:T(8,128)(2,1)S(1)}, u32[]{:S(2)}, u32[]{:S(2)}) collective-permute-start(bf16[448,640]{1,0:T(8,128)(2,1)S(1)} %constant_dynamic-update-slice_fusion.refs_4_), channel_id=1, source_target_pairs={{4,21},{5,20},{6,23},{7,22},{8,25},{9,24},{10,27},{11,26},{25,8},{... | collective-permute-start | bytes 1720328 | tf_op jit(solution)/shard_map/ppermute | solution.py:30
  28.2 3.7 %collective-permute-start.6 = (bf16[448,640]{1,0:T(8,128)(2,1)S(1)}, bf16[448,640]{1,0:T(8,128)(2,1)S(1)}, u32[]{:S(2)}, u32[]{:S(2)}) collective-permute-start(bf16[448,640]{1,0:T(8,128)(2,1)S(1)} %broadcast_select_fusion.1), channel_id=1, source_target_pairs={{4,21},{5,20},{6,23},{7,22},{8,25},{9,24},{10,27},{11,26},{25,8},{... | collective-permute-start | bytes 1720328 | tf_op jit(solution)/shard_map/ppermute | solution.py:30
  29.0 15.7 %collective-permute-start.3 = (bf16[448,640]{1,0:T(8,128)(2,1)S(1)}, bf16[448,640]{1,0:T(8,128)(2,1)S(1)}, u32[]{:S(2)}, u32[]{:S(2)}) collective-permute-start(bf16[448,640]{1,0:T(8,128)(2,1)S(1)} %collective-permute-done.2.refs_6_), channel_id=1, source_target_pairs={{0,4},{1,5},{2,6},{3,7},{4,8},{5,9},{6,10},{7,11},{8,12},{9,13},{1... | collective-permute-start | bytes 1720328 | tf_op jit(solution)/shard_map/ppermute | solution.py:30
  31.8 15.1 %collective-permute-start.5 = (bf16[448,640]{1,0:T(8,128)(2,1)S(1)}, bf16[448,640]{1,0:T(8,128)(2,1)S(1)}, u32[]{:S(2)}, u32[]{:S(2)}) collective-permute-start(bf16[448,640]{1,0:T(8,128)(2,1)S(1)} %collective-permute-done.4.refs_9_), channel_id=1, source_target_pairs={{0,17},{1,16},{2,19},{3,18},{4,0},{5,1},{6,2},{7,3},{8,4},{9,5},{1... | collective-permute-start | bytes 1720328 | tf_op jit(solution)/shard_map/ppermute | solution.py:30
  31.9 47.7 %copy-start.7 = (bf16[448,640]{1,0:T(8,128)(2,1)}, bf16[448,640]{1,0:T(8,128)(2,1)S(1)}, u32[]{:S(2)}) copy-start(bf16[448,640]{1,0:T(8,128)(2,1)S(1)} %collective-permute-done.7.refs_5_) | copy-start | bytes 1720324
  46.9 16.0 %collective-permute-start.8 = (bf16[448,640]{1,0:T(8,128)(2,1)S(1)}, bf16[448,640]{1,0:T(8,128)(2,1)S(1)}, u32[]{:S(2)}, u32[]{:S(2)}) collective-permute-start(bf16[448,640]{1,0:T(8,128)(2,1)S(1)} %collective-permute-done.3.refs_7_), channel_id=1, source_target_pairs={{4,8},{5,9},{6,10},{7,11},{8,12},{9,13},{10,14},{11,15},{12,29},{1... | collective-permute-start | bytes 1720328 | tf_op jit(solution)/shard_map/ppermute | solution.py:30
  48.2 18.0 %collective-permute-start.9 = (bf16[448,640]{1,0:T(8,128)(2,1)S(1)}, bf16[448,640]{1,0:T(8,128)(2,1)S(1)}, u32[]{:S(2)}, u32[]{:S(2)}) collective-permute-start(bf16[448,640]{1,0:T(8,128)(2,1)S(1)} %collective-permute-done.5.refs_10_), channel_id=1, source_target_pairs={{0,17},{1,16},{2,19},{3,18},{4,0},{5,1},{6,2},{7,3},{8,4},{9,5},{1... | collective-permute-start | bytes 1720328 | tf_op jit(solution)/shard_map/ppermute | solution.py:30
  52.5 27.0 %collective-permute-start.15 = (bf16[256,3584]{1,0:T(8,128)(2,1)}, bf16[256,3584]{1,0:T(8,128)(2,1)}, u32[]{:S(2)}, u32[]{:S(2)}) collective-permute-start(bf16[256,3584]{1,0:T(8,128)(2,1)} %refs_15_.1), channel_id=1, source_target_pairs={{0,1},{1,0},{2,3},{3,2},{4,5},{5,4},{6,7},{7,6},{8,9},{9,8},{10,11... | collective-permute-start | bytes 5505032 | tf_op jit(solution)/shard_map/ppermute | solution.py:20
  66.2 13.3 %collective-permute-start.16 = (bf16[256,3584]{1,0:T(8,128)(2,1)}, bf16[256,3584]{1,0:T(8,128)(2,1)}, u32[]{:S(2)}, u32[]{:S(2)}) collective-permute-start(bf16[256,3584]{1,0:T(8,128)(2,1)} %collective-permute-done.1.refs_16_), channel_id=1, source_target_pairs={{0,1},{1,0},{2,3},{3,2},{4,5},{5,4},{6,7},{7,6},{8,9},{9,8},{10,11... | collective-permute-start | bytes 5505032 | tf_op jit(solution)/shard_map/ppermute | solution.py:20
  66.5 11.2 %collective-permute-start.13 = (bf16[224,640]{1,0:T(8,128)(2,1)S(1)}, bf16[224,640]{1,0:T(8,128)(2,1)S(1)}, u32[]{:S(2)}, u32[]{:S(2)}) collective-permute-start(bf16[224,640]{1,0:T(8,128)(2,1)S(1)} %get-tuple-element.32), channel_id=1, source_target_pairs={{0,17},{1,16},{2,19},{3,18},{12,29},{13,28},{14,31},{15,30},{29,12... | collective-permute-start | bytes 860168 | tf_op jit(solution)/shard_map/ppermute | solution.py:30
  68.4 11.1 %collective-permute-start.14 = (bf16[224,640]{1,0:T(8,128)(2,1)S(1)}, bf16[224,640]{1,0:T(8,128)(2,1)S(1)}, u32[]{:S(2)}, u32[]{:S(2)}) collective-permute-start(bf16[224,640]{1,0:T(8,128)(2,1)S(1)} %get-tuple-element.31), channel_id=1, source_target_pairs={{4,0},{5,1},{6,2},{7,3},{8,12},{9,13},{10,14},{11,15},{25,29},{24,... | collective-permute-start | bytes 860168 | tf_op jit(solution)/shard_map/ppermute | solution.py:30
  69.7 1.4 collective-permute-start.11
  71.1 3.6 %collective-permute-start.10 = (s32[1,256]{1,0:T(1,128)S(1)}, s32[1,256]{1,0:T(1,128)S(1)}, u32[]{:S(2)}, u32[]{:S(2)}) collective-permute-start(s32[1,256]{1,0:T(1,128)S(1)} %bitcast.12), channel_id=1, source_target_pairs={{0,2},{1,3},{2,0},{3,1},{4,6},{5,7},{6,4},{7,5},{8,10},{9,11},{10,... | collective-permute-start | bytes 3080 | tf_op jit(solution)/shard_map/ppermute | solution.py:20
  74.7 3.0 %collective-permute-start.12 = (s32[1,256]{1,0:T(1,128)S(1)}, s32[1,256]{1,0:T(1,128)S(1)}, u32[]{:S(2)}, u32[]{:S(2)}) collective-permute-start(s32[1,256]{1,0:T(1,128)S(1)} %bitcast.13), channel_id=1, source_target_pairs={{0,3},{1,2},{2,1},{3,0},{4,7},{5,6},{6,5},{7,4},{8,11},{9,10},{10,... | collective-permute-start | bytes 3080 | tf_op jit(solution)/shard_map/ppermute | solution.py:20
  91.4 34.4 %all-to-all-start = ((bf16[16,64,640]{2,1,0:T(8,128)(2,1)}), bf16[16,64,640]{2,1,0:T(8,128)(2,1)S(1)}, u32[]{:S(2)}, u32[]{:S(2)}) async-start(bf16[16,64,640]{2,1,0:T(8,128)(2,1)} %bitcast.7), calls=%async_computation | async-start | bytes 2621440 | tf_op jit(solution)/shard_map/all_to_all | solution.py:344
  126.4 1.7 %collective-permute-start.17 = (f32[2,1280]{1,0:T(2,128)S(1)}, f32[2,1280]{1,0:T(2,128)S(1)}, u32[]{:S(2)}, u32[]{:S(2)}) collective-permute-start(f32[2,1280]{1,0:T(2,128)S(1)} %shard_map.107), channel_id=1, source_target_pairs={{0,1},{1,0},{2,3},{3,2},{4,5},{5,4},{6,7},{7,6},{8,9},{9,8},{10,11... | collective-permute-start | bytes 30728 | tf_op jit(solution)/shard_map/ppermute | solution.py:20
  128.0 4.0 %collective-permute-start.18 = (f32[2,1280]{1,0:T(2,128)S(1)}, f32[2,1280]{1,0:T(2,128)S(1)}, u32[]{:S(2)}, u32[]{:S(2)}) collective-permute-start(f32[2,1280]{1,0:T(2,128)S(1)} %add.20), channel_id=1, source_target_pairs={{0,2},{1,3},{2,0},{3,1},{4,6},{5,7},{6,4},{7,5},{8,10},{9,11},{10,... | collective-permute-start | bytes 30728 | tf_op jit(solution)/shard_map/ppermute | solution.py:20
  132.0 5.5 %collective-permute-start.19 = (f32[2,1280]{1,0:T(2,128)S(1)}, f32[2,1280]{1,0:T(2,128)S(1)}, u32[]{:S(2)}, u32[]{:S(2)}) collective-permute-start(f32[2,1280]{1,0:T(2,128)S(1)} %add.21), channel_id=1, source_target_pairs={{0,4},{1,5},{2,6},{3,7},{4,0},{5,1},{6,2},{7,3},{8,12},{9,13},{10,... | collective-permute-start | bytes 30728 | tf_op jit(solution)/shard_map/ppermute | solution.py:20
  137.5 5.9 %collective-permute-start.20 = (f32[2,1280]{1,0:T(2,128)S(1)}, f32[2,1280]{1,0:T(2,128)S(1)}, u32[]{:S(2)}, u32[]{:S(2)}) collective-permute-start(f32[2,1280]{1,0:T(2,128)S(1)} %add.22), channel_id=1, source_target_pairs={{0,8},{1,9},{2,10},{3,11},{4,12},{5,13},{6,14},{7,15},{8,0},{9,1},... | collective-permute-start | bytes 30728 | tf_op jit(solution)/shard_map/ppermute | solution.py:20
  (17 other events, 297.2 us)

commit v8 on v7

--- a/solution.py
+++ b/solution.py
@@ -285,12 +285,14 @@
         keep, to_pair = call(cut, (block,) * 2, [ANY, ANY], [pltpu.SemaphoreType.DMA((2,))], VM, WHOLE)(
             audio_proj.T, vision_proj.T
         )
-        from_pair = flip(to_pair, 2, devices)
-        whole = jnp.concatenate([keep, from_pair])
-        r_pair = flip(after(grad_rows, from_pair), 2, devices)
         p = jnp.where(group == 0, line, 7 - line)
         ends, mids = (0, 3, 4, 7), (1, 2, 5, 6)
-        f1, b1 = step(whole, whole, 1, devices)
+        f_own, b_own = step(keep, keep, 1, devices)
+        from_pair = after(flip(to_pair, 2, devices), f_own, b_own)
+        r_pair = flip(after(grad_rows, from_pair), 2, devices)
+        f_far, b_far = step(from_pair, from_pair, 1, devices)
+        whole = jnp.concatenate([keep, from_pair])
+        f1, b1 = jnp.concatenate([f_own, f_far]), jnp.concatenate([b_own, b_far])
         r_core = flip(after(grad_rows, f1, b1), 1, devices)
         i_core = flip(after(ids, f1, b1), 1, devices)
         mirror = cycle(whole, [(a, 7 - a) for a in mids], devices)

time: 144 us -> 141 us (0.979)
  waiting for transfers between devices: 84.2 us -> 80.5 us
    ppermute x11, waiting for transfers between devices: 15.5 us -> 6.01 us  [flip(): return lax.ppermute(value, 'seq', [(i, i ^ bits) for i in range(devices)])]
    ppermute x10 -> x12, waiting for transfers between devices: 41.7 us -> 47.7 us  [cycle(): return lax.ppermute(value, BOTH, pairs)]
    ppermute x10 -> x12, starting transfers between devices: 15 us -> 18.8 us  [cycle(): return lax.ppermute(value, BOTH, pairs)]
    all_to_all x1, starting transfers between devices: 6.93 us -> 3.84 us  [on_device(): arrived = lax.all_to_all(packed, 'seq', 0, 0, tiled=True)]
  transfers between devices with their start and end apart: 22 -> 24, of which waited for: 15 -> 16; matrix products, arithmetic and copies ran while one was open for 1% -> 1% of each run, Pallas kernels for 2% -> 2%
where the time goes in v8:
time: 141 us
  waiting for transfers between devices  80.5 us (57%)
  starting transfers between devices  40.7 us (29%)
  Pallas kernels  16.1 us (11%)
  local copies, waits for them, and re-layouts  1.84 us (1%)
    ppermute x12, waiting for transfers between devices, cycle(): return lax.ppermute(value, BOTH, pairs)  47.7 us
    all_to_all x1, waiting for transfers between devices, on_device(): arrived = lax.all_to_all(packed, 'seq', 0, 0, tiled=True)  26.8 us
    ppermute x12, starting transfers between devices, cycle(): return lax.ppermute(value, BOTH, pairs)  18.8 us
    ppermute x11, starting transfers between devices, flip(): return lax.ppermute(value, 'seq', [(i, i ^ bits) for i in range(devices)])  18.1 us
    pallas_call x1, Pallas kernels, on_device(): call(product_cycle, jax.ShapeDtypeStruct((devices, 4, cap, half), BF16),...  11.1 us
    ppermute x11, waiting for transfers between devices, flip(): return lax.ppermute(value, 'seq', [(i, i ^ bits) for i in range(devices)])  6.01 us
    all_to_all x1, starting transfers between devices, on_device(): arrived = lax.all_to_all(packed, 'seq', 0, 0, tiled=True)  3.84 us
  transfers between devices with their start and end apart: 24, of which 16 were waited for; matrix products, arithmetic and copies ran while one was open for 1% of the time, Pallas kernels for 2%

profile of v8, /device:TPU:0, one launch (start us, length us, event | category | flops | bytes accessed | tf_op | source)
XLA Modules:
  0.0 140.8 jit_solution(901291175182824881)
XLA Ops:
  0.6 1.9 %shard_map.103 = (bf16[224,640]{1,0:T(8,128)(2,1)}, bf16[224,640]{1,0:T(8,128)(2,1)}) custom-call(bf16[224,1280]{1,0:T(8,128)(2,1)} %bitcast.8, bf16[224,1280]{1,0:T(8,128)(2,1)} %bitcast.9), custom_call_target="tpu_custom_call" | custom-call | tf_op jit(solution)/shard_map/pallas_call | solution.py:285
  2.5 3.1 %collective-permute-start.1 = (bf16[224,640]{1,0:T(8,128)(2,1)}, bf16[224,640]{1,0:T(8,128)(2,1)S(1)}, u32[]{:S(2)}, u32[]{:S(2)}) collective-permute-start(bf16[224,640]{1,0:T(8,128)(2,1)} %get-tuple-element.19), channel_id=1, source_target_pairs={{0,4},{1,5},{2,6},{3,7},{4,8},{5,9},{6,10},{7,11},{8,12},{9,13},{1... | collective-permute-start | bytes 860168 | tf_op jit(solution)/shard_map/ppermute | solution.py:30
  5.6 1.7 %collective-permute-start = (bf16[224,640]{1,0:T(8,128)(2,1)}, bf16[224,640]{1,0:T(8,128)(2,1)S(1)}, u32[]{:S(2)}, u32[]{:S(2)}) collective-permute-start(bf16[224,640]{1,0:T(8,128)(2,1)} %get-tuple-element.18), channel_id=1, source_target_pairs={{0,2},{1,3},{2,0},{3,1},{4,6},{5,7},{6,4},{7,5},{8,10},{9,11},{10,... | collective-permute-start | bytes 860168 | tf_op jit(solution)/shard_map/ppermute | solution.py:20
  8.3 3.8 %collective-permute-done.1 = bf16[224,640]{1,0:T(8,128)(2,1)S(1)} collective-permute-done((bf16[224,640]{1,0:T(8,128)(2,1)}, bf16[224,640]{1,0:T(8,128)(2,1)S(1)}, u32[]{:S(2)}, u32[]{:S(2)}) %collective-permute-start.1) | collective-permute-done | bytes 286752 | tf_op jit(solution)/shard_map/ppermute | solution.py:30
  12.0 2.1 %collective-permute-done.2 = bf16[224,640]{1,0:T(8,128)(2,1)S(1)} collective-permute-done((bf16[224,640]{1,0:T(8,128)(2,1)}, bf16[224,640]{1,0:T(8,128)(2,1)S(1)}, u32[]{:S(2)}, u32[]{:S(2)}) %collective-permute-start.2) | collective-permute-done | bytes 286752 | tf_op jit(solution)/shard_map/ppermute | solution.py:30
  18.8 4.7 %collective-permute-done.4 = bf16[224,640]{1,0:T(8,128)(2,1)S(1)} collective-permute-done((bf16[224,640]{1,0:T(8,128)(2,1)S(1)}, bf16[224,640]{1,0:T(8,128)(2,1)S(1)}, u32[]{:S(2)}, u32[]{:S(2)}) %collective-permute-start.4) | collective-permute-done | bytes 286752 | tf_op jit(solution)/shard_map/ppermute | solution.py:30
  24.5 3.6 %collective-permute-start.5 = (bf16[448,640]{1,0:T(8,128)(2,1)S(1)}, bf16[448,640]{1,0:T(8,128)(2,1)S(1)}, u32[]{:S(2)}, u32[]{:S(2)}) collective-permute-start(bf16[448,640]{1,0:T(8,128)(2,1)S(1)} %constant_dynamic-update-slice_fusion.refs_6_), channel_id=1, source_target_pairs={{0,4},{1,5},{2,6},{3,7},{4,8},{5,9},{6,10},{7,11},{8,12},{9,13},{1... | collective-permute-start | bytes 1720328 | tf_op jit(solution)/shard_map/ppermute | solution.py:30
  28.2 12.4 %collective-permute-done.5.refs_7_ = bf16[448,640]{1,0:T(8,128)(2,1)S(1)} collective-permute-done((bf16[448,640]{1,0:T(8,128)(2,1)S(1)}, bf16[448,640]{1,0:T(8,128)(2,1)S(1)}, u32[]{:S(2)}, u32[]{:S(2)}) %collective-permute-start.5) | collective-permute-done | bytes 573472 | tf_op jit(solution)/shard_map/ppermute | solution.py:30
  40.6 2.2 %collective-permute-done.7.refs_10_ = bf16[448,640]{1,0:T(8,128)(2,1)S(1)} collective-permute-done((bf16[448,640]{1,0:T(8,128)(2,1)S(1)}, bf16[448,640]{1,0:T(8,128)(2,1)S(1)}, u32[]{:S(2)}, u32[]{:S(2)}) %collective-permute-start.7) | collective-permute-done | bytes 573472 | tf_op jit(solution)/shard_map/ppermute | solution.py:30
  44.1 4.3 %collective-permute-start.11 = (bf16[448,640]{1,0:T(8,128)(2,1)S(1)}, bf16[448,640]{1,0:T(8,128)(2,1)S(1)}, u32[]{:S(2)}, u32[]{:S(2)}) collective-permute-start(bf16[448,640]{1,0:T(8,128)(2,1)S(1)} %collective-permute-done.7.refs_10_), channel_id=1, source_target_pairs={{0,17},{1,16},{2,19},{3,18},{4,0},{5,1},{6,2},{7,3},{8,4},{9,5},{1... | collective-permute-start | bytes 1720328 | tf_op jit(solution)/shard_map/ppermute | solution.py:30
  48.5 10.7 %collective-permute-done.10.refs_8_ = bf16[448,640]{1,0:T(8,128)(2,1)S(1)} collective-permute-done((bf16[448,640]{1,0:T(8,128)(2,1)S(1)}, bf16[448,640]{1,0:T(8,128)(2,1)S(1)}, u32[]{:S(2)}, u32[]{:S(2)}) %collective-permute-start.10) | collective-permute-done | bytes 573472 | tf_op jit(solution)/shard_map/ppermute | solution.py:30
  59.2 6.7 %collective-permute-done.11.refs_11_ = bf16[448,640]{1,0:T(8,128)(2,1)S(1)} collective-permute-done((bf16[448,640]{1,0:T(8,128)(2,1)S(1)}, bf16[448,640]{1,0:T(8,128)(2,1)S(1)}, u32[]{:S(2)}, u32[]{:S(2)}) %collective-permute-start.11) | collective-permute-done | bytes 573472 | tf_op jit(solution)/shard_map/ppermute | solution.py:30
  66.2 1.9 %collective-permute-start.15 = (bf16[224,640]{1,0:T(8,128)(2,1)S(1)}, bf16[224,640]{1,0:T(8,128)(2,1)S(1)}, u32[]{:S(2)}, u32[]{:S(2)}) collective-permute-start(bf16[224,640]{1,0:T(8,128)(2,1)S(1)} %get-tuple-element.34), channel_id=1, source_target_pairs={{0,17},{1,16},{2,19},{3,18},{12,29},{13,28},{14,31},{15,30},{29,12... | collective-permute-start | bytes 860168 | tf_op jit(solution)/shard_map/ppermute | solution.py:30
  72.3 4.3 %collective-permute-done.15.refs_13_ = bf16[224,640]{1,0:T(8,128)(2,1)S(1)} collective-permute-done((bf16[224,640]{1,0:T(8,128)(2,1)S(1)}, bf16[224,640]{1,0:T(8,128)(2,1)S(1)}, u32[]{:S(2)}, u32[]{:S(2)}) %collective-permute-start.15) | collective-permute-done | bytes 286752 | tf_op jit(solution)/shard_map/ppermute | solution.py:30
  76.6 1.8 %collective-permute-start.14 = (s32[1,256]{1,0:T(1,128)S(1)}, s32[1,256]{1,0:T(1,128)S(1)}, u32[]{:S(2)}, u32[]{:S(2)}) collective-permute-start(s32[1,256]{1,0:T(1,128)S(1)} %bitcast.13), channel_id=1, source_target_pairs={{0,3},{1,2},{2,1},{3,0},{4,7},{5,6},{6,5},{7,4},{8,11},{9,10},{10,... | collective-permute-start | bytes 3080 | tf_op jit(solution)/shard_map/ppermute | solution.py:20
  80.3 11.1 %shard_map.104 = bf16[16,4,16,640]{3,2,1,0:T(8,128)(2,1)} custom-call(s32[1,256]{1,0:T(1,128)} %bitcast.10, s32[1,256]{1,0:T(1,128)} %copy-done.17, s32[1,256]{1,0:T(1,128)} %copy-done.16, s32[1,256]{1,0:T(1,128)} %copy-done.18, bf16[448,640]{1,0:T(8,128)(2,1)} %copy-done.6, bf16[448,640]{1,0:T(8,128)(2,1)} %copy-done.7, bf16[448,640]{1,0:T(8,128)(2,1)} %copy-done.3, ...), custom_call_target="tpu_custom_call" | custom-call | tf_op jit(solution)/shard_map/pallas_call | solution.py:310
  91.4 3.8 %all-to-all-start = ((bf16[16,64,640]{2,1,0:T(8,128)(2,1)}), bf16[16,64,640]{2,1,0:T(8,128)(2,1)S(1)}, u32[]{:S(2)}, u32[]{:S(2)}) async-start(bf16[16,64,640]{2,1,0:T(8,128)(2,1)} %bitcast.7), calls=%async_computation | async-start | bytes 2621440 | tf_op jit(solution)/shard_map/all_to_all | solution.py:346
  95.8 26.8 %all-to-all-done = bf16[16,64,640]{2,1,0:T(8,128)(2,1)S(1)} async-done(((bf16[16,64,640]{2,1,0:T(8,128)(2,1)}), bf16[16,64,640]{2,1,0:T(8,128)(2,1)S(1)}, u32[]{:S(2)}, u32[]{:S(2)}) %all-to-all-start) | async-done | bytes 1310752 | tf_op jit(solution)/shard_map/all_to_all | solution.py:346
  124.9 2.3 %collective-permute-start.20 = (f32[2,1280]{1,0:T(2,128)S(1)}, f32[2,1280]{1,0:T(2,128)S(1)}, u32[]{:S(2)}, u32[]{:S(2)}) collective-permute-start(f32[2,1280]{1,0:T(2,128)S(1)} %add.20), channel_id=1, source_target_pairs={{0,2},{1,3},{2,0},{3,1},{4,6},{5,7},{6,4},{7,5},{8,10},{9,11},{10,... | collective-permute-start | bytes 30728 | tf_op jit(solution)/shard_map/ppermute | solution.py:20
  127.2 1.6 %collective-permute-done.20 = f32[2,1280]{1,0:T(2,128)S(1)} collective-permute-done((f32[2,1280]{1,0:T(2,128)S(1)}, f32[2,1280]{1,0:T(2,128)S(1)}, u32[]{:S(2)}, u32[]{:S(2)}) %collective-permute-start.20) | collective-permute-done | bytes 10272 | tf_op jit(solution)/shard_map/ppermute | solution.py:20
  128.9 3.8 %collective-permute-start.21 = (f32[2,1280]{1,0:T(2,128)S(1)}, f32[2,1280]{1,0:T(2,128)S(1)}, u32[]{:S(2)}, u32[]{:S(2)}) collective-permute-start(f32[2,1280]{1,0:T(2,128)S(1)} %add.21), channel_id=1, source_target_pairs={{0,4},{1,5},{2,6},{3,7},{4,0},{5,1},{6,2},{7,3},{8,12},{9,13},{10,... | collective-permute-start | bytes 30728 | tf_op jit(solution)/shard_map/ppermute | solution.py:20
  132.7 1.7 %collective-permute-done.21 = f32[2,1280]{1,0:T(2,128)S(1)} collective-permute-done((f32[2,1280]{1,0:T(2,128)S(1)}, f32[2,1280]{1,0:T(2,128)S(1)}, u32[]{:S(2)}, u32[]{:S(2)}) %collective-permute-start.21) | collective-permute-done | bytes 10272 | tf_op jit(solution)/shard_map/ppermute | solution.py:20
  134.4 3.8 %collective-permute-start.22 = (f32[2,1280]{1,0:T(2,128)S(1)}, f32[2,1280]{1,0:T(2,128)S(1)}, u32[]{:S(2)}, u32[]{:S(2)}) collective-permute-start(f32[2,1280]{1,0:T(2,128)S(1)} %add.22), channel_id=1, source_target_pairs={{0,8},{1,9},{2,10},{3,11},{4,12},{5,13},{6,14},{7,15},{8,0},{9,1},... | collective-permute-start | bytes 30728 | tf_op jit(solution)/shard_map/ppermute | solution.py:20
  138.2 2.0 %shard_map.106 = (bf16[256,1280]{1,0:T(8,128)(2,1)}, bf16[256,1280]{1,0:T(8,128)(2,1)}) custom-call(bf16[4,2,2,4,16,640]{5,4,3,2,1,0:T(8,128)(2,1)S(1)} %bitcast.6, bf16[256,1280]{1,0:T(8,128)(2,1)S(1)} %copy-done, bf16[256,1280]{1,0:T(8,128)(2,1)S(1)} %copy-done.1, f32[256,1]{1,0:T(8,128)S(1)} %get-tuple-element.28.a_mean, ...), custom_call_target="tpu_custom_call" | custom-call | tf_op jit(solution)/shard_map/pallas_call | solution.py:356
  (82 shorter events, 17.6 us)
Async XLA Ops:
  2.5 9.5 %collective-permute-start.1 = (bf16[224,640]{1,0:T(8,128)(2,1)}, bf16[224,640]{1,0:T(8,128)(2,1)S(1)}, u32[]{:S(2)}, u32[]{:S(2)}) collective-permute-start(bf16[224,640]{1,0:T(8,128)(2,1)} %get-tuple-element.19), channel_id=1, source_target_pairs={{0,4},{1,5},{2,6},{3,7},{4,8},{5,9},{6,10},{7,11},{8,12},{9,13},{1... | collective-permute-start | bytes 860168 | tf_op jit(solution)/shard_map/ppermute | solution.py:30
  5.6 8.5 %collective-permute-start.2 = (bf16[224,640]{1,0:T(8,128)(2,1)}, bf16[224,640]{1,0:T(8,128)(2,1)S(1)}, u32[]{:S(2)}, u32[]{:S(2)}) collective-permute-start(bf16[224,640]{1,0:T(8,128)(2,1)} %get-tuple-element.19), channel_id=1, source_target_pairs={{0,17},{1,16},{2,19},{3,18},{4,0},{5,1},{6,2},{7,3},{8,4},{9,5},{1... | collective-permute-start | bytes 860168 | tf_op jit(solution)/shard_map/ppermute | solution.py:30
  5.6 9.1 %collective-permute-start = (bf16[224,640]{1,0:T(8,128)(2,1)}, bf16[224,640]{1,0:T(8,128)(2,1)S(1)}, u32[]{:S(2)}, u32[]{:S(2)}) collective-permute-start(bf16[224,640]{1,0:T(8,128)(2,1)} %get-tuple-element.18), channel_id=1, source_target_pairs={{0,2},{1,3},{2,0},{3,1},{4,6},{5,7},{6,4},{7,5},{8,10},{9,11},{10,... | collective-permute-start | bytes 860168 | tf_op jit(solution)/shard_map/ppermute | solution.py:20
  14.7 8.8 %collective-permute-start.4 = (bf16[224,640]{1,0:T(8,128)(2,1)S(1)}, bf16[224,640]{1,0:T(8,128)(2,1)S(1)}, u32[]{:S(2)}, u32[]{:S(2)}) collective-permute-start(bf16[224,640]{1,0:T(8,128)(2,1)S(1)} %collective-permute-done), channel_id=1, source_target_pairs={{0,4},{1,5},{2,6},{3,7},{4,8},{5,9},{6,10},{7,11},{8,12},{9,13},{1... | collective-permute-start | bytes 860168 | tf_op jit(solution)/shard_map/ppermute | solution.py:30
  15.9 7.7 %collective-permute-start.6 = (bf16[224,640]{1,0:T(8,128)(2,1)S(1)}, bf16[224,640]{1,0:T(8,128)(2,1)S(1)}, u32[]{:S(2)}, u32[]{:S(2)}) collective-permute-start(bf16[224,640]{1,0:T(8,128)(2,1)S(1)} %collective-permute-done), channel_id=1, source_target_pairs={{0,17},{1,16},{2,19},{3,18},{4,0},{5,1},{6,2},{7,3},{8,4},{9,5},{1... | collective-permute-start | bytes 860168 | tf_op jit(solution)/shard_map/ppermute | solution.py:30
  16.5 11.7 %collective-permute-start.9 = (bf16[448,640]{1,0:T(8,128)(2,1)S(1)}, bf16[448,640]{1,0:T(8,128)(2,1)S(1)}, u32[]{:S(2)}, u32[]{:S(2)}) collective-permute-start(bf16[448,640]{1,0:T(8,128)(2,1)S(1)} %constant_dynamic-update-slice_fusion.4.refs_4_), channel_id=1, source_target_pairs={{4,21},{5,20},{6,23},{7,22},{8,25},{9,24},{10,27},{11,26},{25,8},{... | collective-permute-start | bytes 1720328 | tf_op jit(solution)/shard_map/ppermute | solution.py:30
  17.2 48.7 %collective-permute-start.3 = (bf16[256,3584]{1,0:T(8,128)(2,1)}, bf16[256,3584]{1,0:T(8,128)(2,1)}, u32[]{:S(2)}, u32[]{:S(2)}) collective-permute-start(bf16[256,3584]{1,0:T(8,128)(2,1)} %refs_15_.1), channel_id=1, source_target_pairs={{0,2},{1,3},{2,0},{3,1},{4,6},{5,7},{6,4},{7,5},{8,10},{9,11},{10,... | collective-permute-start | bytes 5505032 | tf_op jit(solution)/shard_map/ppermute | solution.py:20
  23.7 4.5 %collective-permute-start.8 = (bf16[448,640]{1,0:T(8,128)(2,1)S(1)}, bf16[448,640]{1,0:T(8,128)(2,1)S(1)}, u32[]{:S(2)}, u32[]{:S(2)}) collective-permute-start(bf16[448,640]{1,0:T(8,128)(2,1)S(1)} %broadcast_select_fusion.1), channel_id=1, source_target_pairs={{4,21},{5,20},{6,23},{7,22},{8,25},{9,24},{10,27},{11,26},{25,8},{... | collective-permute-start | bytes 1720328 | tf_op jit(solution)/shard_map/ppermute | solution.py:30
  24.5 16.1 %collective-permute-start.5 = (bf16[448,640]{1,0:T(8,128)(2,1)S(1)}, bf16[448,640]{1,0:T(8,128)(2,1)S(1)}, u32[]{:S(2)}, u32[]{:S(2)}) collective-permute-start(bf16[448,640]{1,0:T(8,128)(2,1)S(1)} %constant_dynamic-update-slice_fusion.refs_6_), channel_id=1, source_target_pairs={{0,4},{1,5},{2,6},{3,7},{4,8},{5,9},{6,10},{7,11},{8,12},{9,13},{1... | collective-permute-start | bytes 1720328 | tf_op jit(solution)/shard_map/ppermute | solution.py:30
  28.2 14.7 %collective-permute-start.7 = (bf16[448,640]{1,0:T(8,128)(2,1)S(1)}, bf16[448,640]{1,0:T(8,128)(2,1)S(1)}, u32[]{:S(2)}, u32[]{:S(2)}) collective-permute-start(bf16[448,640]{1,0:T(8,128)(2,1)S(1)} %constant_dynamic-update-slice_fusion.2.refs_9_), channel_id=1, source_target_pairs={{0,17},{1,16},{2,19},{3,18},{4,0},{5,1},{6,2},{7,3},{8,4},{9,5},{1... | collective-permute-start | bytes 1720328 | tf_op jit(solution)/shard_map/ppermute | solution.py:30
  42.8 16.3 %collective-permute-start.10 = (bf16[448,640]{1,0:T(8,128)(2,1)S(1)}, bf16[448,640]{1,0:T(8,128)(2,1)S(1)}, u32[]{:S(2)}, u32[]{:S(2)}) collective-permute-start(bf16[448,640]{1,0:T(8,128)(2,1)S(1)} %collective-permute-done.5.refs_7_), channel_id=1, source_target_pairs={{4,8},{5,9},{6,10},{7,11},{8,12},{9,13},{10,14},{11,15},{12,29},{1... | collective-permute-start | bytes 1720328 | tf_op jit(solution)/shard_map/ppermute | solution.py:30
  44.1 21.8 %collective-permute-start.11 = (bf16[448,640]{1,0:T(8,128)(2,1)S(1)}, bf16[448,640]{1,0:T(8,128)(2,1)S(1)}, u32[]{:S(2)}, u32[]{:S(2)}) collective-permute-start(bf16[448,640]{1,0:T(8,128)(2,1)S(1)} %collective-permute-done.7.refs_10_), channel_id=1, source_target_pairs={{0,17},{1,16},{2,19},{3,18},{4,0},{5,1},{6,2},{7,3},{8,4},{9,5},{1... | collective-permute-start | bytes 1720328 | tf_op jit(solution)/shard_map/ppermute | solution.py:30
  48.4 31.3 %collective-permute-start.17 = (bf16[256,3584]{1,0:T(8,128)(2,1)}, bf16[256,3584]{1,0:T(8,128)(2,1)}, u32[]{:S(2)}, u32[]{:S(2)}) collective-permute-start(bf16[256,3584]{1,0:T(8,128)(2,1)} %refs_15_.1), channel_id=1, source_target_pairs={{0,1},{1,0},{2,3},{3,2},{4,5},{5,4},{6,7},{7,6},{8,9},{9,8},{10,11... | collective-permute-start | bytes 5505032 | tf_op jit(solution)/shard_map/ppermute | solution.py:20
  65.9 13.8 %collective-permute-start.18 = (bf16[256,3584]{1,0:T(8,128)(2,1)}, bf16[256,3584]{1,0:T(8,128)(2,1)}, u32[]{:S(2)}, u32[]{:S(2)}) collective-permute-start(bf16[256,3584]{1,0:T(8,128)(2,1)} %collective-permute-done.3.refs_16_), channel_id=1, source_target_pairs={{0,1},{1,0},{2,3},{3,2},{4,5},{5,4},{6,7},{7,6},{8,9},{9,8},{10,11... | collective-permute-start | bytes 5505032 | tf_op jit(solution)/shard_map/ppermute | solution.py:20
  66.2 10.4 %collective-permute-start.15 = (bf16[224,640]{1,0:T(8,128)(2,1)S(1)}, bf16[224,640]{1,0:T(8,128)(2,1)S(1)}, u32[]{:S(2)}, u32[]{:S(2)}) collective-permute-start(bf16[224,640]{1,0:T(8,128)(2,1)S(1)} %get-tuple-element.34), channel_id=1, source_target_pairs={{0,17},{1,16},{2,19},{3,18},{12,29},{13,28},{14,31},{15,30},{29,12... | collective-permute-start | bytes 860168 | tf_op jit(solution)/shard_map/ppermute | solution.py:30
  68.1 11.1 %collective-permute-start.16 = (bf16[224,640]{1,0:T(8,128)(2,1)S(1)}, bf16[224,640]{1,0:T(8,128)(2,1)S(1)}, u32[]{:S(2)}, u32[]{:S(2)}) collective-permute-start(bf16[224,640]{1,0:T(8,128)(2,1)S(1)} %get-tuple-element.33), channel_id=1, source_target_pairs={{4,0},{5,1},{6,2},{7,3},{8,12},{9,13},{10,14},{11,15},{25,29},{24,... | collective-permute-start | bytes 860168 | tf_op jit(solution)/shard_map/ppermute | solution.py:30
  69.4 1.4 collective-permute-start.13
  70.8 8.4 %collective-permute-start.12 = (s32[1,256]{1,0:T(1,128)S(1)}, s32[1,256]{1,0:T(1,128)S(1)}, u32[]{:S(2)}, u32[]{:S(2)}) collective-permute-start(s32[1,256]{1,0:T(1,128)S(1)} %bitcast.12), channel_id=1, source_target_pairs={{0,2},{1,3},{2,0},{3,1},{4,6},{5,7},{6,4},{7,5},{8,10},{9,11},{10,... | collective-permute-start | bytes 3080 | tf_op jit(solution)/shard_map/ppermute | solution.py:20
  76.6 3.1 %collective-permute-start.14 = (s32[1,256]{1,0:T(1,128)S(1)}, s32[1,256]{1,0:T(1,128)S(1)}, u32[]{:S(2)}, u32[]{:S(2)}) collective-permute-start(s32[1,256]{1,0:T(1,128)S(1)} %bitcast.13), channel_id=1, source_target_pairs={{0,3},{1,2},{2,1},{3,0},{4,7},{5,6},{6,5},{7,4},{8,11},{9,10},{10,... | collective-permute-start | bytes 3080 | tf_op jit(solution)/shard_map/ppermute | solution.py:20
  91.4 31.2 %all-to-all-start = ((bf16[16,64,640]{2,1,0:T(8,128)(2,1)}), bf16[16,64,640]{2,1,0:T(8,128)(2,1)S(1)}, u32[]{:S(2)}, u32[]{:S(2)}) async-start(bf16[16,64,640]{2,1,0:T(8,128)(2,1)} %bitcast.7), calls=%async_computation | async-start | bytes 2621440 | tf_op jit(solution)/shard_map/all_to_all | solution.py:346
  123.2 1.7 %collective-permute-start.19 = (f32[2,1280]{1,0:T(2,128)S(1)}, f32[2,1280]{1,0:T(2,128)S(1)}, u32[]{:S(2)}, u32[]{:S(2)}) collective-permute-start(f32[2,1280]{1,0:T(2,128)S(1)} %shard_map.107), channel_id=1, source_target_pairs={{0,1},{1,0},{2,3},{3,2},{4,5},{5,4},{6,7},{7,6},{8,9},{9,8},{10,11... | collective-permute-start | bytes 30728 | tf_op jit(solution)/shard_map/ppermute | solution.py:20
  124.9 4.0 %collective-permute-start.20 = (f32[2,1280]{1,0:T(2,128)S(1)}, f32[2,1280]{1,0:T(2,128)S(1)}, u32[]{:S(2)}, u32[]{:S(2)}) collective-permute-start(f32[2,1280]{1,0:T(2,128)S(1)} %add.20), channel_id=1, source_target_pairs={{0,2},{1,3},{2,0},{3,1},{4,6},{5,7},{6,4},{7,5},{8,10},{9,11},{10,... | collective-permute-start | bytes 30728 | tf_op jit(solution)/shard_map/ppermute | solution.py:20
  128.9 5.5 %collective-permute-start.21 = (f32[2,1280]{1,0:T(2,128)S(1)}, f32[2,1280]{1,0:T(2,128)S(1)}, u32[]{:S(2)}, u32[]{:S(2)}) collective-permute-start(f32[2,1280]{1,0:T(2,128)S(1)} %add.21), channel_id=1, source_target_pairs={{0,4},{1,5},{2,6},{3,7},{4,0},{5,1},{6,2},{7,3},{8,12},{9,13},{10,... | collective-permute-start | bytes 30728 | tf_op jit(solution)/shard_map/ppermute | solution.py:20
  134.4 5.9 %collective-permute-start.22 = (f32[2,1280]{1,0:T(2,128)S(1)}, f32[2,1280]{1,0:T(2,128)S(1)}, u32[]{:S(2)}, u32[]{:S(2)}) collective-permute-start(f32[2,1280]{1,0:T(2,128)S(1)} %add.22), channel_id=1, source_target_pairs={{0,8},{1,9},{2,10},{3,11},{4,12},{5,13},{6,14},{7,15},{8,0},{9,1},... | collective-permute-start | bytes 30728 | tf_op jit(solution)/shard_map/ppermute | solution.py:20
  (19 other events, 379.8 us)

commit v9 on v8

--- a/solution.py
+++ b/solution.py
@@ -288,13 +288,13 @@
         p = jnp.where(group == 0, line, 7 - line)
         ends, mids = (0, 3, 4, 7), (1, 2, 5, 6)
         f_own, b_own = step(keep, keep, 1, devices)
+        i_core, i_pair, i_both = (flip(after(ids, to_pair), bits, devices) for bits in (1, 2, 3))
         from_pair = after(flip(to_pair, 2, devices), f_own, b_own)
-        r_pair = flip(after(grad_rows, from_pair), 2, devices)
+        r_pair = flip(after(grad_rows, from_pair, i_core, i_pair, i_both), 2, devices)
         f_far, b_far = step(from_pair, from_pair, 1, devices)
         whole = jnp.concatenate([keep, from_pair])
         f1, b1 = jnp.concatenate([f_own, f_far]), jnp.concatenate([b_own, b_far])
         r_core = flip(after(grad_rows, f1, b1), 1, devices)
-        i_core = flip(after(ids, f1, b1), 1, devices)
         mirror = cycle(whole, [(a, 7 - a) for a in mids], devices)
         f2, b2 = step(f1, b1, 2, devices)
         inner = swap(f1, b1, p, mids, devices)
@@ -302,10 +302,7 @@
         opposite = jnp.where(p % 4 < 2, b3, f3)
         over_y = cycle(opposite[:k], [(a, 7 - a) for a in ends], devices)
         along_z = cycle(opposite[k:], [(1, 0), (2, 3), (5, 4), (6, 7)], devices)
-        r_there = after(r_pair, f3, b3)
-        r_both = flip(r_there, 1, devices)
-        late_ids = after(ids, r_there)
-        i_pair, i_both = flip(late_ids, 2, devices), flip(late_ids, 3, devices)
+        r_both = flip(after(r_pair, f3, b3), 1, devices)
         chain = (whole, mirror, f1, f2, f3, b1, b2, b3, inner, over_y, along_z)
         packed = call(
             product_cycle,

time: 141 us -> 141 us (level)
  starting transfers between devices: 40.7 us -> 39.2 us
    ppermute x12, waiting for transfers between devices: 47.7 us -> 50.5 us  [cycle(): return lax.ppermute(value, BOTH, pairs)]
    ppermute x11, waiting for transfers between devices: 6.01 us -> 4.26 us  [flip(): return lax.ppermute(value, 'seq', [(i, i ^ bits) for i in range(devices)])]
  transfers between devices with their start and end apart: 24 -> 24, of which waited for: 16 -> 14; matrix products, arithmetic and copies ran while one was open for 1% -> 1% of each run, Pallas kernels for 2% -> 2%
where the time goes in v9:
time: 141 us
  waiting for transfers between devices  81.5 us (58%)
  starting transfers between devices  39.2 us (28%)
  Pallas kernels  16.1 us (11%)
  local copies, waits for them, and re-layouts  1.96 us (1%)
    ppermute x12, waiting for transfers between devices, cycle(): return lax.ppermute(value, BOTH, pairs)  50.5 us
    all_to_all x1, waiting for transfers between devices, on_device(): arrived = lax.all_to_all(packed, 'seq', 0, 0, tiled=True)  26.8 us
    ppermute x12, starting transfers between devices, cycle(): return lax.ppermute(value, BOTH, pairs)  18.2 us
    ppermute x11, starting transfers between devices, flip(): return lax.ppermute(value, 'seq', [(i, i ^ bits) for i in range(devices)])  17.1 us
    pallas_call x1, Pallas kernels, on_device(): call(product_cycle, jax.ShapeDtypeStruct((devices, 4, cap, half), BF16),...  11.1 us
    ppermute x11, waiting for transfers between devices, flip(): return lax.ppermute(value, 'seq', [(i, i ^ bits) for i in range(devices)])  4.26 us
    all_to_all x1, starting transfers between devices, on_device(): arrived = lax.all_to_all(packed, 'seq', 0, 0, tiled=True)  3.84 us
  transfers between devices with their start and end apart: 24, of which 14 were waited for; matrix products, arithmetic and copies ran while one was open for 1% of the time, Pallas kernels for 2%

profile of v9, /device:TPU:0, one launch (start us, length us, event | category | flops | bytes accessed | tf_op | source)
XLA Modules:
  0.0 140.5 jit_solution(1654729860871729925)
XLA Ops:
  0.6 1.9 %shard_map.103 = (bf16[224,640]{1,0:T(8,128)(2,1)}, bf16[224,640]{1,0:T(8,128)(2,1)}) custom-call(bf16[224,1280]{1,0:T(8,128)(2,1)} %bitcast.8, bf16[224,1280]{1,0:T(8,128)(2,1)} %bitcast.9), custom_call_target="tpu_custom_call" | custom-call | tf_op jit(solution)/shard_map/pallas_call | solution.py:285
  2.5 3.1 %collective-permute-start.4 = (bf16[224,640]{1,0:T(8,128)(2,1)}, bf16[224,640]{1,0:T(8,128)(2,1)S(1)}, u32[]{:S(2)}, u32[]{:S(2)}) collective-permute-start(bf16[224,640]{1,0:T(8,128)(2,1)} %get-tuple-element.19), channel_id=1, source_target_pairs={{0,4},{1,5},{2,6},{3,7},{4,8},{5,9},{6,10},{7,11},{8,12},{9,13},{1... | collective-permute-start | bytes 860168 | tf_op jit(solution)/shard_map/ppermute | solution.py:30
  5.6 1.7 %collective-permute-start.3 = (bf16[224,640]{1,0:T(8,128)(2,1)}, bf16[224,640]{1,0:T(8,128)(2,1)S(1)}, u32[]{:S(2)}, u32[]{:S(2)}) collective-permute-start(bf16[224,640]{1,0:T(8,128)(2,1)} %get-tuple-element.17), channel_id=1, source_target_pairs={{0,2},{1,3},{2,0},{3,1},{4,6},{5,7},{6,4},{7,5},{8,10},{9,11},{10,... | collective-permute-start | bytes 860168 | tf_op jit(solution)/shard_map/ppermute | solution.py:20
  8.6 3.4 %collective-permute-done.4 = bf16[224,640]{1,0:T(8,128)(2,1)S(1)} collective-permute-done((bf16[224,640]{1,0:T(8,128)(2,1)}, bf16[224,640]{1,0:T(8,128)(2,1)S(1)}, u32[]{:S(2)}, u32[]{:S(2)}) %collective-permute-start.4) | collective-permute-done | bytes 286752 | tf_op jit(solution)/shard_map/ppermute | solution.py:30
  12.0 2.6 %collective-permute-start.2 = (s32[1,256]{1,0:T(1,128)}, s32[1,256]{1,0:T(1,128)S(1)}, u32[]{:S(2)}, u32[]{:S(2)}) collective-permute-start(s32[1,256]{1,0:T(1,128)} %bitcast.12), channel_id=1, source_target_pairs={{0,3},{1,2},{2,1},{3,0},{4,7},{5,6},{6,5},{7,4},{8,11},{9,10},{10,... | collective-permute-start | bytes 3080 | tf_op jit(solution)/shard_map/ppermute | solution.py:20
  17.3 1.6 %collective-permute-start.16 = (bf16[256,3584]{1,0:T(8,128)(2,1)}, bf16[256,3584]{1,0:T(8,128)(2,1)}, u32[]{:S(2)}, u32[]{:S(2)}) collective-permute-start(bf16[256,3584]{1,0:T(8,128)(2,1)} %refs_15_.1), channel_id=1, source_target_pairs={{0,2},{1,3},{2,0},{3,1},{4,6},{5,7},{6,4},{7,5},{8,10},{9,11},{10,... | collective-permute-start | bytes 5505032 | tf_op jit(solution)/shard_map/ppermute | solution.py:20
  18.9 4.6 %collective-permute-done.7 = bf16[224,640]{1,0:T(8,128)(2,1)S(1)} collective-permute-done((bf16[224,640]{1,0:T(8,128)(2,1)S(1)}, bf16[224,640]{1,0:T(8,128)(2,1)S(1)}, u32[]{:S(2)}, u32[]{:S(2)}) %collective-permute-start.7) | collective-permute-done | bytes 286752 | tf_op jit(solution)/shard_map/ppermute | solution.py:30
  26.4 1.8 %collective-permute-start.8 = (bf16[448,640]{1,0:T(8,128)(2,1)S(1)}, bf16[448,640]{1,0:T(8,128)(2,1)S(1)}, u32[]{:S(2)}, u32[]{:S(2)}) collective-permute-start(bf16[448,640]{1,0:T(8,128)(2,1)S(1)} %constant_dynamic-update-slice_fusion.2.refs_6_), channel_id=1, source_target_pairs={{0,4},{1,5},{2,6},{3,7},{4,8},{5,9},{6,10},{7,11},{8,12},{9,13},{1... | collective-permute-start | bytes 1720328 | tf_op jit(solution)/shard_map/ppermute | solution.py:30
  28.3 13.5 %collective-permute-done.10.refs_10_ = bf16[448,640]{1,0:T(8,128)(2,1)S(1)} collective-permute-done((bf16[448,640]{1,0:T(8,128)(2,1)S(1)}, bf16[448,640]{1,0:T(8,128)(2,1)S(1)}, u32[]{:S(2)}, u32[]{:S(2)}) %collective-permute-start.10) | collective-permute-done | bytes 573472 | tf_op jit(solution)/shard_map/ppermute | solution.py:30
  43.8 4.5 %collective-permute-start.13 = (bf16[448,640]{1,0:T(8,128)(2,1)S(1)}, bf16[448,640]{1,0:T(8,128)(2,1)S(1)}, u32[]{:S(2)}, u32[]{:S(2)}) collective-permute-start(bf16[448,640]{1,0:T(8,128)(2,1)S(1)} %collective-permute-done.10.refs_10_), channel_id=1, source_target_pairs={{0,17},{1,16},{2,19},{3,18},{4,0},{5,1},{6,2},{7,3},{8,4},{9,5},{1... | collective-permute-start | bytes 1720328 | tf_op jit(solution)/shard_map/ppermute | solution.py:30
  48.4 11.4 %collective-permute-done.12.refs_8_ = bf16[448,640]{1,0:T(8,128)(2,1)S(1)} collective-permute-done((bf16[448,640]{1,0:T(8,128)(2,1)S(1)}, bf16[448,640]{1,0:T(8,128)(2,1)S(1)}, u32[]{:S(2)}, u32[]{:S(2)}) %collective-permute-start.12) | collective-permute-done | bytes 573472 | tf_op jit(solution)/shard_map/ppermute | solution.py:30
  59.8 6.1 %collective-permute-done.13.refs_11_ = bf16[448,640]{1,0:T(8,128)(2,1)S(1)} collective-permute-done((bf16[448,640]{1,0:T(8,128)(2,1)S(1)}, bf16[448,640]{1,0:T(8,128)(2,1)S(1)}, u32[]{:S(2)}, u32[]{:S(2)}) %collective-permute-start.13) | collective-permute-done | bytes 573472 | tf_op jit(solution)/shard_map/ppermute | solution.py:30
  66.2 1.9 %collective-permute-start.14 = (bf16[224,640]{1,0:T(8,128)(2,1)S(1)}, bf16[224,640]{1,0:T(8,128)(2,1)S(1)}, u32[]{:S(2)}, u32[]{:S(2)}) collective-permute-start(bf16[224,640]{1,0:T(8,128)(2,1)S(1)} %get-tuple-element.32), channel_id=1, source_target_pairs={{0,17},{1,16},{2,19},{3,18},{12,29},{13,28},{14,31},{15,30},{29,12... | collective-permute-start | bytes 860168 | tf_op jit(solution)/shard_map/ppermute | solution.py:30
  69.4 7.2 %collective-permute-done.14.refs_13_ = bf16[224,640]{1,0:T(8,128)(2,1)S(1)} collective-permute-done((bf16[224,640]{1,0:T(8,128)(2,1)S(1)}, bf16[224,640]{1,0:T(8,128)(2,1)S(1)}, u32[]{:S(2)}, u32[]{:S(2)}) %collective-permute-start.14) | collective-permute-done | bytes 286752 | tf_op jit(solution)/shard_map/ppermute | solution.py:30
  76.6 2.7 %collective-permute-done.15.refs_14_ = bf16[224,640]{1,0:T(8,128)(2,1)S(1)} collective-permute-done((bf16[224,640]{1,0:T(8,128)(2,1)S(1)}, bf16[224,640]{1,0:T(8,128)(2,1)S(1)}, u32[]{:S(2)}, u32[]{:S(2)}) %collective-permute-start.15) | collective-permute-done | bytes 286752 | tf_op jit(solution)/shard_map/ppermute | solution.py:30
  80.0 11.1 %shard_map.104 = bf16[16,4,16,640]{3,2,1,0:T(8,128)(2,1)} custom-call(s32[1,256]{1,0:T(1,128)} %bitcast.13, s32[1,256]{1,0:T(1,128)} %copy-done.15, s32[1,256]{1,0:T(1,128)} %copy-done.16, s32[1,256]{1,0:T(1,128)} %copy-done.17, bf16[448,640]{1,0:T(8,128)(2,1)} %copy-done.6, bf16[448,640]{1,0:T(8,128)(2,1)} %copy-done.7, bf16[448,640]{1,0:T(8,128)(2,1)} %copy-done.3, ...), custom_call_target="tpu_custom_call" | custom-call | tf_op jit(solution)/shard_map/pallas_call | solution.py:307
  91.1 3.8 %all-to-all-start = ((bf16[16,64,640]{2,1,0:T(8,128)(2,1)}), bf16[16,64,640]{2,1,0:T(8,128)(2,1)S(1)}, u32[]{:S(2)}, u32[]{:S(2)}) async-start(bf16[16,64,640]{2,1,0:T(8,128)(2,1)} %bitcast.7), calls=%async_computation | async-start | bytes 2621440 | tf_op jit(solution)/shard_map/all_to_all | solution.py:343
  95.5 26.8 %all-to-all-done = bf16[16,64,640]{2,1,0:T(8,128)(2,1)S(1)} async-done(((bf16[16,64,640]{2,1,0:T(8,128)(2,1)}), bf16[16,64,640]{2,1,0:T(8,128)(2,1)S(1)}, u32[]{:S(2)}, u32[]{:S(2)}) %all-to-all-start) | async-done | bytes 1310752 | tf_op jit(solution)/shard_map/all_to_all | solution.py:343
  124.6 2.3 %collective-permute-start.20 = (f32[2,1280]{1,0:T(2,128)S(1)}, f32[2,1280]{1,0:T(2,128)S(1)}, u32[]{:S(2)}, u32[]{:S(2)}) collective-permute-start(f32[2,1280]{1,0:T(2,128)S(1)} %add.20), channel_id=1, source_target_pairs={{0,2},{1,3},{2,0},{3,1},{4,6},{5,7},{6,4},{7,5},{8,10},{9,11},{10,... | collective-permute-start | bytes 30728 | tf_op jit(solution)/shard_map/ppermute | solution.py:20
  126.9 1.6 %collective-permute-done.20 = f32[2,1280]{1,0:T(2,128)S(1)} collective-permute-done((f32[2,1280]{1,0:T(2,128)S(1)}, f32[2,1280]{1,0:T(2,128)S(1)}, u32[]{:S(2)}, u32[]{:S(2)}) %collective-permute-start.20) | collective-permute-done | bytes 10272 | tf_op jit(solution)/shard_map/ppermute | solution.py:20
  128.6 3.8 %collective-permute-start.21 = (f32[2,1280]{1,0:T(2,128)S(1)}, f32[2,1280]{1,0:T(2,128)S(1)}, u32[]{:S(2)}, u32[]{:S(2)}) collective-permute-start(f32[2,1280]{1,0:T(2,128)S(1)} %add.21), channel_id=1, source_target_pairs={{0,4},{1,5},{2,6},{3,7},{4,0},{5,1},{6,2},{7,3},{8,12},{9,13},{10,... | collective-permute-start | bytes 30728 | tf_op jit(solution)/shard_map/ppermute | solution.py:20
  132.4 1.7 %collective-permute-done.21 = f32[2,1280]{1,0:T(2,128)S(1)} collective-permute-done((f32[2,1280]{1,0:T(2,128)S(1)}, f32[2,1280]{1,0:T(2,128)S(1)}, u32[]{:S(2)}, u32[]{:S(2)}) %collective-permute-start.21) | collective-permute-done | bytes 10272 | tf_op jit(solution)/shard_map/ppermute | solution.py:20
  134.1 3.8 %collective-permute-start.22 = (f32[2,1280]{1,0:T(2,128)S(1)}, f32[2,1280]{1,0:T(2,128)S(1)}, u32[]{:S(2)}, u32[]{:S(2)}) collective-permute-start(f32[2,1280]{1,0:T(2,128)S(1)} %add.22), channel_id=1, source_target_pairs={{0,8},{1,9},{2,10},{3,11},{4,12},{5,13},{6,14},{7,15},{8,0},{9,1},... | collective-permute-start | bytes 30728 | tf_op jit(solution)/shard_map/ppermute | solution.py:20
  137.9 2.0 %shard_map.106 = (bf16[256,1280]{1,0:T(8,128)(2,1)}, bf16[256,1280]{1,0:T(8,128)(2,1)}) custom-call(bf16[4,2,2,4,16,640]{5,4,3,2,1,0:T(8,128)(2,1)S(1)} %bitcast.6, bf16[256,1280]{1,0:T(8,128)(2,1)S(1)} %copy-done, bf16[256,1280]{1,0:T(8,128)(2,1)S(1)} %copy-done.1, f32[256,1]{1,0:T(8,128)S(1)} %get-tuple-element.26.a_mean, ...), custom_call_target="tpu_custom_call" | custom-call | tf_op jit(solution)/shard_map/pallas_call | solution.py:353
  (80 shorter events, 14.5 us)
Async XLA Ops:
  2.5 9.5 %collective-permute-start.4 = (bf16[224,640]{1,0:T(8,128)(2,1)}, bf16[224,640]{1,0:T(8,128)(2,1)S(1)}, u32[]{:S(2)}, u32[]{:S(2)}) collective-permute-start(bf16[224,640]{1,0:T(8,128)(2,1)} %get-tuple-element.19), channel_id=1, source_target_pairs={{0,4},{1,5},{2,6},{3,7},{4,8},{5,9},{6,10},{7,11},{8,12},{9,13},{1... | collective-permute-start | bytes 860168 | tf_op jit(solution)/shard_map/ppermute | solution.py:30
  5.6 9.0 %collective-permute-start.5 = (bf16[224,640]{1,0:T(8,128)(2,1)}, bf16[224,640]{1,0:T(8,128)(2,1)S(1)}, u32[]{:S(2)}, u32[]{:S(2)}) collective-permute-start(bf16[224,640]{1,0:T(8,128)(2,1)} %get-tuple-element.19), channel_id=1, source_target_pairs={{0,17},{1,16},{2,19},{3,18},{4,0},{5,1},{6,2},{7,3},{8,4},{9,5},{1... | collective-permute-start | bytes 860168 | tf_op jit(solution)/shard_map/ppermute | solution.py:30
  5.6 9.1 %collective-permute-start.3 = (bf16[224,640]{1,0:T(8,128)(2,1)}, bf16[224,640]{1,0:T(8,128)(2,1)S(1)}, u32[]{:S(2)}, u32[]{:S(2)}) collective-permute-start(bf16[224,640]{1,0:T(8,128)(2,1)} %get-tuple-element.17), channel_id=1, source_target_pairs={{0,2},{1,3},{2,0},{3,1},{4,6},{5,7},{6,4},{7,5},{8,10},{9,11},{10,... | collective-permute-start | bytes 860168 | tf_op jit(solution)/shard_map/ppermute | solution.py:20
  7.3 9.2 %collective-permute-start = (s32[1,256]{1,0:T(1,128)}, s32[1,256]{1,0:T(1,128)S(1)}, u32[]{:S(2)}, u32[]{:S(2)}) collective-permute-start(s32[1,256]{1,0:T(1,128)} %bitcast.10), channel_id=1, source_target_pairs={{0,2},{1,3},{2,0},{3,1},{4,6},{5,7},{6,4},{7,5},{8,10},{9,11},{10,... | collective-permute-start | bytes 3080 | tf_op jit(solution)/shard_map/ppermute | solution.py:20
  7.6 9.6 %collective-permute-start.1 = (s32[1,256]{1,0:T(1,128)}, s32[1,256]{1,0:T(1,128)S(1)}, u32[]{:S(2)}, u32[]{:S(2)}) collective-permute-start(s32[1,256]{1,0:T(1,128)} %bitcast.11), channel_id=1, source_target_pairs={{0,1},{1,0},{2,3},{3,2},{4,5},{5,4},{6,7},{7,6},{8,9},{9,8},{10,11... | collective-permute-start | bytes 3080 | tf_op jit(solution)/shard_map/ppermute | solution.py:20
  12.0 5.2 %collective-permute-start.2 = (s32[1,256]{1,0:T(1,128)}, s32[1,256]{1,0:T(1,128)S(1)}, u32[]{:S(2)}, u32[]{:S(2)}) collective-permute-start(s32[1,256]{1,0:T(1,128)} %bitcast.12), channel_id=1, source_target_pairs={{0,3},{1,2},{2,1},{3,0},{4,7},{5,6},{6,5},{7,4},{8,11},{9,10},{10,... | collective-permute-start | bytes 3080 | tf_op jit(solution)/shard_map/ppermute | solution.py:20
  14.7 8.8 %collective-permute-start.7 = (bf16[224,640]{1,0:T(8,128)(2,1)S(1)}, bf16[224,640]{1,0:T(8,128)(2,1)S(1)}, u32[]{:S(2)}, u32[]{:S(2)}) collective-permute-start(bf16[224,640]{1,0:T(8,128)(2,1)S(1)} %collective-permute-done.3), channel_id=1, source_target_pairs={{0,4},{1,5},{2,6},{3,7},{4,8},{5,9},{6,10},{7,11},{8,12},{9,13},{1... | collective-permute-start | bytes 860168 | tf_op jit(solution)/shard_map/ppermute | solution.py:30
  15.9 8.6 %collective-permute-start.9 = (bf16[224,640]{1,0:T(8,128)(2,1)S(1)}, bf16[224,640]{1,0:T(8,128)(2,1)S(1)}, u32[]{:S(2)}, u32[]{:S(2)}) collective-permute-start(bf16[224,640]{1,0:T(8,128)(2,1)S(1)} %collective-permute-done.3), channel_id=1, source_target_pairs={{0,17},{1,16},{2,19},{3,18},{4,0},{5,1},{6,2},{7,3},{8,4},{9,5},{1... | collective-permute-start | bytes 860168 | tf_op jit(solution)/shard_map/ppermute | solution.py:30
  16.5 11.8 %collective-permute-start.6 = (bf16[448,640]{1,0:T(8,128)(2,1)S(1)}, bf16[448,640]{1,0:T(8,128)(2,1)S(1)}, u32[]{:S(2)}, u32[]{:S(2)}) collective-permute-start(bf16[448,640]{1,0:T(8,128)(2,1)S(1)} %constant_dynamic-update-slice_fusion.refs_4_), channel_id=1, source_target_pairs={{4,21},{5,20},{6,23},{7,22},{8,25},{9,24},{10,27},{11,26},{25,8},{... | collective-permute-start | bytes 1720328 | tf_op jit(solution)/shard_map/ppermute | solution.py:30
  17.3 48.7 %collective-permute-start.16 = (bf16[256,3584]{1,0:T(8,128)(2,1)}, bf16[256,3584]{1,0:T(8,128)(2,1)}, u32[]{:S(2)}, u32[]{:S(2)}) collective-permute-start(bf16[256,3584]{1,0:T(8,128)(2,1)} %refs_15_.1), channel_id=1, source_target_pairs={{0,2},{1,3},{2,0},{3,1},{4,6},{5,7},{6,4},{7,5},{8,10},{9,11},{10,... | collective-permute-start | bytes 5505032 | tf_op jit(solution)/shard_map/ppermute | solution.py:20
  24.6 3.6 %collective-permute-start.11 = (bf16[448,640]{1,0:T(8,128)(2,1)S(1)}, bf16[448,640]{1,0:T(8,128)(2,1)S(1)}, u32[]{:S(2)}, u32[]{:S(2)}) collective-permute-start(bf16[448,640]{1,0:T(8,128)(2,1)S(1)} %broadcast_select_fusion.1), channel_id=1, source_target_pairs={{4,21},{5,20},{6,23},{7,22},{8,25},{9,24},{10,27},{11,26},{25,8},{... | collective-permute-start | bytes 1720328 | tf_op jit(solution)/shard_map/ppermute | solution.py:30
  25.3 16.5 %collective-permute-start.10 = (bf16[448,640]{1,0:T(8,128)(2,1)S(1)}, bf16[448,640]{1,0:T(8,128)(2,1)S(1)}, u32[]{:S(2)}, u32[]{:S(2)}) collective-permute-start(bf16[448,640]{1,0:T(8,128)(2,1)S(1)} %constant_dynamic-update-slice_fusion.4.refs_9_), channel_id=1, source_target_pairs={{0,17},{1,16},{2,19},{3,18},{4,0},{5,1},{6,2},{7,3},{8,4},{9,5},{1... | collective-permute-start | bytes 1720328 | tf_op jit(solution)/shard_map/ppermute | solution.py:30
  26.4 16.1 %collective-permute-start.8 = (bf16[448,640]{1,0:T(8,128)(2,1)S(1)}, bf16[448,640]{1,0:T(8,128)(2,1)S(1)}, u32[]{:S(2)}, u32[]{:S(2)}) collective-permute-start(bf16[448,640]{1,0:T(8,128)(2,1)S(1)} %constant_dynamic-update-slice_fusion.2.refs_6_), channel_id=1, source_target_pairs={{0,4},{1,5},{2,6},{3,7},{4,8},{5,9},{6,10},{7,11},{8,12},{9,13},{1... | collective-permute-start | bytes 1720328 | tf_op jit(solution)/shard_map/ppermute | solution.py:30
  42.5 17.3 %collective-permute-start.12 = (bf16[448,640]{1,0:T(8,128)(2,1)S(1)}, bf16[448,640]{1,0:T(8,128)(2,1)S(1)}, u32[]{:S(2)}, u32[]{:S(2)}) collective-permute-start(bf16[448,640]{1,0:T(8,128)(2,1)S(1)} %collective-permute-done.8.refs_7_), channel_id=1, source_target_pairs={{4,8},{5,9},{6,10},{7,11},{8,12},{9,13},{10,14},{11,15},{12,29},{1... | collective-permute-start | bytes 1720328 | tf_op jit(solution)/shard_map/ppermute | solution.py:30
  43.8 22.1 %collective-permute-start.13 = (bf16[448,640]{1,0:T(8,128)(2,1)S(1)}, bf16[448,640]{1,0:T(8,128)(2,1)S(1)}, u32[]{:S(2)}, u32[]{:S(2)}) collective-permute-start(bf16[448,640]{1,0:T(8,128)(2,1)S(1)} %collective-permute-done.10.refs_10_), channel_id=1, source_target_pairs={{0,17},{1,16},{2,19},{3,18},{4,0},{5,1},{6,2},{7,3},{8,4},{9,5},{1... | collective-permute-start | bytes 1720328 | tf_op jit(solution)/shard_map/ppermute | solution.py:30
  48.3 30.9 %collective-permute-start.17 = (bf16[256,3584]{1,0:T(8,128)(2,1)}, bf16[256,3584]{1,0:T(8,128)(2,1)}, u32[]{:S(2)}, u32[]{:S(2)}) collective-permute-start(bf16[256,3584]{1,0:T(8,128)(2,1)} %refs_15_.1), channel_id=1, source_target_pairs={{0,1},{1,0},{2,3},{3,2},{4,5},{5,4},{6,7},{7,6},{8,9},{9,8},{10,11... | collective-permute-start | bytes 5505032 | tf_op jit(solution)/shard_map/ppermute | solution.py:20
  66.0 13.3 %collective-permute-start.18 = (bf16[256,3584]{1,0:T(8,128)(2,1)}, bf16[256,3584]{1,0:T(8,128)(2,1)}, u32[]{:S(2)}, u32[]{:S(2)}) collective-permute-start(bf16[256,3584]{1,0:T(8,128)(2,1)} %collective-permute-done.16.refs_16_), channel_id=1, source_target_pairs={{0,1},{1,0},{2,3},{3,2},{4,5},{5,4},{6,7},{7,6},{8,9},{9,8},{10,11... | collective-permute-start | bytes 5505032 | tf_op jit(solution)/shard_map/ppermute | solution.py:20
  66.2 10.4 %collective-permute-start.14 = (bf16[224,640]{1,0:T(8,128)(2,1)S(1)}, bf16[224,640]{1,0:T(8,128)(2,1)S(1)}, u32[]{:S(2)}, u32[]{:S(2)}) collective-permute-start(bf16[224,640]{1,0:T(8,128)(2,1)S(1)} %get-tuple-element.32), channel_id=1, source_target_pairs={{0,17},{1,16},{2,19},{3,18},{12,29},{13,28},{14,31},{15,30},{29,12... | collective-permute-start | bytes 860168 | tf_op jit(solution)/shard_map/ppermute | solution.py:30
  68.1 11.1 %collective-permute-start.15 = (bf16[224,640]{1,0:T(8,128)(2,1)S(1)}, bf16[224,640]{1,0:T(8,128)(2,1)S(1)}, u32[]{:S(2)}, u32[]{:S(2)}) collective-permute-start(bf16[224,640]{1,0:T(8,128)(2,1)S(1)} %get-tuple-element.31), channel_id=1, source_target_pairs={{4,0},{5,1},{6,2},{7,3},{8,12},{9,13},{10,14},{11,15},{25,29},{24,... | collective-permute-start | bytes 860168 | tf_op jit(solution)/shard_map/ppermute | solution.py:30
  91.1 31.2 %all-to-all-start = ((bf16[16,64,640]{2,1,0:T(8,128)(2,1)}), bf16[16,64,640]{2,1,0:T(8,128)(2,1)S(1)}, u32[]{:S(2)}, u32[]{:S(2)}) async-start(bf16[16,64,640]{2,1,0:T(8,128)(2,1)} %bitcast.7), calls=%async_computation | async-start | bytes 2621440 | tf_op jit(solution)/shard_map/all_to_all | solution.py:343
  122.9 1.7 %collective-permute-start.19 = (f32[2,1280]{1,0:T(2,128)S(1)}, f32[2,1280]{1,0:T(2,128)S(1)}, u32[]{:S(2)}, u32[]{:S(2)}) collective-permute-start(f32[2,1280]{1,0:T(2,128)S(1)} %shard_map.107), channel_id=1, source_target_pairs={{0,1},{1,0},{2,3},{3,2},{4,5},{5,4},{6,7},{7,6},{8,9},{9,8},{10,11... | collective-permute-start | bytes 30728 | tf_op jit(solution)/shard_map/ppermute | solution.py:20
  124.6 4.0 %collective-permute-start.20 = (f32[2,1280]{1,0:T(2,128)S(1)}, f32[2,1280]{1,0:T(2,128)S(1)}, u32[]{:S(2)}, u32[]{:S(2)}) collective-permute-start(f32[2,1280]{1,0:T(2,128)S(1)} %add.20), channel_id=1, source_target_pairs={{0,2},{1,3},{2,0},{3,1},{4,6},{5,7},{6,4},{7,5},{8,10},{9,11},{10,... | collective-permute-start | bytes 30728 | tf_op jit(solution)/shard_map/ppermute | solution.py:20
  128.6 5.5 %collective-permute-start.21 = (f32[2,1280]{1,0:T(2,128)S(1)}, f32[2,1280]{1,0:T(2,128)S(1)}, u32[]{:S(2)}, u32[]{:S(2)}) collective-permute-start(f32[2,1280]{1,0:T(2,128)S(1)} %add.21), channel_id=1, source_target_pairs={{0,4},{1,5},{2,6},{3,7},{4,0},{5,1},{6,2},{7,3},{8,12},{9,13},{10,... | collective-permute-start | bytes 30728 | tf_op jit(solution)/shard_map/ppermute | solution.py:20
  134.1 5.9 %collective-permute-start.22 = (f32[2,1280]{1,0:T(2,128)S(1)}, f32[2,1280]{1,0:T(2,128)S(1)}, u32[]{:S(2)}, u32[]{:S(2)}) collective-permute-start(f32[2,1280]{1,0:T(2,128)S(1)} %add.22), channel_id=1, source_target_pairs={{0,8},{1,9},{2,10},{3,11},{4,12},{5,13},{6,14},{7,15},{8,0},{9,1},... | collective-permute-start | bytes 30728 | tf_op jit(solution)/shard_map/ppermute | solution.py:20
  (18 other events, 344.7 us)
